TPU v7x, 32 devices: a whole 2x2x4 slice. The times are simulated.
32 devices in a mesh: group: 2 (over x), dp: 4 (over y, core), mp: 4 (over z).
Axes of the slice: x: 2, y: 2, z: 4, core: 2. Of those that a mesh axis runs over, the one named last changes fastest.
Arguments:
- image_features: bfloat16 [1024, 6144], P('dp', 'mp'), may hold values from -6 to 6
- text_features: bfloat16 [1024, 1024], P('dp', 'mp'), may hold values from -6 to 6
- image_gain: float32 [6144], P('mp'), may hold values from 0.25 to 1.75
- text_gain: float32 [1024], P('mp'), may hold values from 0.25 to 1.75
- image_proj: bfloat16 [6144, 1024], P('mp'), may hold values from -1 to 1
- text_proj: bfloat16 [1024, 1024], P('mp'), may hold values from -1 to 1
- pair: int32 [1024], replicated, may hold values from 0 to 1023, each once
- logit_scale: float32 [], replicated, may hold values from 10 to 100
Outputs:
- embedding_grads: float32 [2, 1024, 1024], P('group', ('dp', 'mp'))
- loss: float32 [], replicated
Inputs may be any that keep to these rules, and one draw needn't show every extreme that they name: `pair`: each caption belongs to exactly one image.
All inputs are finite; a program needn't handle non-finite values.
Results may differ from a plain program's by a relative error of at most 0.0061.
Values may be sent and summed in bfloat16 or wider, within the bound.
No kernel may reach another device: no remote copies, remote signals or barrier semaphores. Data moves between devices by JAX's collectives and lax.ppermute only.
A program may use at most 128 MiB of HBM per device.

v0:
```python
import jax
import jax.numpy as jnp
from jax import lax
from jax.sharding import PartitionSpec as P

epsilon = 1e-05


def partner(shard, axis, distance):
    return lax.ppermute(shard, axis, [(i, i ^ 1 << distance) for i in range(lax.axis_size(axis))])


def moments(features):
    values = features.astype(jnp.float32)
    return (jnp.sum(values, axis=1), jnp.sum(values * values, axis=1))


def body(
    image_features, text_features, image_gain, text_gain, image_proj, text_proj, pair, logit_scale
):
    row_total = image_features.shape[0]
    shards = lax.axis_size("mp")
    span = row_total // shards
    text_side = lax.axis_index("group") == 1
    first_sum, second_sum = lax.cond(
        text_side, lambda: moments(text_features), lambda: moments(image_features)
    )
    first_sum, second_sum = lax.psum((first_sum, second_sum), "mp")
    width = jnp.where(
        text_side, text_features.shape[1] * shards, image_features.shape[1] * shards
    ).astype(jnp.float32)
    average = first_sum / width
    inverse = lax.rsqrt(second_sum / width - average * average + epsilon)

    def apply(features, gain, projection):
        values = features.astype(jnp.float32)
        normed = ((values - average[:, None]) * inverse[:, None] * gain[None, :]).astype(
            jnp.bfloat16
        )
        return jnp.dot(normed, projection, preferred_element_type=jnp.float32)

    embedded = lax.psum_scatter(
        lax.cond(
            text_side,
            lambda: apply(text_features, text_gain, text_proj),
            lambda: apply(image_features, image_gain, image_proj),
        ),
        "mp",
        scatter_dimension=0,
        tiled=True,
    )
    unit = (
        embedded * lax.rsqrt(jnp.sum(embedded * embedded, axis=1, keepdims=True) + 1e-06)
    ).astype(jnp.bfloat16)
    theirs = partner(unit, "group", 0)
    others = lax.all_gather(theirs, ("dp", "mp"), axis=0, tiled=True)
    count_all = others.shape[0]
    scores = logit_scale * jnp.einsum("re,ne->rn", unit, others, preferred_element_type=jnp.float32)
    row_peak = jnp.max(scores, axis=1)
    own_total = row_peak + jnp.log(jnp.sum(jnp.exp(scores - row_peak[:, None]), axis=1))
    their_total = partner(own_total, "group", 0)
    other_total = lax.all_gather(their_total, ("dp", "mp"), axis=0, tiled=True)
    block_index = lax.axis_index("dp") * shards + lax.axis_index("mp")
    row_ids = block_index * span + jnp.arange(span, dtype=jnp.int32)
    column_ids = jnp.arange(count_all, dtype=jnp.int32)
    image_match = jnp.take(pair, row_ids)[:, None] == column_ids[None, :]
    text_match = pair[None, :] == row_ids[:, None]
    flags = jnp.where(text_side, text_match, image_match).astype(jnp.float32)
    target = jnp.sum(flags * scores)
    weights = logit_scale * (
        jnp.exp(scores - own_total[:, None]) + jnp.exp(scores - other_total[None, :]) - 2.0 * flags
    )
    grads = jnp.dot(weights.astype(jnp.bfloat16), others, preferred_element_type=jnp.float32)
    partial_loss = jnp.sum(own_total) - target
    summed = lax.psum(partial_loss, ("group", "dp", "mp"))
    loss = summed / (2.0 * count_all)
    return (grads[None, :, :], loss)


def solution(mesh):
    in_specs = (
        P("dp", "mp"),
        P("dp", "mp"),
        P("mp"),
        P("mp"),
        P("mp", None),
        P("mp", None),
        P(),
        P(),
    )
    out_specs = (P("group", ("dp", "mp"), None), P())
    return jax.shard_map(body, mesh=mesh, in_specs=in_specs, out_specs=out_specs, check_vma=False)
```

profile of v0, /device:TPU:0, one launch (start us, length us, event | category | flops | bytes accessed | tf_op | source)
XLA Modules:
  0.0 186.4 jit_solution(10108770344644790638)
XLA Ops:
  7.2 0.0 reduce-scatter.2.cloned.1.call-start
  7.2 1.4 conditional.2
  7.2 1.4 fusion
  8.7 13.5 %all-reduce.1 = (f32[256]{0:T(256)S(1)}, f32[256]{0:T(256)S(1)}) all-reduce(f32[256]{0:T(256)S(1)} %get-tuple-element.39, f32[256]{0:T(256)S(1)} %get-tuple-element.40), channel_id=1, replica_groups=mesh['group'=2,'dp'=4,'mp'=4] {'mp'}, use_global_device_ids=true, to_apply=%region_6.0 | all-reduce | flops 512 | bytes 4096 | tf_op jit(solution)/shard_map/psum | solution.py:28
  22.1 0.0 copy-start.4
  22.1 3.2 %conditional.3 = (f32[256,1024]{1,0:T(8,128)S(1)}) conditional(s32[]{:T(128)} %convert_element_type.32, (bf16[256,1536]{1,0:T(8,128)(2,1)}, f32[256]{0:T(256)S(1)}, f32[256]{0:T(256)S(1)}, f32[1536]{0:T(1024)}, bf16[1536,1024]{1,0:T(8,128)(2,1)}) %tuple.22, (bf16[256,256]{1,0:T(8,128)(2,1)}, f32[256]{0:T(256)S(1)}, f32[256]{0:T(256)S(1)}, ...), branch_computations={%region_8.9_spmd, %region_9.10_spmd} | conditional | flops 807272448 | bytes 4988936 | solution.py:43
  22.2 3.2 %fusion.2 = f32[256,1024]{1,0:T(8,128)S(1)} fusion(bf16[1536,1024]{1,0:T(8,128)(2,1)} %get-tuple-element.44, bf16[256,1536]{1,0:T(8,128)(2,1)} %get-tuple-element.25, f32[1536]{0:T(1024)} %get-tuple-element.43, f32[256]{0:T(256)S(1)} %get-tuple-element.27, f32[256]{0:T(256)S(1)} %get-tuple-element.26), kind=kOutput, calls=%fused_computation.8 | convolution fusion | flops 807272448 | bytes 4988928 | tf_op jit(solution)/shard_map/cond/branch_0_fun/dot_general | solution.py:40
  25.4 0.0 copy-start.2
  25.4 0.0 copy-start
  25.4 1.0 copy-done.2
  26.3 0.0 reduce-scatter.2.cloned.1.call-update
  26.4 0.0 all-gather.2.cloned.1.call-start
  26.4 24.5 %reduce-scatter.2.cloned.1.call-done = f32[64,1024]{1,0:T(8,128)} async-done(((f32[256,1024]{1,0:T(8,128)}), f32[64,1024]{1,0:T(8,128)}) %reduce-scatter.2.cloned.1.call-update) | async-done | bytes 262160 | tf_op jit(solution)/shard_map/reduce_scatter | solution.py:42
  51.0 1.1 multiply_reduce_fusion
  52.0 1.0 multiply_convert_fusion.5
  53.1 1.5 collective-permute-start
  54.6 3.6 %collective-permute-done = bf16[64,1024]{1,0:T(8,128)(2,1)S(1)} collective-permute-done((bf16[64,1024]{1,0:T(8,128)(2,1)S(1)}, bf16[64,1024]{1,0:T(8,128)(2,1)S(1)}, u32[]{:S(2)}, u32[]{:S(2)}) %collective-permute-start) | collective-permute-done | bytes 131104 | tf_op jit(solution)/shard_map/ppermute | solution.py:10
  58.2 0.0 copy-start.3
  58.2 0.7 copy-done.3
  58.9 0.0 all-gather.2.cloned.1.call-update
  59.6 0.0 copy-done.4
  59.6 0.6 dynamic-slice
  60.2 0.0 copy-done
  60.2 0.7 gather_fusion
  60.9 38.3 %all-gather.2.cloned.1.call-done = bf16[1024,1024]{1,0:T(8,128)(2,1)} async-done(((bf16[64,1024]{1,0:T(8,128)(2,1)}), bf16[1024,1024]{1,0:T(8,128)(2,1)}) %all-gather.2.cloned.1.call-update) | async-done | bytes 2097168 | tf_op jit(solution)/shard_map/all_gather | solution.py:56
  99.2 0.0 copy-start.1
  99.2 2.6 %fusion.24 = (f32[64]{0:T(128)S(1)}, f32[64,1024]{1,0:T(8,128)S(1)}) fusion(bf16[64,1024]{1,0:T(8,128)(2,1)S(1)} %multiply_convert_fusion.5, bf16[1024,1024]{1,0:T(8,128)(2,1)} %all-gather.2.cloned.1.call-done, f32[]{:T(128)S(6)} %copy.21), kind=kOutput, calls=%fused_computation.49 | convolution fusion | flops 134348736 | bytes 2490628 | tf_op jit(solution)/shard_map/re,ne->rn/dot_general | solution.py:58
  101.8 0.8 select_reduce_fusion
  102.6 0.6 fusion.23
  103.2 1.5 collective-permute-start.1
  106.6 38.2 %psum.23 = f32[]{:T(128)} all-reduce(f32[]{:T(128)S(6)} %sub.57), channel_id=1, replica_groups=mesh['group'=2,'dp'=4,'mp'=4] {'group','dp','mp'}, use_global_device_ids=true, to_apply=%region_16.17 | all-reduce | flops 1 | bytes 8 | tf_op jit(solution)/shard_map/psum | solution.py:75
  145.5 0.0 collective-permute-done.1
  145.5 0.2 dynamic-update-slice
  145.8 31.3 %all-reduce = f32[1024]{0:T(1024)S(1)} all-reduce(f32[1024]{0:T(1024)S(1)} %dynamic-update-slice), channel_id=1, replica_groups=mesh['group'=2,'dp'=4,'mp'=4] {'dp','mp'}, use_global_device_ids=true, to_apply=%add | all-reduce | flops 1024 | bytes 8192
  177.1 0.0 copy-done.1
  177.1 1.3 convolution_bitcast_fusion
  (6 shorter events, 0.1 us)
Async XLA Ops:
  7.2 43.8 %reduce-scatter.2.cloned.1.call-start = ((), (), s32[]{:S(2)}) async-start(), calls=%async_computation.1 | async-start | bytes 1310720 | tf_op jit(solution)/shard_map/reduce_scatter | solution.py:42
  22.1 37.4 %copy-start.4 = (u32[32]{0:T(128)S(1)}, u32[32]{0:T(128)}, u32[]{:S(2)}) copy-start(u32[32]{0:T(128)} %constant.59) | copy-start | bytes 388
  25.4 1.0 copy-start.2
  25.4 34.8 %copy-start = (s32[1024]{0:T(1024)S(1)}, s32[1024]{0:T(1024)}, u32[]{:S(2)}) copy-start(s32[1024]{0:T(1024)} %param.18) | copy-start | bytes 12292
  26.4 72.9 %all-gather.2.cloned.1.call-start = ((), (), s32[]{:S(2)}) async-start(), calls=%async_computation.2 | async-start | bytes 2228224 | tf_op jit(solution)/shard_map/all_gather | solution.py:56
  53.1 5.1 %collective-permute-start = (bf16[64,1024]{1,0:T(8,128)(2,1)S(1)}, bf16[64,1024]{1,0:T(8,128)(2,1)S(1)}, u32[]{:S(2)}, u32[]{:S(2)}) collective-permute-start(bf16[64,1024]{1,0:T(8,128)(2,1)S(1)} %multiply_convert_fusion.5), channel_id=1, source_target_pairs={{0,16},{16,0},{1,17},{17,1},{2,18},{18,2},{3,19},{19,3},{4,20},{20... | collective-permute-start | bytes 393224 | tf_op jit(solution)/shard_map/ppermute | solution.py:10
  58.2 0.7 copy-start.3
  99.2 77.9 %copy-start.1 = (bf16[1024,1024]{1,0:T(8,128)(2,1)S(1)}, bf16[1024,1024]{1,0:T(8,128)(2,1)}, u32[]{:S(2)}) copy-start(bf16[1024,1024]{1,0:T(8,128)(2,1)} %all-gather.2.cloned.1.call-done) | copy-start | bytes 6291460
  103.2 42.3 %collective-permute-start.1 = (f32[64]{0:T(128)S(1)}, f32[64]{0:T(128)S(1)}, u32[]{:S(2)}, u32[]{:S(2)}) collective-permute-start(f32[64]{0:T(128)S(1)} %get-tuple-element.58), channel_id=1, source_target_pairs={{0,16},{16,0},{1,17},{17,1},{2,18},{18,2},{3,19},{19,3},{4,20},{20... | collective-permute-start | bytes 776 | tf_op jit(solution)/shard_map/ppermute | solution.py:10
Sparse Core Ops, SparseCore 0:
  26.5 24.4 reduce-scatter.1
  59.0 40.1 all-gather.1
where the time goes:
time: 187 us; the launch traced here: 186 us
  blocking collectives  83 us (44%)
  waiting for transfers between devices  66.5 us (36%)
  between operations  18.5 us (10%)
  matrix products  7.12 us (4%)
  other arithmetic  4.99 us (3%)
  local copies, waits for them, and re-layouts  3.21 us (2%)
  starting transfers between devices  3.09 us (2%)
    all_gather x1, waiting for transfers between devices, body(): others = lax.all_gather(theirs, ('dp', 'mp'), axis=0, tiled=True)  38.3 us
    psum x1, blocking collectives, body(): summed = lax.psum(partial_loss, ('group', 'dp', 'mp'))  38.2 us
    unnamed x1, blocking collectives  31.3 us
    reduce_scatter x1, waiting for transfers between devices, body(): lax.psum_scatter(lax.cond(text_side, lambda: apply(text_features, text_ga...  24.5 us
    psum x1, blocking collectives, body(): first_sum, second_sum = lax.psum((first_sum, second_sum), 'mp')  13.5 us
  transfers between devices with their start and end apart: 4, of which 3 were waited for; matrix products, arithmetic and copies ran while one was open for 1% of the time, Pallas kernels for 0%

commit v1 on v0

v1 whole, which is shorter than its diff:
```python
import functools

import jax
import jax.numpy as jnp
from jax import lax
from jax.experimental import pallas as pl
from jax.experimental.pallas import tpu as pltpu
from jax.sharding import PartitionSpec as P

norm_epsilon = 1e-05
unit_epsilon = 1e-06
lanes = 128
VMEM = pl.BlockSpec(memory_space=pltpu.VMEM)
SMEM = pl.BlockSpec(memory_space=pltpu.SMEM)
ANY = pl.BlockSpec(memory_space=pl.ANY)
PARAMS = pltpu.CompilerParams(vmem_limit_bytes=48 * 1024 * 1024)


def exchange(shard, axis, distance):
    return lax.ppermute(shard, axis, [(i, i ^ distance) for i in range(lax.axis_size(axis))])


def cross_exchange(shard, distance):
    count = lax.axis_size("dp")
    pairs = [
        (side * count + i, (1 - side) * count + (i ^ distance))
        for side in range(2)
        for i in range(count)
    ]
    return lax.ppermute(shard, ("group", "dp"), pairs)


def tree(values, combine):
    values = list(values)
    while len(values) > 1:
        values = [combine(values[i], values[i + 1]) for i in range(0, len(values), 2)]
    return values[0]


def log_add(a, b):
    peak = jnp.maximum(a, b)
    return peak + jnp.log1p(jnp.exp(jnp.minimum(a, b) - peak))


def rows_to_lanes(columns):
    return jnp.transpose(columns)


def project_kernel(shards, info, image_x, text_x, image_g, text_g, image_p, text_p, *rest):
    own_out = rest[0]
    parts = rest[1:shards]
    notes = rest[shards : 2 * shards]
    x_buf, p_buf, total, stats, sems = rest[2 * shards :]
    rows = x_buf.shape[0]
    span = rows // shards
    width_out = total.shape[1]
    me = info[1]

    def tower(x_hbm, gain, p_hbm):
        width = x_hbm.shape[1]
        step = min(width, 512)
        chunks = width // step
        x_copy = pltpu.make_async_copy(x_hbm, x_buf.at[:, pl.ds(0, width)], sems.at[0])
        x_copy.start()
        copies = []
        for c in range(chunks):
            copy = pltpu.make_async_copy(
                p_hbm.at[pl.ds(c * step, step)], p_buf.at[pl.ds(c * step, step)], sems.at[1 + c]
            )
            copy.start()
            copies.append(copy)
        x_copy.wait()
        values = x_buf[:, :width].astype(jnp.float32)
        mean = jnp.sum(values, axis=1, keepdims=True) / width
        spread = jnp.sum((values - mean) * (values - mean), axis=1, keepdims=True)
        lane = lax.broadcasted_iota(jnp.int32, (rows, lanes), 1)
        stats[...] = jnp.where(lane == 0, mean, jnp.where(lane == 1, spread, 0.0))
        offset = jnp.zeros((16, width_out), jnp.float32)
        for c in range(chunks):
            g = gain[:, c * step : (c + 1) * step]
            high = g.astype(jnp.bfloat16).astype(jnp.float32)
            middle = (g - high).astype(jnp.bfloat16).astype(jnp.float32)
            low = g - high - middle
            row = lax.broadcasted_iota(jnp.int32, (16, step), 0)
            split = jnp.where(
                row == 0, high, jnp.where(row == 1, middle, jnp.where(row == 2, low, 0.0))
            ).astype(jnp.bfloat16)
            x = x_buf[:, c * step : (c + 1) * step].astype(jnp.float32)
            x = ((x - mean) * g).astype(jnp.bfloat16)
            copies[c].wait()
            p = p_buf[c * step : (c + 1) * step, :]
            product = jnp.dot(x, p, preferred_element_type=jnp.float32)
            if c == 0:
                total[...] = product
            else:
                total[...] += product
            offset += jnp.dot(split, p, preferred_element_type=jnp.float32)
        offset = jnp.sum(offset, axis=0, keepdims=True)
        height = width_out // lanes
        for k in range(shards):
            for j in range(height):
                notes[k][j : j + 1, :] = offset[:, j * lanes : (j + 1) * lanes]

    @pl.when(info[0] == 1)
    def _():
        tower(text_x, text_g, text_p)

    @pl.when(info[0] == 0)
    def _():
        tower(image_x, image_g, image_p)

    height = width_out // lanes
    for k in range(shards):
        first = pl.multiple_of((me ^ k) * span, span)
        block = total[pl.ds(first, span), :]
        if k == 0:
            own_out[...] = block
        else:
            parts[k - 1][...] = block.astype(jnp.bfloat16)
        one = stats[pl.ds(first, span), :]
        square = jnp.concatenate([one] * (lanes // span), axis=0)
        notes[k][height : height + 8, :] = rows_to_lanes(square)[:8, :]


def finish_kernel(shards, info, own, *rest):
    parts = rest[: shards - 1]
    notes = rest[shards - 1 : 2 * shards - 1]
    unit_out = rest[2 * shards - 1]
    span, width_out = own.shape
    height = width_out // lanes
    width = info[2].astype(jnp.float32)
    means, spreads = [], []
    for k in range(shards):
        stat = notes[k][height : height + 8, :]
        square = rows_to_lanes(jnp.concatenate([stat] * (lanes // 8), axis=0))[:span]
        means.append(square[:, 0:1])
        spreads.append(square[:, 1:2])
    mean = tree(means, jnp.add) / shards
    spread = tree(spreads, jnp.add) / width
    spread += tree([(m - mean) * (m - mean) for m in means], jnp.add) / shards
    inverse = lax.rsqrt(spread + norm_epsilon)
    pieces = []
    squares = jnp.zeros((span, lanes), jnp.float32)
    for j in range(height):
        at = slice(j * lanes, (j + 1) * lanes)
        value = own[:, at]
        for part in parts:
            value += part[:, at].astype(jnp.float32)
        for k in range(shards):
            value += (means[k] - mean) * notes[k][j : j + 1, :]
        value *= inverse
        squares += value * value
        pieces.append(value)
    scale = lax.rsqrt(jnp.sum(squares, axis=1, keepdims=True) + unit_epsilon)
    for j in range(height):
        unit_out[:, j * lanes : (j + 1) * lanes] = (pieces[j] * scale).astype(jnp.bfloat16)


def scores_kernel(owners, shards, info, multiplier, left, right, *rest):
    owns = rest[:owners]
    others = rest[owners : owners + shards]
    scores_out, row_out, column_out, gathered, mine = rest[owners + shards :]
    span = owns[0].shape[0]
    for k in range(shards):
        gathered[pl.ds(pl.multiple_of((info[1] ^ k) * span, span), span), :] = others[k][...]
    for k in range(owners):
        mine[pl.ds(pl.multiple_of((info[0] ^ k) * span, span), span), :] = owns[k][...]
    scores = multiplier[0] * lax.dot_general(
        mine[...], gathered[...], (((1,), (1,)), ((), ())), preferred_element_type=jnp.float32
    )
    scores_out[...] = scores
    row_peak = jnp.max(scores, axis=1, keepdims=True)
    row_part = row_peak + jnp.log(jnp.sum(jnp.exp(scores - row_peak), axis=1, keepdims=True))
    matched = left[...] == right[...]
    target = jnp.sum(jnp.where(matched, scores, 0.0), axis=1, keepdims=True)
    lane = lax.broadcasted_iota(jnp.int32, (scores.shape[0], lanes), 1)
    packed = jnp.where(lane == 0, row_part, jnp.where(lane == 1, target, 0.0))
    row_out[...] = rows_to_lanes(packed)[:8, :]
    column_peak = jnp.max(scores, axis=0, keepdims=True)
    column_out[...] = column_peak + jnp.log(
        jnp.sum(jnp.exp(scores - column_peak), axis=0, keepdims=True)
    )


def grads_kernel(owners, shards, info, multiplier, left, right, scores, gathered, *rest):
    row_parts = rest[:owners]
    column_parts = rest[owners : owners + shards]
    own_out, *outs, loss_out, total = rest[owners + shards :]
    span = own_out.shape[0]
    row_total = tree([r[0:1, :] for r in row_parts], log_add)
    target = tree([r[1:2, :] for r in row_parts], jnp.add)
    column_total = tree([c[...] for c in column_parts], log_add)
    loss = jnp.sum(row_total - target, axis=1, keepdims=True)
    loss_out[...] = jnp.broadcast_to(loss, loss_out.shape)
    row_total = jnp.transpose(jnp.broadcast_to(row_total, (lanes, row_total.shape[1])))[:, 0:1]
    matched = left[...] == right[...]
    values = scores[...]
    weights = multiplier[0] * (
        jnp.exp(values - row_total)
        + jnp.exp(values - column_total)
        - jnp.where(matched, 2.0, 0.0)
    )
    total[...] = jnp.dot(
        weights.astype(jnp.bfloat16), gathered[...], preferred_element_type=jnp.float32
    )
    for k in range(owners):
        first = pl.multiple_of((info[0] ^ k) * span, span)
        block = total[pl.ds(first, span), :]
        if k == 0:
            own_out[...] = block
        else:
            outs[k - 1][...] = block.astype(jnp.bfloat16)


def sum_kernel(own, *rest):
    value = own[...]
    for part in rest[:-1]:
        value += part[...].astype(jnp.float32)
    rest[-1][...] = value


def body(
    image_features, text_features, image_gain, text_gain, image_proj, text_proj, pair, logit_scale
):
    rows = image_features.shape[0]
    shards = lax.axis_size("mp")
    owners = lax.axis_size("dp")
    span = rows // shards
    width_out = image_proj.shape[1]
    group = lax.axis_index("group")
    me = lax.axis_index("mp")
    owner = lax.axis_index("dp")
    height = width_out // lanes + 8
    f32 = jnp.float32
    shape = jax.ShapeDtypeStruct

    text_side = group == 0
    widest = max(image_features.shape[1], text_features.shape[1])
    width = jnp.where(text_side, text_features.shape[1], image_features.shape[1]) * shards
    info = jnp.stack([text_side.astype(jnp.int32), me, width.astype(jnp.int32)])
    outs = pl.pallas_call(
        functools.partial(project_kernel, shards),
        out_shape=[shape((span, width_out), f32)]
        + [shape((span, width_out), jnp.bfloat16)] * (shards - 1)
        + [shape((height, lanes), f32)] * shards,
        in_specs=[SMEM, ANY, ANY, VMEM, VMEM, ANY, ANY],
        out_specs=[VMEM] * (2 * shards),
        scratch_shapes=[
            pltpu.VMEM((rows, widest), jnp.bfloat16),
            pltpu.VMEM((widest, width_out), jnp.bfloat16),
            pltpu.VMEM((rows, width_out), f32),
            pltpu.VMEM((rows, lanes), f32),
            pltpu.SemaphoreType.DMA((1 + max(1, widest // 512),)),
        ],
        compiler_params=PARAMS,
        name="project",
    )(
        info,
        image_features,
        text_features,
        image_gain[None, :],
        text_gain[None, :],
        image_proj,
        text_proj,
    )
    own, parts, notes = outs[0], outs[1:shards], outs[shards:]
    order = sorted(range(1, shards), key=lambda k: -k)
    parts = {k: exchange(parts[k - 1], "mp", k) for k in order}
    notes = [notes[0]] + [exchange(notes[k], "mp", k) for k in range(1, shards)]
    unit = pl.pallas_call(
        functools.partial(finish_kernel, shards),
        out_shape=shape((span, width_out), jnp.bfloat16),
        in_specs=[SMEM] + [VMEM] * (2 * shards),
        out_specs=VMEM,
        compiler_params=PARAMS,
        name="finish",
    )(info, own, *[parts[k] for k in range(1, shards)], *notes)

    others = [unit] + [exchange(unit, "mp", k) for k in range(1, shards)]
    owns = [cross_exchange(unit, k) for k in range(owners)]

    blocks = pair.reshape(owners, shards, span)
    row_count, column_count = owners * span, shards * span
    numbers = jnp.arange(owners * rows, dtype=jnp.int32).reshape(owners, shards, span)
    image_rows = group == 0
    row_pairs = lax.dynamic_slice_in_dim(blocks, me, 1, 1).reshape(row_count, 1)
    row_ids = lax.dynamic_slice_in_dim(numbers, me, 1, 1).reshape(row_count, 1)
    column_pairs = lax.dynamic_slice_in_dim(pair, owner * column_count, column_count, 0)[None, :]
    column_ids = owner * column_count + jnp.arange(column_count, dtype=jnp.int32)[None, :]
    left = jnp.where(image_rows, row_pairs, row_ids)
    right = jnp.where(image_rows, column_ids, column_pairs)
    place = jnp.stack([owner, me]).astype(jnp.int32)
    multiplier = logit_scale.reshape(1)

    scores, row_part, column_part, gathered = pl.pallas_call(
        functools.partial(scores_kernel, owners, shards),
        out_shape=[
            shape((row_count, column_count), f32),
            shape((8, row_count), f32),
            shape((1, column_count), f32),
            shape((column_count, width_out), jnp.bfloat16),
        ],
        in_specs=[SMEM, SMEM] + [VMEM] * (2 + owners + shards),
        out_specs=[VMEM] * 4,
        scratch_shapes=[pltpu.VMEM((row_count, width_out), jnp.bfloat16)],
        compiler_params=PARAMS,
        name="scores",
    )(place, multiplier, left, right, *owns, *others)
    row_parts = [row_part] + [exchange(row_part, "dp", k) for k in range(1, owners)]
    column_parts = [column_part] + [exchange(column_part, "mp", k) for k in range(1, shards)]

    own_grads, *grad_parts, loss = pl.pallas_call(
        functools.partial(grads_kernel, owners, shards),
        out_shape=[shape((span, width_out), f32)]
        + [shape((span, width_out), jnp.bfloat16)] * (owners - 1)
        + [shape((1, lanes), f32)],
        in_specs=[SMEM, SMEM] + [VMEM] * (4 + owners + shards),
        out_specs=[VMEM] * (owners + 1),
        scratch_shapes=[pltpu.VMEM((row_count, width_out), f32)],
        compiler_params=PARAMS,
        name="grads",
    )(place, multiplier, left, right, scores, gathered, *row_parts, *column_parts)
    grad_parts = [exchange(grad_parts[k - 1], "dp", k) for k in range(1, owners)]
    loss = loss + exchange(loss, "group", 1)
    distance = 1
    while distance < shards:
        loss = loss + exchange(loss, "mp", distance)
        distance *= 2
    loss = loss[0, 0] / (2.0 * owners * rows)
    grads = pl.pallas_call(
        sum_kernel,
        out_shape=shape((span, width_out), f32),
        in_specs=[VMEM] * owners,
        out_specs=VMEM,
        compiler_params=PARAMS,
        name="total",
    )(own_grads, *grad_parts)
    return (grads[None, :, :], loss)


def solution(mesh):
    in_specs = (
        P("dp", "mp"),
        P("dp", "mp"),
        P("mp"),
        P("mp"),
        P("mp", None),
        P("mp", None),
        P(),
        P(),
    )
    out_specs = (P("group", ("dp", "mp"), None), P())
    return jax.shard_map(body, mesh=mesh, in_specs=in_specs, out_specs=out_specs, check_vma=False)
```

time: 187 us -> 76 us (0.41)
  blocking collectives: 83 us -> 0 us
  waiting for transfers between devices: 66.5 us -> 25.5 us
  starting transfers between devices: 3.09 us -> 35.4 us
  between operations: 18.5 us -> 2.61 us
  matrix products: 7.12 us -> 0 us
  Pallas kernels: 0 us -> 5.3 us
  other arithmetic: 4.99 us -> 0.27 us
  local copies, waits for them, and re-layouts: 3.21 us -> 6.57 us
    psum x2 -> x0, blocking collectives: 51.7 us -> none  [the longest x1 38.2 us: body(): summed = lax.psum(partial_loss, ('group', 'dp', 'mp'))]
    all_gather x1 -> x0, waiting for transfers between devices: 38.3 us -> none  [body(): others = lax.all_gather(theirs, ('dp', 'mp'), axis=0, tiled=True)]
    ppermute x2 -> x25, starting transfers between devices: 3.01 us -> 35.4 us  [the longest x21 26.4 us: exchange(): lax.ppermute(shard, axis, [(i, i ^ distance) for i in range(lax.axis_size...]
    unnamed x1 -> x0, blocking collectives: 31.3 us -> none
    reduce_scatter x1 -> x0, waiting for transfers between devices: 24.5 us -> none  [body(): lax.psum_scatter(lax.cond(text_side, lambda: apply(text_features, text_ga...]
    ppermute x2 -> x25, waiting for transfers between devices: 3.6 us -> 25.5 us  [the longest x21 22.9 us: exchange(): lax.ppermute(shard, axis, [(i, i ^ distance) for i in range(lax.axis_size...]
    dot_general x3 -> x0, matrix products: 7.12 us -> none  [the longest x1 3.18 us: apply(): return jnp.dot(normed, projection, preferred_element_type=jnp.float32)]
    pallas_call x0 -> x5, Pallas kernels: none -> 5.3 us  [the longest x1 1.31 us: body(): pl.pallas_call(functools.partial(project_kernel, shards), out_shape=[shap...]
  transfers between devices with their start and end apart: 4 -> 25, of which waited for: 3 -> 10; matrix products, arithmetic and copies ran while one was open for 1% -> 1% of each run, Pallas kernels for 0% -> 0%
where the time goes in v1:
time: 76 us; the launch traced here: 75.6 us
  starting transfers between devices  35.4 us (47%)
  waiting for transfers between devices  25.5 us (34%)
  local copies, waits for them, and re-layouts  6.57 us (9%)
  Pallas kernels  5.3 us (7%)
  between operations  2.61 us (3%)
    ppermute x21, starting transfers between devices, exchange(): lax.ppermute(shard, axis, [(i, i ^ distance) for i in range(lax.axis_size...  26.4 us
    ppermute x21, waiting for transfers between devices, exchange(): lax.ppermute(shard, axis, [(i, i ^ distance) for i in range(lax.axis_size...  22.9 us
    ppermute x4, starting transfers between devices, cross_exchange(): return lax.ppermute(shard, ('group', 'dp'), pairs)  8.98 us
    unnamed x12, local copies, waits for them, and re-layouts  5.65 us
    ppermute x4, waiting for transfers between devices, cross_exchange(): return lax.ppermute(shard, ('group', 'dp'), pairs)  2.57 us
  transfers between devices with their start and end apart: 25, of which 10 were waited for; matrix products, arithmetic and copies ran while one was open for 1% of the time, Pallas kernels for 0%

profile of v1, /device:TPU:0, one launch (start us, length us, event | category | flops | bytes accessed | tf_op | source)
XLA Modules:
  0.0 75.6 jit_solution(17584664682903025003)
XLA Ops:
  0.6 0.7 broadcast_in_dim.11.image_g
  1.4 0.1 pad_add_fusion.1.info
  1.4 1.9 %copy-done = bf16[1536,1024]{1,0:T(8,128)(2,1)S(1)} copy-done((bf16[1536,1024]{1,0:T(8,128)(2,1)S(1)}, bf16[1536,1024]{1,0:T(8,128)(2,1)}, u32[]{:S(2)}) %copy-start) | copy-done | bytes 3145752
  3.3 1.1 %copy-done.1 = bf16[256,1536]{1,0:T(8,128)(2,1)S(1)} copy-done((bf16[256,1536]{1,0:T(8,128)(2,1)S(1)}, bf16[256,1536]{1,0:T(8,128)(2,1)}, u32[]{:S(2)}) %copy-start.1) | copy-done | bytes 786456
  4.5 1.0 %copy-done.2 = bf16[256,1024]{1,0:T(8,128)(2,1)S(1)} copy-done((bf16[256,1024]{1,0:T(8,128)(2,1)S(1)}, bf16[256,1024]{1,0:T(8,128)(2,1)}, u32[]{:S(2)}) %copy-start.2) | copy-done | bytes 524312
  5.5 0.9 %copy-done.3 = bf16[256,256]{1,0:T(8,128)(2,1)S(1)} copy-done((bf16[256,256]{1,0:T(8,128)(2,1)S(1)}, bf16[256,256]{1,0:T(8,128)(2,1)}, u32[]{:S(2)}) %copy-start.3) | copy-done | bytes 131096
  6.4 0.7 copy-done.4
  7.1 1.3 %project.1 = (f32[64,1024]{1,0:T(8,128)S(1)}, bf16[64,1024]{1,0:T(8,128)(2,1)S(1)}, bf16[64,1024]{1,0:T(8,128)(2,1)S(1)}, bf16[64,1024]{1,0:T(8,128)(2,1)S(1)}, ...) custom-call(s32[3]{0:T(128)S(1)} %pad_add_fusion.1.info, ...), custom_call_target="tpu_custom_call" | custom-call | tf_op jit(solution)/shard_map/project/pallas_call | solution.py:241
  8.4 3.1 %collective-permute-start = (bf16[64,1024]{1,0:T(8,128)(2,1)S(1)}, bf16[64,1024]{1,0:T(8,128)(2,1)S(1)}, u32[]{:S(2)}, u32[]{:S(2)}) collective-permute-start(bf16[64,1024]{1,0:T(8,128)(2,1)S(1)} %get-tuple-element.20), channel_id=1, source_target_pairs={{0,1},{1,0},{2,3},{3,2},{4,5},{5,4},{6,7},{7,6},{8,9},{9,8},{10,11... | collective-permute-start | bytes 393224 | tf_op jit(solution)/shard_map/ppermute | solution.py:20
  11.5 2.6 %collective-permute-start.1 = (bf16[64,1024]{1,0:T(8,128)(2,1)S(1)}, bf16[64,1024]{1,0:T(8,128)(2,1)S(1)}, u32[]{:S(2)}, u32[]{:S(2)}) collective-permute-start(bf16[64,1024]{1,0:T(8,128)(2,1)S(1)} %get-tuple-element.21), channel_id=1, source_target_pairs={{0,2},{1,3},{2,0},{3,1},{4,6},{5,7},{6,4},{7,5},{8,10},{9,11},{10,... | collective-permute-start | bytes 393224 | tf_op jit(solution)/shard_map/ppermute | solution.py:20
  14.1 0.0 collective-permute-start.2
  14.1 0.9 %collective-permute-start.3 = (f32[16,128]{1,0:T(8,128)S(1)}, f32[16,128]{1,0:T(8,128)S(1)}, u32[]{:S(2)}, u32[]{:S(2)}) collective-permute-start(f32[16,128]{1,0:T(8,128)S(1)} %get-tuple-element.24), channel_id=1, source_target_pairs={{0,1},{1,0},{2,3},{3,2},{4,5},{5,4},{6,7},{7,6},{8,9},{9,8},{10,11... | collective-permute-start | bytes 24584 | tf_op jit(solution)/shard_map/ppermute | solution.py:20
  15.0 3.5 %collective-permute-start.4 = (f32[16,128]{1,0:T(8,128)S(1)}, f32[16,128]{1,0:T(8,128)S(1)}, u32[]{:S(2)}, u32[]{:S(2)}) collective-permute-start(f32[16,128]{1,0:T(8,128)S(1)} %get-tuple-element.25), channel_id=1, source_target_pairs={{0,2},{1,3},{2,0},{3,1},{4,6},{5,7},{6,4},{7,5},{8,10},{9,11},{10,... | collective-permute-start | bytes 24584 | tf_op jit(solution)/shard_map/ppermute | solution.py:20
  18.5 1.7 %collective-permute-done.3.rest_4_ = f32[16,128]{1,0:T(8,128)S(1)} collective-permute-done((f32[16,128]{1,0:T(8,128)S(1)}, f32[16,128]{1,0:T(8,128)S(1)}, u32[]{:S(2)}, u32[]{:S(2)}) %collective-permute-start.3) | collective-permute-done | bytes 8224 | tf_op jit(solution)/shard_map/ppermute | solution.py:20
  20.2 2.5 %collective-permute-start.5 = (f32[16,128]{1,0:T(8,128)S(1)}, f32[16,128]{1,0:T(8,128)S(1)}, u32[]{:S(2)}, u32[]{:S(2)}) collective-permute-start(f32[16,128]{1,0:T(8,128)S(1)} %get-tuple-element.26), channel_id=1, source_target_pairs={{0,3},{1,2},{2,1},{3,0},{4,7},{5,6},{6,5},{7,4},{8,11},{9,10},{10,... | collective-permute-start | bytes 24584 | tf_op jit(solution)/shard_map/ppermute | solution.py:20
  22.6 3.8 %collective-permute-done.4.rest_5_ = f32[16,128]{1,0:T(8,128)S(1)} collective-permute-done((f32[16,128]{1,0:T(8,128)S(1)}, f32[16,128]{1,0:T(8,128)S(1)}, u32[]{:S(2)}, u32[]{:S(2)}) %collective-permute-start.4) | collective-permute-done | bytes 8224 | tf_op jit(solution)/shard_map/ppermute | solution.py:20
  26.4 0.0 collective-permute-done.5.rest_6_
  26.4 0.0 collective-permute-done.rest_0_
  26.4 0.0 collective-permute-done.1.rest_1_
  26.4 0.0 collective-permute-done.2.rest_2_
  26.5 0.9 %finish.1.rest_4_ = bf16[64,1024]{1,0:T(8,128)(2,1)S(1)} custom-call(s32[3]{0:T(128)S(1)} %pad_add_fusion.1.info, f32[64,1024]{1,0:T(8,128)S(1)} %get-tuple-element.19.own, bf16[64,1024]{1,0:T(8,128)(2,1)S(1)} %collective-permute-done.rest_0_, bf16[64,1024]{1,0:T(8,128)(2,1)S(1)} %collective-permute-done.1.rest_1_, ...), custom_call_target="tpu_custom_call" | custom-call | tf_op jit(solution)/shard_map/finish/pallas_call | solution.py:270
  27.4 2.5 %collective-permute-start.12 = (bf16[64,1024]{1,0:T(8,128)(2,1)S(1)}, bf16[64,1024]{1,0:T(8,128)(2,1)S(1)}, u32[]{:S(2)}, u32[]{:S(2)}) collective-permute-start(bf16[64,1024]{1,0:T(8,128)(2,1)S(1)} %finish.1.rest_4_), channel_id=1, source_target_pairs={{0,3},{1,2},{2,1},{3,0},{4,7},{5,6},{6,5},{7,4},{8,11},{9,10},{10,... | collective-permute-start | bytes 393224 | tf_op jit(solution)/shard_map/ppermute | solution.py:20
  29.9 0.0 collective-permute-start.11
  29.9 1.9 %collective-permute-start.10 = (bf16[64,1024]{1,0:T(8,128)(2,1)S(1)}, bf16[64,1024]{1,0:T(8,128)(2,1)S(1)}, u32[]{:S(2)}, u32[]{:S(2)}) collective-permute-start(bf16[64,1024]{1,0:T(8,128)(2,1)S(1)} %finish.1.rest_4_), channel_id=1, source_target_pairs={{0,1},{1,0},{2,3},{3,2},{4,5},{5,4},{6,7},{7,6},{8,9},{9,8},{10,11... | collective-permute-start | bytes 393224 | tf_op jit(solution)/shard_map/ppermute | solution.py:20
  31.9 1.4 %collective-permute-start.9 = (bf16[64,1024]{1,0:T(8,128)(2,1)S(1)}, bf16[64,1024]{1,0:T(8,128)(2,1)S(1)}, u32[]{:S(2)}, u32[]{:S(2)}) collective-permute-start(bf16[64,1024]{1,0:T(8,128)(2,1)S(1)} %finish.1.rest_4_), channel_id=1, source_target_pairs={{0,28},{4,24},{8,20},{12,16},{16,12},{20,8},{24,4},{28,0},{1,29},{... | collective-permute-start | bytes 393224 | tf_op jit(solution)/shard_map/ppermute | solution.py:30
  33.3 2.9 %collective-permute-start.8 = (bf16[64,1024]{1,0:T(8,128)(2,1)S(1)}, bf16[64,1024]{1,0:T(8,128)(2,1)S(1)}, u32[]{:S(2)}, u32[]{:S(2)}) collective-permute-start(bf16[64,1024]{1,0:T(8,128)(2,1)S(1)} %finish.1.rest_4_), channel_id=1, source_target_pairs={{0,24},{4,28},{8,16},{12,20},{16,8},{20,12},{24,0},{28,4},{1,25},{... | collective-permute-start | bytes 393224 | tf_op jit(solution)/shard_map/ppermute | solution.py:30
  36.1 0.0 collective-permute-done.12.rest_7_
  36.2 1.4 %collective-permute-start.7 = (bf16[64,1024]{1,0:T(8,128)(2,1)S(1)}, bf16[64,1024]{1,0:T(8,128)(2,1)S(1)}, u32[]{:S(2)}, u32[]{:S(2)}) collective-permute-start(bf16[64,1024]{1,0:T(8,128)(2,1)S(1)} %finish.1.rest_4_), channel_id=1, source_target_pairs={{0,20},{4,16},{8,28},{12,24},{16,4},{20,0},{24,12},{28,8},{1,21},{... | collective-permute-start | bytes 393224 | tf_op jit(solution)/shard_map/ppermute | solution.py:30
  37.5 2.5 %collective-permute-done.11.rest_6_ = bf16[64,1024]{1,0:T(8,128)(2,1)S(1)} collective-permute-done((bf16[64,1024]{1,0:T(8,128)(2,1)S(1)}, bf16[64,1024]{1,0:T(8,128)(2,1)S(1)}, u32[]{:S(2)}, u32[]{:S(2)}) %collective-permute-start.11) | collective-permute-done | bytes 131104 | tf_op jit(solution)/shard_map/ppermute | solution.py:20
  40.1 3.3 %collective-permute-start.6 = (bf16[64,1024]{1,0:T(8,128)(2,1)S(1)}, bf16[64,1024]{1,0:T(8,128)(2,1)S(1)}, u32[]{:S(2)}, u32[]{:S(2)}) collective-permute-start(bf16[64,1024]{1,0:T(8,128)(2,1)S(1)} %finish.1.rest_4_), channel_id=1, source_target_pairs={{0,16},{4,20},{8,24},{12,28},{16,0},{20,4},{24,8},{28,12},{1,17},{... | collective-permute-start | bytes 393224 | tf_op jit(solution)/shard_map/ppermute | solution.py:30
  43.4 0.1 pad_add_fusion.info
  44.1 0.1 reshape.53
  44.2 0.1 select_n.40.left
  44.4 0.1 dynamic-slice_select_fusion
  44.4 0.0 collective-permute-done.10.rest_5_
  44.4 0.0 collective-permute-done.9.rest_3_
  44.4 0.0 collective-permute-done.8.rest_2_
  44.5 0.0 collective-permute-done.7.rest_1_
  44.5 2.6 %collective-permute-done.6.rest_0_ = bf16[64,1024]{1,0:T(8,128)(2,1)S(1)} collective-permute-done((bf16[64,1024]{1,0:T(8,128)(2,1)S(1)}, bf16[64,1024]{1,0:T(8,128)(2,1)S(1)}, u32[]{:S(2)}, u32[]{:S(2)}) %collective-permute-start.6) | collective-permute-done | bytes 131104 | tf_op jit(solution)/shard_map/ppermute | solution.py:30
  47.0 1.1 %scores.1 = (f32[256,256]{1,0:T(8,128)S(1)}, f32[8,256]{1,0:T(8,128)S(1)}, f32[1,256]{1,0:T(1,128)S(1)}, bf16[256,1024]{1,0:T(8,128)(2,1)S(1)}) custom-call(s32[2]{0:T(128)S(1)} %pad_add_fusion.info, f32[1]{0:T(128)} %bitcast.10.multiplier, s32[256,1]{1,0:T(8,128)S(1)} %select_n.40.left, s32[1,256]{1,0:T(1,128)S(1)} %bitcast.12, ...), custom_call_target="tpu_custom_call" | custom-call | tf_op jit(solution)/shard_map/scores/pallas_call | solution.py:295
  48.2 0.0 collective-permute-start.15
  48.2 1.1 %collective-permute-start.14 = (f32[8,256]{1,0:T(8,128)S(1)}, f32[8,256]{1,0:T(8,128)S(1)}, u32[]{:S(2)}, u32[]{:S(2)}) collective-permute-start(f32[8,256]{1,0:T(8,128)S(1)} %get-tuple-element.29.rest_0_), channel_id=1, source_target_pairs={{0,8},{4,12},{8,0},{12,4},{1,9},{5,13},{9,1},{13,5},{2,10},{6,14},... | collective-permute-start | bytes 24584 | tf_op jit(solution)/shard_map/ppermute | solution.py:20
  49.3 0.8 %collective-permute-start.13 = (f32[8,256]{1,0:T(8,128)S(1)}, f32[8,256]{1,0:T(8,128)S(1)}, u32[]{:S(2)}, u32[]{:S(2)}) collective-permute-start(f32[8,256]{1,0:T(8,128)S(1)} %get-tuple-element.29.rest_0_), channel_id=1, source_target_pairs={{0,4},{4,0},{8,12},{12,8},{1,5},{5,1},{9,13},{13,9},{2,6},{6,2},{1... | collective-permute-start | bytes 24584 | tf_op jit(solution)/shard_map/ppermute | solution.py:20
  50.1 2.5 %collective-permute-start.18 = (f32[1,256]{1,0:T(1,128)S(1)}, f32[1,256]{1,0:T(1,128)S(1)}, u32[]{:S(2)}, u32[]{:S(2)}) collective-permute-start(f32[1,256]{1,0:T(1,128)S(1)} %get-tuple-element.30.rest_4_), channel_id=1, source_target_pairs={{0,3},{1,2},{2,1},{3,0},{4,7},{5,6},{6,5},{7,4},{8,11},{9,10},{10,... | collective-permute-start | bytes 3080 | tf_op jit(solution)/shard_map/ppermute | solution.py:20
  52.5 0.2 collective-permute-start.17
  52.7 2.7 %collective-permute-done.18.rest_7_ = f32[1,256]{1,0:T(1,128)S(1)} collective-permute-done((f32[1,256]{1,0:T(1,128)S(1)}, f32[1,256]{1,0:T(1,128)S(1)}, u32[]{:S(2)}, u32[]{:S(2)}) %collective-permute-start.18) | collective-permute-done | bytes 1056 | tf_op jit(solution)/shard_map/ppermute | solution.py:20
  55.4 0.0 collective-permute-start.16
  55.4 1.6 %collective-permute-done.17.rest_6_ = f32[1,256]{1,0:T(1,128)S(1)} collective-permute-done((f32[1,256]{1,0:T(1,128)S(1)}, f32[1,256]{1,0:T(1,128)S(1)}, u32[]{:S(2)}, u32[]{:S(2)}) %collective-permute-start.17) | collective-permute-done | bytes 1056 | tf_op jit(solution)/shard_map/ppermute | solution.py:20
  57.0 2.0 %collective-permute-done.16.rest_5_ = f32[1,256]{1,0:T(1,128)S(1)} collective-permute-done((f32[1,256]{1,0:T(1,128)S(1)}, f32[1,256]{1,0:T(1,128)S(1)}, u32[]{:S(2)}, u32[]{:S(2)}) %collective-permute-start.16) | collective-permute-done | bytes 1056 | tf_op jit(solution)/shard_map/ppermute | solution.py:20
  59.0 0.0 collective-permute-done.15.rest_3_
  59.0 0.0 collective-permute-done.14.rest_2_
  59.0 1.1 %grads.1 = (f32[64,1024]{1,0:T(8,128)S(1)}, bf16[64,1024]{1,0:T(8,128)(2,1)S(1)}, bf16[64,1024]{1,0:T(8,128)(2,1)S(1)}, bf16[64,1024]{1,0:T(8,128)(2,1)S(1)}, f32[1,128]{1,0:T(1,128)S(1)}) custom-call(s32[2]{0:T(128)S(1)} %pad_add_fusion.info, f32[1]{0:T(128)} %bitcast.11.multiplier, s32[256,1]{1,0:T(8,128)S(1)} %select_n.40.left, s32[1,256]{1,0:T(1,128)S(1)} %bitcast.13, ...), custom_call_target="tpu_custom_call" | custom-call | tf_op jit(solution)/shard_map/grads/pallas_call | solution.py:312
  60.2 0.1 collective-permute-start.19
  60.3 1.1 %collective-permute-start.20 = (bf16[64,1024]{1,0:T(8,128)(2,1)S(1)}, bf16[64,1024]{1,0:T(8,128)(2,1)S(1)}, u32[]{:S(2)}, u32[]{:S(2)}) collective-permute-start(bf16[64,1024]{1,0:T(8,128)(2,1)S(1)} %get-tuple-element.33), channel_id=1, source_target_pairs={{0,8},{4,12},{8,0},{12,4},{1,9},{5,13},{9,1},{13,5},{2,10},{6,14},... | collective-permute-start | bytes 393224 | tf_op jit(solution)/shard_map/ppermute | solution.py:20
  61.3 0.8 %collective-permute-start.21 = (bf16[64,1024]{1,0:T(8,128)(2,1)S(1)}, bf16[64,1024]{1,0:T(8,128)(2,1)S(1)}, u32[]{:S(2)}, u32[]{:S(2)}) collective-permute-start(bf16[64,1024]{1,0:T(8,128)(2,1)S(1)} %get-tuple-element.34), channel_id=1, source_target_pairs={{0,12},{4,8},{8,4},{12,0},{1,13},{5,9},{9,5},{13,1},{2,14},{6,10},... | collective-permute-start | bytes 393224 | tf_op jit(solution)/shard_map/ppermute | solution.py:20
  62.1 1.9 %collective-permute-start.22 = (f32[1,128]{1,0:T(1,128)S(1)}, f32[1,128]{1,0:T(1,128)S(1)}, u32[]{:S(2)}, u32[]{:S(2)}) collective-permute-start(f32[1,128]{1,0:T(1,128)S(1)} %get-tuple-element.35), channel_id=1, source_target_pairs={{0,16},{16,0},{1,17},{17,1},{2,18},{18,2},{3,19},{19,3},{4,20},{20... | collective-permute-start | bytes 1544 | tf_op jit(solution)/shard_map/ppermute | solution.py:20
  64.0 1.6 %collective-permute-done.22 = f32[1,128]{1,0:T(1,128)S(1)} collective-permute-done((f32[1,128]{1,0:T(1,128)S(1)}, f32[1,128]{1,0:T(1,128)S(1)}, u32[]{:S(2)}, u32[]{:S(2)}) %collective-permute-start.22) | collective-permute-done | bytes 544 | tf_op jit(solution)/shard_map/ppermute | solution.py:20
  65.7 0.0 collective-permute-start.23
  65.7 3.5 %collective-permute-done.23 = f32[1,128]{1,0:T(1,128)S(1)} collective-permute-done((f32[1,128]{1,0:T(1,128)S(1)}, f32[1,128]{1,0:T(1,128)S(1)}, u32[]{:S(2)}, u32[]{:S(2)}) %collective-permute-start.23) | collective-permute-done | bytes 544 | tf_op jit(solution)/shard_map/ppermute | solution.py:20
  69.2 1.0 %collective-permute-start.24 = (f32[1,128]{1,0:T(1,128)S(1)}, f32[1,128]{1,0:T(1,128)S(1)}, u32[]{:S(2)}, u32[]{:S(2)}) collective-permute-start(f32[1,128]{1,0:T(1,128)S(1)} %add.30), channel_id=1, source_target_pairs={{0,2},{1,3},{2,0},{3,1},{4,6},{5,7},{6,4},{7,5},{8,10},{9,11},{10,... | collective-permute-start | bytes 1544 | tf_op jit(solution)/shard_map/ppermute | solution.py:20
  70.2 3.4 %collective-permute-done.24 = f32[1,128]{1,0:T(1,128)S(1)} collective-permute-done((f32[1,128]{1,0:T(1,128)S(1)}, f32[1,128]{1,0:T(1,128)S(1)}, u32[]{:S(2)}, u32[]{:S(2)}) %collective-permute-start.24) | collective-permute-done | bytes 544 | tf_op jit(solution)/shard_map/ppermute | solution.py:20
  73.7 0.0 collective-permute-done.20.rest_1_
  73.7 0.0 collective-permute-done.21.rest_2_
  73.7 0.8 %total.1 = f32[64,1024]{1,0:T(8,128)} custom-call(f32[64,1024]{1,0:T(8,128)S(1)} %get-tuple-element.31.own, bf16[64,1024]{1,0:T(8,128)(2,1)S(1)} %collective-permute-done.19.rest_0_, bf16[64,1024]{1,0:T(8,128)(2,1)S(1)} %collective-permute-done.20.rest_1_, bf16[64,1024]{1,0:T(8,128)(2,1)S(1)} %collective-permute-done.21.rest_2_), custom_call_target="tpu_custom_call" | custom-call | tf_op jit(solution)/shard_map/total/pallas_call | solution.py:330
  (13 shorter events, 0.1 us)
Async XLA Ops:
  0.6 43.5 %copy-start.5 = (s32[1024]{0:T(1024)S(1)}, s32[1024]{0:T(1024)}, u32[]{:S(2)}) copy-start(s32[1024]{0:T(1024)} %param.14) | copy-start | bytes 12292
  1.4 1.9 %copy-start = (bf16[1536,1024]{1,0:T(8,128)(2,1)S(1)}, bf16[1536,1024]{1,0:T(8,128)(2,1)}, u32[]{:S(2)}) copy-start(bf16[1536,1024]{1,0:T(8,128)(2,1)} %image_p.1) | copy-start | bytes 9437188
  3.3 1.1 %copy-start.1 = (bf16[256,1536]{1,0:T(8,128)(2,1)S(1)}, bf16[256,1536]{1,0:T(8,128)(2,1)}, u32[]{:S(2)}) copy-start(bf16[256,1536]{1,0:T(8,128)(2,1)} %image_x.1) | copy-start | bytes 2359300
  4.5 1.0 %copy-start.2 = (bf16[256,1024]{1,0:T(8,128)(2,1)S(1)}, bf16[256,1024]{1,0:T(8,128)(2,1)}, u32[]{:S(2)}) copy-start(bf16[256,1024]{1,0:T(8,128)(2,1)} %text_p.1) | copy-start | bytes 1572868
  5.5 0.9 %copy-start.3 = (bf16[256,256]{1,0:T(8,128)(2,1)S(1)}, bf16[256,256]{1,0:T(8,128)(2,1)}, u32[]{:S(2)}) copy-start(bf16[256,256]{1,0:T(8,128)(2,1)} %text_x.1) | copy-start | bytes 393220
  6.4 0.7 copy-start.4
  8.4 18.0 %collective-permute-start = (bf16[64,1024]{1,0:T(8,128)(2,1)S(1)}, bf16[64,1024]{1,0:T(8,128)(2,1)S(1)}, u32[]{:S(2)}, u32[]{:S(2)}) collective-permute-start(bf16[64,1024]{1,0:T(8,128)(2,1)S(1)} %get-tuple-element.20), channel_id=1, source_target_pairs={{0,1},{1,0},{2,3},{3,2},{4,5},{5,4},{6,7},{7,6},{8,9},{9,8},{10,11... | collective-permute-start | bytes 393224 | tf_op jit(solution)/shard_map/ppermute | solution.py:20
  11.5 15.0 %collective-permute-start.1 = (bf16[64,1024]{1,0:T(8,128)(2,1)S(1)}, bf16[64,1024]{1,0:T(8,128)(2,1)S(1)}, u32[]{:S(2)}, u32[]{:S(2)}) collective-permute-start(bf16[64,1024]{1,0:T(8,128)(2,1)S(1)} %get-tuple-element.21), channel_id=1, source_target_pairs={{0,2},{1,3},{2,0},{3,1},{4,6},{5,7},{6,4},{7,5},{8,10},{9,11},{10,... | collective-permute-start | bytes 393224 | tf_op jit(solution)/shard_map/ppermute | solution.py:20
  14.1 12.4 %collective-permute-start.2 = (bf16[64,1024]{1,0:T(8,128)(2,1)S(1)}, bf16[64,1024]{1,0:T(8,128)(2,1)S(1)}, u32[]{:S(2)}, u32[]{:S(2)}) collective-permute-start(bf16[64,1024]{1,0:T(8,128)(2,1)S(1)} %get-tuple-element.22), channel_id=1, source_target_pairs={{0,3},{1,2},{2,1},{3,0},{4,7},{5,6},{6,5},{7,4},{8,11},{9,10},{10,... | collective-permute-start | bytes 393224 | tf_op jit(solution)/shard_map/ppermute | solution.py:20
  14.1 6.1 %collective-permute-start.3 = (f32[16,128]{1,0:T(8,128)S(1)}, f32[16,128]{1,0:T(8,128)S(1)}, u32[]{:S(2)}, u32[]{:S(2)}) collective-permute-start(f32[16,128]{1,0:T(8,128)S(1)} %get-tuple-element.24), channel_id=1, source_target_pairs={{0,1},{1,0},{2,3},{3,2},{4,5},{5,4},{6,7},{7,6},{8,9},{9,8},{10,11... | collective-permute-start | bytes 24584 | tf_op jit(solution)/shard_map/ppermute | solution.py:20
  15.0 11.5 %collective-permute-start.4 = (f32[16,128]{1,0:T(8,128)S(1)}, f32[16,128]{1,0:T(8,128)S(1)}, u32[]{:S(2)}, u32[]{:S(2)}) collective-permute-start(f32[16,128]{1,0:T(8,128)S(1)} %get-tuple-element.25), channel_id=1, source_target_pairs={{0,2},{1,3},{2,0},{3,1},{4,6},{5,7},{6,4},{7,5},{8,10},{9,11},{10,... | collective-permute-start | bytes 24584 | tf_op jit(solution)/shard_map/ppermute | solution.py:20
  20.2 6.3 %collective-permute-start.5 = (f32[16,128]{1,0:T(8,128)S(1)}, f32[16,128]{1,0:T(8,128)S(1)}, u32[]{:S(2)}, u32[]{:S(2)}) collective-permute-start(f32[16,128]{1,0:T(8,128)S(1)} %get-tuple-element.26), channel_id=1, source_target_pairs={{0,3},{1,2},{2,1},{3,0},{4,7},{5,6},{6,5},{7,4},{8,11},{9,10},{10,... | collective-permute-start | bytes 24584 | tf_op jit(solution)/shard_map/ppermute | solution.py:20
  27.4 8.8 %collective-permute-start.12 = (bf16[64,1024]{1,0:T(8,128)(2,1)S(1)}, bf16[64,1024]{1,0:T(8,128)(2,1)S(1)}, u32[]{:S(2)}, u32[]{:S(2)}) collective-permute-start(bf16[64,1024]{1,0:T(8,128)(2,1)S(1)} %finish.1.rest_4_), channel_id=1, source_target_pairs={{0,3},{1,2},{2,1},{3,0},{4,7},{5,6},{6,5},{7,4},{8,11},{9,10},{10,... | collective-permute-start | bytes 393224 | tf_op jit(solution)/shard_map/ppermute | solution.py:20
  29.9 10.1 %collective-permute-start.11 = (bf16[64,1024]{1,0:T(8,128)(2,1)S(1)}, bf16[64,1024]{1,0:T(8,128)(2,1)S(1)}, u32[]{:S(2)}, u32[]{:S(2)}) collective-permute-start(bf16[64,1024]{1,0:T(8,128)(2,1)S(1)} %finish.1.rest_4_), channel_id=1, source_target_pairs={{0,2},{1,3},{2,0},{3,1},{4,6},{5,7},{6,4},{7,5},{8,10},{9,11},{10,... | collective-permute-start | bytes 393224 | tf_op jit(solution)/shard_map/ppermute | solution.py:20
  29.9 14.5 %collective-permute-start.10 = (bf16[64,1024]{1,0:T(8,128)(2,1)S(1)}, bf16[64,1024]{1,0:T(8,128)(2,1)S(1)}, u32[]{:S(2)}, u32[]{:S(2)}) collective-permute-start(bf16[64,1024]{1,0:T(8,128)(2,1)S(1)} %finish.1.rest_4_), channel_id=1, source_target_pairs={{0,1},{1,0},{2,3},{3,2},{4,5},{5,4},{6,7},{7,6},{8,9},{9,8},{10,11... | collective-permute-start | bytes 393224 | tf_op jit(solution)/shard_map/ppermute | solution.py:20
  31.9 12.6 %collective-permute-start.9 = (bf16[64,1024]{1,0:T(8,128)(2,1)S(1)}, bf16[64,1024]{1,0:T(8,128)(2,1)S(1)}, u32[]{:S(2)}, u32[]{:S(2)}) collective-permute-start(bf16[64,1024]{1,0:T(8,128)(2,1)S(1)} %finish.1.rest_4_), channel_id=1, source_target_pairs={{0,28},{4,24},{8,20},{12,16},{16,12},{20,8},{24,4},{28,0},{1,29},{... | collective-permute-start | bytes 393224 | tf_op jit(solution)/shard_map/ppermute | solution.py:30
  33.3 11.2 %collective-permute-start.8 = (bf16[64,1024]{1,0:T(8,128)(2,1)S(1)}, bf16[64,1024]{1,0:T(8,128)(2,1)S(1)}, u32[]{:S(2)}, u32[]{:S(2)}) collective-permute-start(bf16[64,1024]{1,0:T(8,128)(2,1)S(1)} %finish.1.rest_4_), channel_id=1, source_target_pairs={{0,24},{4,28},{8,16},{12,20},{16,8},{20,12},{24,0},{28,4},{1,25},{... | collective-permute-start | bytes 393224 | tf_op jit(solution)/shard_map/ppermute | solution.py:30
  36.2 8.3 %collective-permute-start.7 = (bf16[64,1024]{1,0:T(8,128)(2,1)S(1)}, bf16[64,1024]{1,0:T(8,128)(2,1)S(1)}, u32[]{:S(2)}, u32[]{:S(2)}) collective-permute-start(bf16[64,1024]{1,0:T(8,128)(2,1)S(1)} %finish.1.rest_4_), channel_id=1, source_target_pairs={{0,20},{4,16},{8,28},{12,24},{16,4},{20,0},{24,12},{28,8},{1,21},{... | collective-permute-start | bytes 393224 | tf_op jit(solution)/shard_map/ppermute | solution.py:30
  40.1 7.0 %collective-permute-start.6 = (bf16[64,1024]{1,0:T(8,128)(2,1)S(1)}, bf16[64,1024]{1,0:T(8,128)(2,1)S(1)}, u32[]{:S(2)}, u32[]{:S(2)}) collective-permute-start(bf16[64,1024]{1,0:T(8,128)(2,1)S(1)} %finish.1.rest_4_), channel_id=1, source_target_pairs={{0,16},{4,20},{8,24},{12,28},{16,0},{20,4},{24,8},{28,12},{1,17},{... | collective-permute-start | bytes 393224 | tf_op jit(solution)/shard_map/ppermute | solution.py:30
  48.2 10.8 %collective-permute-start.15 = (f32[8,256]{1,0:T(8,128)S(1)}, f32[8,256]{1,0:T(8,128)S(1)}, u32[]{:S(2)}, u32[]{:S(2)}) collective-permute-start(f32[8,256]{1,0:T(8,128)S(1)} %get-tuple-element.29.rest_0_), channel_id=1, source_target_pairs={{0,12},{4,8},{8,4},{12,0},{1,13},{5,9},{9,5},{13,1},{2,14},{6,10},... | collective-permute-start | bytes 24584 | tf_op jit(solution)/shard_map/ppermute | solution.py:20
  48.2 10.8 %collective-permute-start.14 = (f32[8,256]{1,0:T(8,128)S(1)}, f32[8,256]{1,0:T(8,128)S(1)}, u32[]{:S(2)}, u32[]{:S(2)}) collective-permute-start(f32[8,256]{1,0:T(8,128)S(1)} %get-tuple-element.29.rest_0_), channel_id=1, source_target_pairs={{0,8},{4,12},{8,0},{12,4},{1,9},{5,13},{9,1},{13,5},{2,10},{6,14},... | collective-permute-start | bytes 24584 | tf_op jit(solution)/shard_map/ppermute | solution.py:20
  49.3 9.7 %collective-permute-start.13 = (f32[8,256]{1,0:T(8,128)S(1)}, f32[8,256]{1,0:T(8,128)S(1)}, u32[]{:S(2)}, u32[]{:S(2)}) collective-permute-start(f32[8,256]{1,0:T(8,128)S(1)} %get-tuple-element.29.rest_0_), channel_id=1, source_target_pairs={{0,4},{4,0},{8,12},{12,8},{1,5},{5,1},{9,13},{13,9},{2,6},{6,2},{1... | collective-permute-start | bytes 24584 | tf_op jit(solution)/shard_map/ppermute | solution.py:20
  50.1 5.4 %collective-permute-start.18 = (f32[1,256]{1,0:T(1,128)S(1)}, f32[1,256]{1,0:T(1,128)S(1)}, u32[]{:S(2)}, u32[]{:S(2)}) collective-permute-start(f32[1,256]{1,0:T(1,128)S(1)} %get-tuple-element.30.rest_4_), channel_id=1, source_target_pairs={{0,3},{1,2},{2,1},{3,0},{4,7},{5,6},{6,5},{7,4},{8,11},{9,10},{10,... | collective-permute-start | bytes 3080 | tf_op jit(solution)/shard_map/ppermute | solution.py:20
  52.5 4.5 %collective-permute-start.17 = (f32[1,256]{1,0:T(1,128)S(1)}, f32[1,256]{1,0:T(1,128)S(1)}, u32[]{:S(2)}, u32[]{:S(2)}) collective-permute-start(f32[1,256]{1,0:T(1,128)S(1)} %get-tuple-element.30.rest_4_), channel_id=1, source_target_pairs={{0,2},{1,3},{2,0},{3,1},{4,6},{5,7},{6,4},{7,5},{8,10},{9,11},{10,... | collective-permute-start | bytes 3080 | tf_op jit(solution)/shard_map/ppermute | solution.py:20
  55.4 3.6 %collective-permute-start.16 = (f32[1,256]{1,0:T(1,128)S(1)}, f32[1,256]{1,0:T(1,128)S(1)}, u32[]{:S(2)}, u32[]{:S(2)}) collective-permute-start(f32[1,256]{1,0:T(1,128)S(1)} %get-tuple-element.30.rest_4_), channel_id=1, source_target_pairs={{0,1},{1,0},{2,3},{3,2},{4,5},{5,4},{6,7},{7,6},{8,9},{9,8},{10,11... | collective-permute-start | bytes 3080 | tf_op jit(solution)/shard_map/ppermute | solution.py:20
  60.2 13.5 %collective-permute-start.19 = (bf16[64,1024]{1,0:T(8,128)(2,1)S(1)}, bf16[64,1024]{1,0:T(8,128)(2,1)S(1)}, u32[]{:S(2)}, u32[]{:S(2)}) collective-permute-start(bf16[64,1024]{1,0:T(8,128)(2,1)S(1)} %get-tuple-element.32), channel_id=1, source_target_pairs={{0,4},{4,0},{8,12},{12,8},{1,5},{5,1},{9,13},{13,9},{2,6},{6,2},{1... | collective-permute-start | bytes 393224 | tf_op jit(solution)/shard_map/ppermute | solution.py:20
  60.3 13.5 %collective-permute-start.20 = (bf16[64,1024]{1,0:T(8,128)(2,1)S(1)}, bf16[64,1024]{1,0:T(8,128)(2,1)S(1)}, u32[]{:S(2)}, u32[]{:S(2)}) collective-permute-start(bf16[64,1024]{1,0:T(8,128)(2,1)S(1)} %get-tuple-element.33), channel_id=1, source_target_pairs={{0,8},{4,12},{8,0},{12,4},{1,9},{5,13},{9,1},{13,5},{2,10},{6,14},... | collective-permute-start | bytes 393224 | tf_op jit(solution)/shard_map/ppermute | solution.py:20
  61.3 12.4 %collective-permute-start.21 = (bf16[64,1024]{1,0:T(8,128)(2,1)S(1)}, bf16[64,1024]{1,0:T(8,128)(2,1)S(1)}, u32[]{:S(2)}, u32[]{:S(2)}) collective-permute-start(bf16[64,1024]{1,0:T(8,128)(2,1)S(1)} %get-tuple-element.34), channel_id=1, source_target_pairs={{0,12},{4,8},{8,4},{12,0},{1,13},{5,9},{9,5},{13,1},{2,14},{6,10},... | collective-permute-start | bytes 393224 | tf_op jit(solution)/shard_map/ppermute | solution.py:20
  62.1 3.5 %collective-permute-start.22 = (f32[1,128]{1,0:T(1,128)S(1)}, f32[1,128]{1,0:T(1,128)S(1)}, u32[]{:S(2)}, u32[]{:S(2)}) collective-permute-start(f32[1,128]{1,0:T(1,128)S(1)} %get-tuple-element.35), channel_id=1, source_target_pairs={{0,16},{16,0},{1,17},{17,1},{2,18},{18,2},{3,19},{19,3},{4,20},{20... | collective-permute-start | bytes 1544 | tf_op jit(solution)/shard_map/ppermute | solution.py:20
  65.7 3.5 %collective-permute-start.23 = (f32[1,128]{1,0:T(1,128)S(1)}, f32[1,128]{1,0:T(1,128)S(1)}, u32[]{:S(2)}, u32[]{:S(2)}) collective-permute-start(f32[1,128]{1,0:T(1,128)S(1)} %add.29), channel_id=1, source_target_pairs={{0,1},{1,0},{2,3},{3,2},{4,5},{5,4},{6,7},{7,6},{8,9},{9,8},{10,11... | collective-permute-start | bytes 1544 | tf_op jit(solution)/shard_map/ppermute | solution.py:20
  69.2 4.4 %collective-permute-start.24 = (f32[1,128]{1,0:T(1,128)S(1)}, f32[1,128]{1,0:T(1,128)S(1)}, u32[]{:S(2)}, u32[]{:S(2)}) collective-permute-start(f32[1,128]{1,0:T(1,128)S(1)} %add.30), channel_id=1, source_target_pairs={{0,2},{1,3},{2,0},{3,1},{4,6},{5,7},{6,4},{7,5},{8,10},{9,11},{10,... | collective-permute-start | bytes 1544 | tf_op jit(solution)/shard_map/ppermute | solution.py:20

commit v2 on v1

v2 whole, which is shorter than its diff:
```python
import functools

import jax
import jax.numpy as jnp
from jax import lax
from jax.experimental import pallas as pl
from jax.experimental.pallas import tpu as pltpu
from jax.sharding import PartitionSpec as P

norm_epsilon = 1e-05
unit_epsilon = 1e-06
lanes = 128
VMEM = pl.BlockSpec(memory_space=pltpu.VMEM)
SMEM = pl.BlockSpec(memory_space=pltpu.SMEM)
HBM = pl.BlockSpec(memory_space=pltpu.HBM)
PARAMS_P = pltpu.CompilerParams(vmem_limit_bytes=55500000)
PARAMS = pltpu.CompilerParams(vmem_limit_bytes=48 * 1024 * 1024)
f32 = jnp.float32
bf16 = jnp.bfloat16


def exchange(shard, axis, distance):
    return lax.ppermute(shard, axis, [(i, i ^ distance) for i in range(lax.axis_size(axis))])


def cross_exchange(shard, distance):
    count = lax.axis_size("mp")
    pairs = [
        (side * count + i, (1 - side) * count + (i ^ distance))
        for side in range(2)
        for i in range(count)
    ]
    return lax.ppermute(shard, ("group", "mp"), pairs)


def tree(values, combine):
    values = list(values)
    while len(values) > 1:
        values = [combine(values[i], values[i + 1]) for i in range(0, len(values), 2)]
    return values[0]


def log_add(a, b):
    peak = jnp.maximum(a, b)
    return peak + jnp.log1p(jnp.exp(jnp.minimum(a, b) - peak))


def merge_columns(a, b):
    row = lax.broadcasted_iota(jnp.int32, a.shape, 0)
    return jnp.where(row == 0, log_add(a, b), a + b)


def project_kernel(shards, image_x, text_x, image_g, text_g, image_p, text_p, *rest):
    own_out = rest[0]
    parts = rest[1:shards]
    note = rest[shards]
    x_buf, p_buf, total, sems = rest[shards + 1 :]
    rows = x_buf.shape[0]
    span = rows // shards
    width_out = total.shape[1]
    me = lax.axis_index("mp")

    def tower(x_hbm, gain, p_hbm):
        width = x_hbm.shape[1]
        step = min(width, 512)
        chunks = width // step
        x_copy = pltpu.make_async_copy(x_hbm, x_buf.at[:, pl.ds(0, width)], sems.at[0])
        x_copy.start()
        copies = []
        for c in range(chunks):
            copy = pltpu.make_async_copy(
                p_hbm.at[pl.ds(c * step, step)], p_buf.at[pl.ds(c * step, step)], sems.at[1 + c]
            )
            copy.start()
            copies.append(copy)
        x_copy.wait()
        values = x_buf[:, :width].astype(f32)
        mean = jnp.sum(values, axis=1, keepdims=True) / width
        spread = jnp.sum((values - mean) * (values - mean), axis=1, keepdims=True)
        lane = lax.broadcasted_iota(jnp.int32, (rows, lanes), 1)
        stats = jnp.transpose(jnp.where(lane == 0, mean, jnp.where(lane == 1, spread, 0.0)))
        offset = jnp.zeros((16, width_out), f32)
        for c in range(chunks):
            g = gain[c * step : (c + 1) * step].reshape(1, step)
            high = g.astype(bf16).astype(f32)
            middle = (g - high).astype(bf16).astype(f32)
            low = g - high - middle
            row = lax.broadcasted_iota(jnp.int32, (16, step), 0)
            split = jnp.where(
                row == 0, high, jnp.where(row == 1, middle, jnp.where(row == 2, low, 0.0))
            ).astype(bf16)
            x = x_buf[:, c * step : (c + 1) * step].astype(f32)
            x = ((x - mean) * g).astype(bf16)
            copies[c].wait()
            p = p_buf[c * step : (c + 1) * step, :]
            product = jnp.dot(x, p, preferred_element_type=f32)
            if c == 0:
                total[...] = product
            else:
                total[...] += product
            offset += jnp.dot(split, p, preferred_element_type=f32)
        offset = jnp.sum(offset, axis=0, keepdims=True)
        height = width_out // lanes
        for j in range(height):
            note[0, j : j + 1, :] = offset[:, j * lanes : (j + 1) * lanes]
        many = rows // lanes
        for j in range(many):
            for kind in range(2):
                at = height + kind * many + j
                note[0, at : at + 1, :] = stats[kind : kind + 1, j * lanes : (j + 1) * lanes]

    side = lax.axis_index("group")

    @pl.when(side == 0)
    def _():
        tower(text_x, text_g, text_p)

    @pl.when(side == 1)
    def _():
        tower(image_x, image_g, image_p)

    for k in range(shards):
        block = total[pl.ds(pl.multiple_of((me ^ k) * span, span), span), :]
        if k == 0:
            own_out[...] = block
        else:
            parts[k - 1][...] = block.astype(bf16)


def finish_kernel(shards, many, widths, own, *rest):
    parts = rest[: shards - 1]
    notes = rest[shards - 1 : -4]
    unit_out, turned = rest[-2:]
    span, width_out = own.shape
    height = width_out // lanes
    me = lax.axis_index("mp")
    width = jnp.where(lax.axis_index("group") == 0, widths[0], widths[1]).astype(f32)
    rows_of = []
    for n in notes:
        rows_of += [(n, i) for i in range(n.shape[0])]
    tail = notes[0].shape[1] - height
    stacked = [n[i, height:, :] for n, i in rows_of]
    stacked.append(jnp.zeros((-(-shards * tail // lanes) * lanes - shards * tail, lanes), f32))
    turned[...] = jnp.transpose(jnp.concatenate(stacked, axis=0))
    first = me * span
    block = turned[pl.ds(pl.multiple_of(lax.rem(first, lanes), span), span), :]
    lane = lax.broadcasted_iota(jnp.int32, block.shape, 1)
    pick = lax.div(first, lanes)

    def column(at):
        return jnp.sum(jnp.where(lane == at + pick, block, 0.0), axis=1, keepdims=True)

    means = [column(k * tail) for k in range(shards)]
    spreads = [column(k * tail + many) for k in range(shards)]
    mean = tree(means, jnp.add) / shards
    spread = tree(spreads, jnp.add) / width
    spread += tree([(m - mean) * (m - mean) for m in means], jnp.add) / shards
    inverse = lax.rsqrt(spread + norm_epsilon)
    pieces = []
    squares = jnp.zeros((span, lanes), f32)
    for j in range(height):
        at = slice(j * lanes, (j + 1) * lanes)
        value = own[:, at]
        for part in parts:
            value += part[:, at].astype(f32)
        for k, (n, i) in enumerate(rows_of):
            value += (means[k] - mean) * n[i, j : j + 1, :]
        value *= inverse
        squares += value * value
        pieces.append(value)
    scale = lax.rsqrt(jnp.sum(squares, axis=1, keepdims=True) + unit_epsilon)
    for j in range(height):
        unit_out[:, j * lanes : (j + 1) * lanes] = (pieces[j] * scale).astype(bf16)


def scores_kernel(halves, shards, multiplier, left, right, *rest):
    owns = rest[:4]
    others = rest[4:-5]
    scores_out, row_out, column_out, gathered, mine = rest[-5:]
    span = owns[0].shape[0]
    fars = shards // 2
    dp, mp = lax.axis_index("dp"), lax.axis_index("mp")
    core, near = lax.rem(dp, 2), lax.rem(mp, 2)
    half, far = lax.div(dp, 2), lax.div(mp, 2)
    for h in range(halves):
        for m in range(fars):
            at = ((half ^ h) * fars + (far ^ m)) * span
            gathered[pl.ds(pl.multiple_of(at, span), span), :] = others[h * fars + m][...]
    for c in range(2):
        for n in range(2):
            at = ((core ^ c) * 2 + (near ^ n)) * span
            mine[pl.ds(pl.multiple_of(at, span), span), :] = owns[c * 2 + n][...]
    scores = multiplier[0] * lax.dot_general(
        mine[...], gathered[...], (((1,), (1,)), ((), ())), preferred_element_type=f32
    )
    scores_out[...] = scores
    row_peak = jnp.max(scores, axis=1, keepdims=True)
    row_part = row_peak + jnp.log(jnp.sum(jnp.exp(scores - row_peak), axis=1, keepdims=True))
    row_out[...] = jnp.transpose(jnp.broadcast_to(row_part, (scores.shape[0], lanes)))[0:1, :]
    column_peak = jnp.max(scores, axis=0, keepdims=True)
    column_out[0:1, :] = column_peak + jnp.log(
        jnp.sum(jnp.exp(scores - column_peak), axis=0, keepdims=True)
    )
    matched = left[...] == right[...]
    column_out[1:2, :] = jnp.sum(jnp.where(matched, scores, 0.0), axis=0, keepdims=True)


def merge_kernel(row, row_other, column, column_other, row_out, column_out):
    row_out[...] = log_add(row[...], row_other[...])
    column_out[...] = merge_columns(column[...], column_other[...])


def grads_kernel(
    multiplier, left, right, scores, gathered, row, row_other, column, column_other, *rest
):
    kept_out, sent_out, loss_out, total = rest
    rows = kept_out.shape[0]
    core = lax.rem(lax.axis_index("dp"), 2)
    row_total = log_add(row[...], row_other[...])
    column_both = merge_columns(column[...], column_other[...])
    column_total = column_both[0:1, :]
    loss = jnp.sum(column_total - column_both[1:2, :], axis=1, keepdims=True)
    loss_out[...] = jnp.broadcast_to(loss, loss_out.shape)
    row_total = jnp.transpose(jnp.broadcast_to(row_total, (lanes, row_total.shape[1])))[:, 0:1]
    matched = left[...] == right[...]
    values = scores[...]
    weights = multiplier[0] * (
        jnp.exp(values - row_total)
        + jnp.exp(values - column_total)
        - jnp.where(matched, 2.0, 0.0)
    )
    total[...] = jnp.dot(weights.astype(bf16), gathered[...], preferred_element_type=f32)
    kept_out[...] = total[pl.ds(pl.multiple_of(core * rows, rows), rows), :]
    sent_out[...] = total[pl.ds(pl.multiple_of((1 - core) * rows, rows), rows), :].astype(bf16)


def halve_kernel(kept, received, loss, loss_other, own_out, sent_out, loss_out):
    rows = own_out.shape[0]
    near = lax.rem(lax.axis_index("mp"), 2)
    mine = pl.ds(pl.multiple_of(near * rows, rows), rows)
    yours = pl.ds(pl.multiple_of((1 - near) * rows, rows), rows)
    own_out[...] = kept[mine, :] + received[mine, :].astype(f32)
    sent_out[...] = (kept[yours, :] + received[yours, :].astype(f32)).astype(bf16)
    loss_out[...] = loss[...] + loss_other[...]


def total_kernel(scale, own, received, *rest):
    losses = rest[:4]
    out, loss_out = rest[4:]
    out[...] = own[...] + received[...].astype(f32)
    loss = tree([l[...] for l in losses], jnp.add)
    loss_out[...] = loss[:, 0:1] * scale


def body(
    image_features, text_features, image_gain, text_gain, image_proj, text_proj, pair, logit_scale
):
    rows = image_features.shape[0]
    shards = lax.axis_size("mp")
    owners = lax.axis_size("dp")
    halves, fars = owners // 2, shards // 2
    span = rows // shards
    width_out = image_proj.shape[1]
    group = lax.axis_index("group")
    me = lax.axis_index("mp")
    owner = lax.axis_index("dp")
    many = rows // lanes
    note_height = -(-(width_out // lanes + 2 * many) // 8) * 8
    shape = jax.ShapeDtypeStruct

    widest = max(image_features.shape[1], text_features.shape[1])
    own, *parts, note = pl.pallas_call(
        functools.partial(project_kernel, shards),
        out_shape=[shape((span, width_out), f32)]
        + [shape((span, width_out), bf16)] * (shards - 1)
        + [shape((1, note_height, lanes), f32)],
        in_specs=[HBM, HBM, VMEM, VMEM, HBM, HBM],
        out_specs=[VMEM] * (shards + 1),
        scratch_shapes=[
            pltpu.VMEM((rows, widest), bf16),
            pltpu.VMEM((widest, width_out), bf16),
            pltpu.VMEM((rows, width_out), f32),
            pltpu.SemaphoreType.DMA((1 + max(1, widest // 512),)),
        ],
        compiler_params=PARAMS_P,
        name="project",
    )(
        image_features,
        text_features,
        image_gain,
        text_gain,
        image_proj,
        text_proj,
    )
    parts = [exchange(parts[k - 1], "mp", k) for k in range(1, shards)]
    notes = [note]
    distance = 1
    while distance < shards:
        held = jnp.concatenate(notes, axis=0) if len(notes) > 1 else notes[0]
        notes.append(exchange(held, "mp", distance))
        distance *= 2

    core, near = owner % 2, me % 2
    half, far = owner // 2, me // 2
    numbers = jnp.arange(owners * rows, dtype=jnp.int32)
    cut = (halves, 2, fars, 2, span)

    def of_rows(v):
        return lax.dynamic_slice(
            v.reshape(cut), (half, 0, far, 0, 0), (1, 2, 1, 2, span)
        ).reshape(4 * span, 1)

    def of_columns(v):
        return lax.dynamic_slice(
            v.reshape(cut), (0, core, 0, near, 0), (halves, 1, fars, 1, span)
        ).reshape(1, halves * fars * span)

    image_rows = group == 0
    left = of_rows(jnp.where(image_rows, pair, numbers))
    right = of_columns(jnp.where(image_rows, numbers, pair))
    row_count, column_count = 4 * span, halves * fars * span
    multiplier = logit_scale.reshape(1)

    unit = pl.pallas_call(
        functools.partial(
            finish_kernel,
            shards,
            many,
            (text_features.shape[1] * shards, image_features.shape[1] * shards),
        ),
        out_shape=shape((span, width_out), bf16),
        in_specs=[VMEM] * (shards + len(notes) + 2),
        out_specs=VMEM,
        scratch_shapes=[
            pltpu.VMEM(
                (
                    lanes,
                    -(-shards * (note_height - width_out // lanes) // lanes) * lanes,
                ),
                f32,
            )
        ],
        compiler_params=PARAMS,
        name="finish",
    )(own, *parts, *notes, left, right)

    others = [unit] + [exchange(unit, "mp", m * 2) for m in range(1, fars)]
    mine = cross_exchange(unit, 0)
    owns = [mine, exchange(mine, "mp", 1)]
    blocks = list(others)
    for h in range(1, halves):
        blocks += [exchange(b, "dp", h * 2) for b in others]
    owns += [exchange(b, "dp", 1) for b in owns]

    scores, row_part, column_part, gathered = pl.pallas_call(
        functools.partial(scores_kernel, halves, shards),
        out_shape=[
            shape((row_count, column_count), f32),
            shape((1, row_count), f32),
            shape((2, column_count), f32),
            shape((column_count, width_out), bf16),
        ],
        in_specs=[SMEM] + [VMEM] * (2 + 4 + halves * fars),
        out_specs=[VMEM] * 4,
        scratch_shapes=[pltpu.VMEM((row_count, width_out), bf16)],
        compiler_params=PARAMS,
        name="scores",
    )(multiplier, left, right, *owns, *blocks)

    row_steps = [("dp", 1), ("mp", 1)]
    column_steps = [("dp", 2 << i) for i in range((halves - 1).bit_length())]
    column_steps += [("mp", 2 << i) for i in range((fars - 1).bit_length())]
    row, column = row_part, column_part
    while len(column_steps) > 2:
        axis, distance = column_steps.pop(0)
        column = merge_columns(column, exchange(column, axis, distance))
    for (row_axis, row_distance), (column_axis, column_distance) in zip(row_steps, column_steps):
        row_other = exchange(row, row_axis, row_distance)
        column_other = exchange(column, column_axis, column_distance)
        if row_axis == "dp":
            row, column = pl.pallas_call(
                merge_kernel,
                out_shape=[shape(row.shape, f32), shape(column.shape, f32)],
                in_specs=[VMEM] * 4,
                out_specs=[VMEM] * 2,
                compiler_params=PARAMS,
        name="merge",
            )(row, row_other, column, column_other)

    kept, sent, loss = pl.pallas_call(
        grads_kernel,
        out_shape=[
            shape((2 * span, width_out), f32),
            shape((2 * span, width_out), bf16),
            shape((1, lanes), f32),
        ],
        in_specs=[SMEM] + [VMEM] * 8,
        out_specs=[VMEM] * 3,
        scratch_shapes=[pltpu.VMEM((row_count, width_out), f32)],
        compiler_params=PARAMS,
        name="grads",
    )(multiplier, left, right, scores, gathered, row, row_other, column, column_other)
    own, sent, loss = pl.pallas_call(
        halve_kernel,
        out_shape=[
            shape((span, width_out), f32),
            shape((span, width_out), bf16),
            shape((1, lanes), f32),
        ],
        in_specs=[VMEM] * 4,
        out_specs=[VMEM] * 3,
        compiler_params=PARAMS,
        name="halve",
    )(kept, exchange(sent, "dp", 1), loss, exchange(loss, "dp", 1))
    grads, loss = pl.pallas_call(
        functools.partial(total_kernel, 1.0 / (2.0 * owners * rows)),
        out_shape=[shape((span, width_out), f32), shape((1, 1), f32)],
        in_specs=[VMEM] * 6,
        out_specs=[VMEM] * 2,
        compiler_params=PARAMS,
        name="total",
    )(
        own,
        exchange(sent, "mp", 1),
        loss,
        exchange(loss, "mp", 1),
        cross_exchange(loss, 0),
        cross_exchange(loss, 1),
    )
    return (grads[None, :, :], loss[0, 0])


def solution(mesh):
    in_specs = (
        P("dp", "mp"),
        P("dp", "mp"),
        P("mp"),
        P("mp"),
        P("mp", None),
        P("mp", None),
        P(),
        P(),
    )
    out_specs = (P("group", ("dp", "mp"), None), P())
    return jax.shard_map(body, mesh=mesh, in_specs=in_specs, out_specs=out_specs, check_vma=False)
```

time: 76 us -> 60 us (0.79)
  starting transfers between devices: 35.4 us -> 30.7 us
  waiting for transfers between devices: 25.5 us -> 21 us
  local copies, waits for them, and re-layouts: 6.57 us -> 2.68 us
  Pallas kernels: 5.3 us -> 4.01 us
  between operations: 2.61 us -> 1.39 us
    ppermute x21 -> x19, waiting for transfers between devices: 22.9 us -> 18.9 us  [exchange(): lax.ppermute(shard, axis, [(i, i ^ distance) for i in range(lax.axis_size...]
    ppermute x4 -> x3, starting transfers between devices: 8.98 us -> 5.31 us  [cross_exchange(): return lax.ppermute(shard, ('group', 'mp'), pairs)]
    unnamed x12 -> x8, local copies, waits for them, and re-layouts: 5.65 us -> 2.28 us
    pallas_call x4 -> x6, Pallas kernels: 3.99 us -> 2.52 us  [the longest x1 0.73 us: body(): pl.pallas_call(functools.partial(total_kernel, 1.0 / (2.0 * owners * rows...]
    ppermute x21 -> x19, starting transfers between devices: 26.4 us -> 25.3 us  [exchange(): lax.ppermute(shard, axis, [(i, i ^ distance) for i in range(lax.axis_size...]
    ppermute x4 -> x3, waiting for transfers between devices: 2.57 us -> 2.12 us  [cross_exchange(): return lax.ppermute(shard, ('group', 'mp'), pairs)]
  transfers between devices with their start and end apart: 25 -> 22, of which waited for: 10 -> 10; matrix products, arithmetic and copies ran while one was open for 1% -> 1% of each run, Pallas kernels for 0% -> 0%
where the time goes in v2:
time: 60 us; the launch traced here: 59.8 us
  starting transfers between devices  30.7 us (51%)
  waiting for transfers between devices  21 us (35%)
  Pallas kernels  4.01 us (7%)
  local copies, waits for them, and re-layouts  2.68 us (4%)
  between operations  1.39 us (2%)
    ppermute x19, starting transfers between devices, exchange(): lax.ppermute(shard, axis, [(i, i ^ distance) for i in range(lax.axis_size...  25.3 us
    ppermute x19, waiting for transfers between devices, exchange(): lax.ppermute(shard, axis, [(i, i ^ distance) for i in range(lax.axis_size...  18.9 us
    ppermute x3, starting transfers between devices, cross_exchange(): return lax.ppermute(shard, ('group', 'mp'), pairs)  5.31 us
    unnamed x8, local copies, waits for them, and re-layouts  2.28 us
    ppermute x3, waiting for transfers between devices, cross_exchange(): return lax.ppermute(shard, ('group', 'mp'), pairs)  2.12 us
    pallas_call x1, Pallas kernels, body(): pl.pallas_call(functools.partial(project_kernel, shards), out_shape=[shap...  1.5 us
  transfers between devices with their start and end apart: 22, of which 10 were waited for; matrix products, arithmetic and copies ran while one was open for 1% of the time, Pallas kernels for 0%

profile of v2, /device:TPU:0, one launch (start us, length us, event | category | flops | bytes accessed | tf_op | source)
XLA Modules:
  0.0 59.8 jit_solution(12958084638273721064)
XLA Ops:
  0.6 0.0 copy-start
  0.6 0.9 %copy-done = bf16[256,256]{1,0:T(8,128)(2,1)S(1)} copy-done((bf16[256,256]{1,0:T(8,128)(2,1)S(1)}, bf16[256,256]{1,0:T(8,128)(2,1)}, u32[]{:S(2)}) %copy-start) | copy-done | bytes 131096
  1.5 0.0 copy-start.1
  1.5 0.7 %copy-done.1 = f32[1536]{0:T(1024)S(1)} copy-done((f32[1536]{0:T(1024)S(1)}, f32[1536]{0:T(1024)}, u32[]{:S(2)}) %copy-start.1) | copy-done | bytes 6168
  2.2 0.0 copy-start.2
  2.2 0.7 %copy-done.2 = f32[256]{0:T(256)S(1)} copy-done((f32[256]{0:T(256)S(1)}, f32[256]{0:T(256)}, u32[]{:S(2)}) %copy-start.2) | copy-done | bytes 1048
  2.9 0.0 copy-start.3
  2.9 1.5 %project.1 = (f32[64,1024]{1,0:T(8,128)S(1)}, bf16[64,1024]{1,0:T(8,128)(2,1)S(1)}, bf16[64,1024]{1,0:T(8,128)(2,1)S(1)}, bf16[64,1024]{1,0:T(8,128)(2,1)S(1)}, f32[1,16,128]{2,1,0:T(8,128)S(1)}) custom-call(bf16[256,1536]{1,0:T(8,128)(2,1)} %image_x.1, bf16[256,256]{1,0:T(8,128)(2,1)S(1)} %copy-done, f32[1536]{0:T(1024)S(1)} %copy-done.1, ...), custom_call_target="tpu_custom_call" | custom-call | tf_op jit(solution)/shard_map/project/pallas_call | solution.py:272
  4.4 3.1 %collective-permute-start.3 = (f32[1,16,128]{2,1,0:T(8,128)S(1)}, f32[1,16,128]{2,1,0:T(8,128)S(1)}, u32[]{:S(2)}, u32[]{:S(2)}) collective-permute-start(f32[1,16,128]{2,1,0:T(8,128)S(1)} %get-tuple-element.25.rest_3_), channel_id=1, source_target_pairs={{0,1},{1,0},{2,3},{3,2},{4,5},{5,4},{6,7},{7,6},{8,9},{9,8},{10,11... | collective-permute-start | bytes 24584 | tf_op jit(solution)/shard_map/ppermute | solution.py:23
  7.5 0.1 collective-permute-start
  7.6 3.0 %collective-permute-start.1 = (bf16[64,1024]{1,0:T(8,128)(2,1)S(1)}, bf16[64,1024]{1,0:T(8,128)(2,1)S(1)}, u32[]{:S(2)}, u32[]{:S(2)}) collective-permute-start(bf16[64,1024]{1,0:T(8,128)(2,1)S(1)} %get-tuple-element.23), channel_id=1, source_target_pairs={{0,2},{1,3},{2,0},{3,1},{4,6},{5,7},{6,4},{7,5},{8,10},{9,11},{10,... | collective-permute-start | bytes 393224 | tf_op jit(solution)/shard_map/ppermute | solution.py:23
  10.6 1.3 %collective-permute-start.2 = (bf16[64,1024]{1,0:T(8,128)(2,1)S(1)}, bf16[64,1024]{1,0:T(8,128)(2,1)S(1)}, u32[]{:S(2)}, u32[]{:S(2)}) collective-permute-start(bf16[64,1024]{1,0:T(8,128)(2,1)S(1)} %get-tuple-element.24), channel_id=1, source_target_pairs={{0,3},{1,2},{2,1},{3,0},{4,7},{5,6},{6,5},{7,4},{8,11},{9,10},{10,... | collective-permute-start | bytes 393224 | tf_op jit(solution)/shard_map/ppermute | solution.py:23
  11.9 0.0 copy-done.3
  11.9 0.1 reshape.20
  12.0 0.0 collective-permute-done.3.rest_4_
  12.0 1.8 %collective-permute-start.4 = (f32[2,16,128]{2,1,0:T(8,128)S(1)}, f32[2,16,128]{2,1,0:T(8,128)S(1)}, u32[]{:S(2)}, u32[]{:S(2)}) collective-permute-start(f32[2,16,128]{2,1,0:T(8,128)S(1)} %pad_maximum_fusion), channel_id=1, source_target_pairs={{0,2},{1,3},{2,0},{3,1},{4,6},{5,7},{6,4},{7,5},{8,10},{9,11},{10,... | collective-permute-start | bytes 49160 | tf_op jit(solution)/shard_map/ppermute | solution.py:23
  13.8 0.1 reshape.22
  13.9 0.1 reshape.23.rest_7_.right
  13.9 0.1 reshape.24.rest_6_.left
  14.1 8.6 %collective-permute-done.4.rest_5_ = f32[2,16,128]{2,1,0:T(8,128)S(1)} collective-permute-done((f32[2,16,128]{2,1,0:T(8,128)S(1)}, f32[2,16,128]{2,1,0:T(8,128)S(1)}, u32[]{:S(2)}, u32[]{:S(2)}) %collective-permute-start.4) | collective-permute-done | bytes 16416 | tf_op jit(solution)/shard_map/ppermute | solution.py:23
  22.7 0.0 collective-permute-done.rest_0_
  22.7 0.0 collective-permute-done.1.rest_1_
  22.7 0.0 collective-permute-done.2.rest_2_
  22.7 0.4 finish.1.rest_4_
  23.1 3.8 %collective-permute-start.5 = (bf16[64,1024]{1,0:T(8,128)(2,1)S(1)}, bf16[64,1024]{1,0:T(8,128)(2,1)S(1)}, u32[]{:S(2)}, u32[]{:S(2)}) collective-permute-start(bf16[64,1024]{1,0:T(8,128)(2,1)S(1)} %finish.1.rest_4_), channel_id=1, source_target_pairs={{0,16},{1,17},{2,18},{3,19},{16,0},{17,1},{18,2},{19,3},{4,20},{5,... | collective-permute-start | bytes 393224 | tf_op jit(solution)/shard_map/ppermute | solution.py:33
  26.9 2.2 %collective-permute-start.9 = (bf16[64,1024]{1,0:T(8,128)(2,1)S(1)}, bf16[64,1024]{1,0:T(8,128)(2,1)S(1)}, u32[]{:S(2)}, u32[]{:S(2)}) collective-permute-start(bf16[64,1024]{1,0:T(8,128)(2,1)S(1)} %finish.1.rest_4_), channel_id=1, source_target_pairs={{0,2},{1,3},{2,0},{3,1},{4,6},{5,7},{6,4},{7,5},{8,10},{9,11},{10,... | collective-permute-start | bytes 393224 | tf_op jit(solution)/shard_map/ppermute | solution.py:23
  29.0 0.8 %collective-permute-done.5.rest_0_ = bf16[64,1024]{1,0:T(8,128)(2,1)S(1)} collective-permute-done((bf16[64,1024]{1,0:T(8,128)(2,1)S(1)}, bf16[64,1024]{1,0:T(8,128)(2,1)S(1)}, u32[]{:S(2)}, u32[]{:S(2)}) %collective-permute-start.5) | collective-permute-done | bytes 131104 | tf_op jit(solution)/shard_map/ppermute | solution.py:33
  29.8 0.9 %collective-permute-start.6 = (bf16[64,1024]{1,0:T(8,128)(2,1)S(1)}, bf16[64,1024]{1,0:T(8,128)(2,1)S(1)}, u32[]{:S(2)}, u32[]{:S(2)}) collective-permute-start(bf16[64,1024]{1,0:T(8,128)(2,1)S(1)} %collective-permute-done.5.rest_0_), channel_id=1, source_target_pairs={{0,1},{1,0},{2,3},{3,2},{4,5},{5,4},{6,7},{7,6},{8,9},{9,8},{10,11... | collective-permute-start | bytes 393224 | tf_op jit(solution)/shard_map/ppermute | solution.py:23
  30.7 1.5 %collective-permute-start.10 = (bf16[64,1024]{1,0:T(8,128)(2,1)S(1)}, bf16[64,1024]{1,0:T(8,128)(2,1)S(1)}, u32[]{:S(2)}, u32[]{:S(2)}) collective-permute-start(bf16[64,1024]{1,0:T(8,128)(2,1)S(1)} %finish.1.rest_4_), channel_id=1, source_target_pairs={{0,8},{4,12},{8,0},{12,4},{1,9},{5,13},{9,1},{13,5},{2,10},{6,14},... | collective-permute-start | bytes 393224 | tf_op jit(solution)/shard_map/ppermute | solution.py:23
  32.2 0.0 collective-permute-start.7
  32.2 2.6 %collective-permute-done.9.rest_5_ = bf16[64,1024]{1,0:T(8,128)(2,1)S(1)} collective-permute-done((bf16[64,1024]{1,0:T(8,128)(2,1)S(1)}, bf16[64,1024]{1,0:T(8,128)(2,1)S(1)}, u32[]{:S(2)}, u32[]{:S(2)}) %collective-permute-start.9) | collective-permute-done | bytes 131104 | tf_op jit(solution)/shard_map/ppermute | solution.py:23
  34.9 1.5 %collective-permute-start.11 = (bf16[64,1024]{1,0:T(8,128)(2,1)S(1)}, bf16[64,1024]{1,0:T(8,128)(2,1)S(1)}, u32[]{:S(2)}, u32[]{:S(2)}) collective-permute-start(bf16[64,1024]{1,0:T(8,128)(2,1)S(1)} %collective-permute-done.9.rest_5_), channel_id=1, source_target_pairs={{0,8},{4,12},{8,0},{12,4},{1,9},{5,13},{9,1},{13,5},{2,10},{6,14},... | collective-permute-start | bytes 393224 | tf_op jit(solution)/shard_map/ppermute | solution.py:23
  36.4 0.0 collective-permute-done.6.rest_1_
  36.4 0.0 collective-permute-start.8
  37.0 0.0 collective-permute-done.10.rest_6_
  37.1 2.8 %collective-permute-done.11.rest_7_ = bf16[64,1024]{1,0:T(8,128)(2,1)S(1)} collective-permute-done((bf16[64,1024]{1,0:T(8,128)(2,1)S(1)}, bf16[64,1024]{1,0:T(8,128)(2,1)S(1)}, u32[]{:S(2)}, u32[]{:S(2)}) %collective-permute-start.11) | collective-permute-done | bytes 131104 | tf_op jit(solution)/shard_map/ppermute | solution.py:23
  39.8 0.0 collective-permute-done.7.rest_2_
  39.8 0.0 collective-permute-done.8.rest_3_
  39.8 0.6 %scores.1 = (f32[256,256]{1,0:T(8,128)S(1)}, f32[1,256]{1,0:T(1,128)S(1)}, f32[2,256]{1,0:T(2,128)S(1)}, bf16[256,1024]{1,0:T(8,128)(2,1)S(1)}) custom-call(f32[1]{0:T(128)} %bitcast.3.multiplier, s32[256,1]{1,0:T(8,128)S(1)} %reshape.24.rest_6_.left, s32[1,256]{1,0:T(1,128)S(1)} %reshape.23.rest_7_.right, ...), custom_call_target="tpu_custom_call" | custom-call | tf_op jit(solution)/shard_map/scores/pallas_call | solution.py:355
  40.5 1.6 %collective-permute-start.13 = (f32[2,256]{1,0:T(2,128)S(1)}, f32[2,256]{1,0:T(2,128)S(1)}, u32[]{:S(2)}, u32[]{:S(2)}) collective-permute-start(f32[2,256]{1,0:T(2,128)S(1)} %get-tuple-element.29.column), channel_id=1, source_target_pairs={{0,8},{4,12},{8,0},{12,4},{1,9},{5,13},{9,1},{13,5},{2,10},{6,14},... | collective-permute-start | bytes 6152 | tf_op jit(solution)/shard_map/ppermute | solution.py:23
  42.1 0.0 collective-permute-start.12
  42.1 1.1 %collective-permute-done.12.row_other = f32[1,256]{1,0:T(1,128)S(1)} collective-permute-done((f32[1,256]{1,0:T(1,128)S(1)}, f32[1,256]{1,0:T(1,128)S(1)}, u32[]{:S(2)}, u32[]{:S(2)}) %collective-permute-start.12) | collective-permute-done | bytes 1056 | tf_op jit(solution)/shard_map/ppermute | solution.py:23
  43.2 0.9 %collective-permute-done.13.column_other = f32[2,256]{1,0:T(2,128)S(1)} collective-permute-done((f32[2,256]{1,0:T(2,128)S(1)}, f32[2,256]{1,0:T(2,128)S(1)}, u32[]{:S(2)}, u32[]{:S(2)}) %collective-permute-start.13) | collective-permute-done | bytes 2080 | tf_op jit(solution)/shard_map/ppermute | solution.py:23
  44.2 1.7 %collective-permute-start.15 = (f32[2,256]{1,0:T(2,128)S(1)}, f32[2,256]{1,0:T(2,128)S(1)}, u32[]{:S(2)}, u32[]{:S(2)}) collective-permute-start(f32[2,256]{1,0:T(2,128)S(1)} %get-tuple-element.31.column), channel_id=1, source_target_pairs={{0,2},{1,3},{2,0},{3,1},{4,6},{5,7},{6,4},{7,5},{8,10},{9,11},{10,... | collective-permute-start | bytes 6152 | tf_op jit(solution)/shard_map/ppermute | solution.py:23
  45.8 2.2 %collective-permute-start.14 = (f32[1,256]{1,0:T(1,128)S(1)}, f32[1,256]{1,0:T(1,128)S(1)}, u32[]{:S(2)}, u32[]{:S(2)}) collective-permute-start(f32[1,256]{1,0:T(1,128)S(1)} %get-tuple-element.30.row), channel_id=1, source_target_pairs={{0,1},{1,0},{2,3},{3,2},{4,5},{5,4},{6,7},{7,6},{8,9},{9,8},{10,11... | collective-permute-start | bytes 3080 | tf_op jit(solution)/shard_map/ppermute | solution.py:23
  48.0 1.5 %collective-permute-done.14.row_other = f32[1,256]{1,0:T(1,128)S(1)} collective-permute-done((f32[1,256]{1,0:T(1,128)S(1)}, f32[1,256]{1,0:T(1,128)S(1)}, u32[]{:S(2)}, u32[]{:S(2)}) %collective-permute-start.14) | collective-permute-done | bytes 1056 | tf_op jit(solution)/shard_map/ppermute | solution.py:23
  49.6 0.0 collective-permute-done.15.column_other
  49.6 0.6 %grads.1 = (f32[128,1024]{1,0:T(8,128)S(1)}, bf16[128,1024]{1,0:T(8,128)(2,1)S(1)}, f32[1,128]{1,0:T(1,128)S(1)}) custom-call(f32[1]{0:T(128)} %bitcast.4.multiplier, s32[256,1]{1,0:T(8,128)S(1)} %reshape.24.rest_6_.left, s32[1,256]{1,0:T(1,128)S(1)} %reshape.23.rest_7_.right, f32[256,256]{1,0:T(8,128)S(1)} %get-tuple-element.26.scores, ...), custom_call_target="tpu_custom_call" | custom-call | tf_op jit(solution)/shard_map/grads/pallas_call | solution.py:390
  50.2 0.1 collective-permute-start.16
  50.3 0.5 collective-permute-start.17
  50.8 1.0 %collective-permute-done.17.loss_other = f32[1,128]{1,0:T(1,128)S(1)} collective-permute-done((f32[1,128]{1,0:T(1,128)S(1)}, f32[1,128]{1,0:T(1,128)S(1)}, u32[]{:S(2)}, u32[]{:S(2)}) %collective-permute-start.17) | collective-permute-done | bytes 544 | tf_op jit(solution)/shard_map/ppermute | solution.py:23
  51.8 0.0 collective-permute-done.16.received
  51.8 0.1 halve.1
  51.9 2.1 %collective-permute-start.18 = (bf16[64,1024]{1,0:T(8,128)(2,1)S(1)}, bf16[64,1024]{1,0:T(8,128)(2,1)S(1)}, u32[]{:S(2)}, u32[]{:S(2)}) collective-permute-start(bf16[64,1024]{1,0:T(8,128)(2,1)S(1)} %get-tuple-element.36), channel_id=1, source_target_pairs={{0,1},{1,0},{2,3},{3,2},{4,5},{5,4},{6,7},{7,6},{8,9},{9,8},{10,11... | collective-permute-start | bytes 393224 | tf_op jit(solution)/shard_map/ppermute | solution.py:23
  54.0 1.3 %collective-permute-start.21 = (f32[1,128]{1,0:T(1,128)S(1)}, f32[1,128]{1,0:T(1,128)S(1)}, u32[]{:S(2)}, u32[]{:S(2)}) collective-permute-start(f32[1,128]{1,0:T(1,128)S(1)} %get-tuple-element.37.rest_0_), channel_id=1, source_target_pairs={{0,17},{1,16},{2,19},{3,18},{16,1},{17,0},{18,3},{19,2},{4,21},{5,... | collective-permute-start | bytes 1544 | tf_op jit(solution)/shard_map/ppermute | solution.py:33
  55.3 0.3 collective-permute-start.20
  55.5 1.9 %collective-permute-start.19 = (f32[1,128]{1,0:T(1,128)S(1)}, f32[1,128]{1,0:T(1,128)S(1)}, u32[]{:S(2)}, u32[]{:S(2)}) collective-permute-start(f32[1,128]{1,0:T(1,128)S(1)} %get-tuple-element.37.rest_0_), channel_id=1, source_target_pairs={{0,1},{1,0},{2,3},{3,2},{4,5},{5,4},{6,7},{7,6},{8,9},{9,8},{10,11... | collective-permute-start | bytes 1544 | tf_op jit(solution)/shard_map/ppermute | solution.py:23
  57.5 1.3 %collective-permute-done.21.rest_3_ = f32[1,128]{1,0:T(1,128)S(1)} collective-permute-done((f32[1,128]{1,0:T(1,128)S(1)}, f32[1,128]{1,0:T(1,128)S(1)}, u32[]{:S(2)}, u32[]{:S(2)}) %collective-permute-start.21) | collective-permute-done | bytes 544 | tf_op jit(solution)/shard_map/ppermute | solution.py:33
  58.8 0.0 collective-permute-done.20.rest_2_
  58.8 0.3 collective-permute-done.19.rest_1_
  59.1 0.0 collective-permute-done.18.received
  59.1 0.7 %total.1 = (f32[64,1024]{1,0:T(8,128)}, f32[1,1]{1,0:T(1,128)}) custom-call(f32[64,1024]{1,0:T(8,128)S(1)} %get-tuple-element.35.own, bf16[64,1024]{1,0:T(8,128)(2,1)S(1)} %collective-permute-done.18.received, f32[1,128]{1,0:T(1,128)S(1)} %get-tuple-element.37.rest_0_, f32[1,128]{1,0:T(1,128)S(1)} %collective-permute-done.19.rest_1_, ...), custom_call_target="tpu_custom_call" | custom-call | tf_op jit(solution)/shard_map/total/pallas_call | solution.py:415
  (5 shorter events, 0.1 us)
Async XLA Ops:
  0.6 0.9 %copy-start = (bf16[256,256]{1,0:T(8,128)(2,1)S(1)}, bf16[256,256]{1,0:T(8,128)(2,1)}, u32[]{:S(2)}) copy-start(bf16[256,256]{1,0:T(8,128)(2,1)} %text_x.1) | copy-start | bytes 393220
  1.5 0.7 %copy-start.1 = (f32[1536]{0:T(1024)S(1)}, f32[1536]{0:T(1024)}, u32[]{:S(2)}) copy-start(f32[1536]{0:T(1024)} %image_g.1) | copy-start | bytes 18436
  2.2 0.7 %copy-start.2 = (f32[256]{0:T(256)S(1)}, f32[256]{0:T(256)}, u32[]{:S(2)}) copy-start(f32[256]{0:T(256)} %text_g.1) | copy-start | bytes 3076
  2.9 9.0 %copy-start.3 = (s32[1024]{0:T(1024)S(1)}, s32[1024]{0:T(1024)}, u32[]{:S(2)}) copy-start(s32[1024]{0:T(1024)} %param.14) | copy-start | bytes 12292
  4.4 7.6 %collective-permute-start.3 = (f32[1,16,128]{2,1,0:T(8,128)S(1)}, f32[1,16,128]{2,1,0:T(8,128)S(1)}, u32[]{:S(2)}, u32[]{:S(2)}) collective-permute-start(f32[1,16,128]{2,1,0:T(8,128)S(1)} %get-tuple-element.25.rest_3_), channel_id=1, source_target_pairs={{0,1},{1,0},{2,3},{3,2},{4,5},{5,4},{6,7},{7,6},{8,9},{9,8},{10,11... | collective-permute-start | bytes 24584 | tf_op jit(solution)/shard_map/ppermute | solution.py:23
  7.5 15.2 %collective-permute-start = (bf16[64,1024]{1,0:T(8,128)(2,1)S(1)}, bf16[64,1024]{1,0:T(8,128)(2,1)S(1)}, u32[]{:S(2)}, u32[]{:S(2)}) collective-permute-start(bf16[64,1024]{1,0:T(8,128)(2,1)S(1)} %get-tuple-element.22), channel_id=1, source_target_pairs={{0,1},{1,0},{2,3},{3,2},{4,5},{5,4},{6,7},{7,6},{8,9},{9,8},{10,11... | collective-permute-start | bytes 393224 | tf_op jit(solution)/shard_map/ppermute | solution.py:23
  7.6 15.1 %collective-permute-start.1 = (bf16[64,1024]{1,0:T(8,128)(2,1)S(1)}, bf16[64,1024]{1,0:T(8,128)(2,1)S(1)}, u32[]{:S(2)}, u32[]{:S(2)}) collective-permute-start(bf16[64,1024]{1,0:T(8,128)(2,1)S(1)} %get-tuple-element.23), channel_id=1, source_target_pairs={{0,2},{1,3},{2,0},{3,1},{4,6},{5,7},{6,4},{7,5},{8,10},{9,11},{10,... | collective-permute-start | bytes 393224 | tf_op jit(solution)/shard_map/ppermute | solution.py:23
  10.6 12.1 %collective-permute-start.2 = (bf16[64,1024]{1,0:T(8,128)(2,1)S(1)}, bf16[64,1024]{1,0:T(8,128)(2,1)S(1)}, u32[]{:S(2)}, u32[]{:S(2)}) collective-permute-start(bf16[64,1024]{1,0:T(8,128)(2,1)S(1)} %get-tuple-element.24), channel_id=1, source_target_pairs={{0,3},{1,2},{2,1},{3,0},{4,7},{5,6},{6,5},{7,4},{8,11},{9,10},{10,... | collective-permute-start | bytes 393224 | tf_op jit(solution)/shard_map/ppermute | solution.py:23
  12.0 10.7 %collective-permute-start.4 = (f32[2,16,128]{2,1,0:T(8,128)S(1)}, f32[2,16,128]{2,1,0:T(8,128)S(1)}, u32[]{:S(2)}, u32[]{:S(2)}) collective-permute-start(f32[2,16,128]{2,1,0:T(8,128)S(1)} %pad_maximum_fusion), channel_id=1, source_target_pairs={{0,2},{1,3},{2,0},{3,1},{4,6},{5,7},{6,4},{7,5},{8,10},{9,11},{10,... | collective-permute-start | bytes 49160 | tf_op jit(solution)/shard_map/ppermute | solution.py:23
  23.1 6.7 %collective-permute-start.5 = (bf16[64,1024]{1,0:T(8,128)(2,1)S(1)}, bf16[64,1024]{1,0:T(8,128)(2,1)S(1)}, u32[]{:S(2)}, u32[]{:S(2)}) collective-permute-start(bf16[64,1024]{1,0:T(8,128)(2,1)S(1)} %finish.1.rest_4_), channel_id=1, source_target_pairs={{0,16},{1,17},{2,18},{3,19},{16,0},{17,1},{18,2},{19,3},{4,20},{5,... | collective-permute-start | bytes 393224 | tf_op jit(solution)/shard_map/ppermute | solution.py:33
  26.9 8.0 %collective-permute-start.9 = (bf16[64,1024]{1,0:T(8,128)(2,1)S(1)}, bf16[64,1024]{1,0:T(8,128)(2,1)S(1)}, u32[]{:S(2)}, u32[]{:S(2)}) collective-permute-start(bf16[64,1024]{1,0:T(8,128)(2,1)S(1)} %finish.1.rest_4_), channel_id=1, source_target_pairs={{0,2},{1,3},{2,0},{3,1},{4,6},{5,7},{6,4},{7,5},{8,10},{9,11},{10,... | collective-permute-start | bytes 393224 | tf_op jit(solution)/shard_map/ppermute | solution.py:23
  29.8 6.6 %collective-permute-start.6 = (bf16[64,1024]{1,0:T(8,128)(2,1)S(1)}, bf16[64,1024]{1,0:T(8,128)(2,1)S(1)}, u32[]{:S(2)}, u32[]{:S(2)}) collective-permute-start(bf16[64,1024]{1,0:T(8,128)(2,1)S(1)} %collective-permute-done.5.rest_0_), channel_id=1, source_target_pairs={{0,1},{1,0},{2,3},{3,2},{4,5},{5,4},{6,7},{7,6},{8,9},{9,8},{10,11... | collective-permute-start | bytes 393224 | tf_op jit(solution)/shard_map/ppermute | solution.py:23
  30.7 6.3 %collective-permute-start.10 = (bf16[64,1024]{1,0:T(8,128)(2,1)S(1)}, bf16[64,1024]{1,0:T(8,128)(2,1)S(1)}, u32[]{:S(2)}, u32[]{:S(2)}) collective-permute-start(bf16[64,1024]{1,0:T(8,128)(2,1)S(1)} %finish.1.rest_4_), channel_id=1, source_target_pairs={{0,8},{4,12},{8,0},{12,4},{1,9},{5,13},{9,1},{13,5},{2,10},{6,14},... | collective-permute-start | bytes 393224 | tf_op jit(solution)/shard_map/ppermute | solution.py:23
  32.2 7.6 %collective-permute-start.7 = (bf16[64,1024]{1,0:T(8,128)(2,1)S(1)}, bf16[64,1024]{1,0:T(8,128)(2,1)S(1)}, u32[]{:S(2)}, u32[]{:S(2)}) collective-permute-start(bf16[64,1024]{1,0:T(8,128)(2,1)S(1)} %collective-permute-done.5.rest_0_), channel_id=1, source_target_pairs={{0,4},{4,0},{8,12},{12,8},{1,5},{5,1},{9,13},{13,9},{2,6},{6,2},{1... | collective-permute-start | bytes 393224 | tf_op jit(solution)/shard_map/ppermute | solution.py:23
  34.9 5.0 %collective-permute-start.11 = (bf16[64,1024]{1,0:T(8,128)(2,1)S(1)}, bf16[64,1024]{1,0:T(8,128)(2,1)S(1)}, u32[]{:S(2)}, u32[]{:S(2)}) collective-permute-start(bf16[64,1024]{1,0:T(8,128)(2,1)S(1)} %collective-permute-done.9.rest_5_), channel_id=1, source_target_pairs={{0,8},{4,12},{8,0},{12,4},{1,9},{5,13},{9,1},{13,5},{2,10},{6,14},... | collective-permute-start | bytes 393224 | tf_op jit(solution)/shard_map/ppermute | solution.py:23
  36.4 3.5 %collective-permute-start.8 = (bf16[64,1024]{1,0:T(8,128)(2,1)S(1)}, bf16[64,1024]{1,0:T(8,128)(2,1)S(1)}, u32[]{:S(2)}, u32[]{:S(2)}) collective-permute-start(bf16[64,1024]{1,0:T(8,128)(2,1)S(1)} %collective-permute-done.6.rest_1_), channel_id=1, source_target_pairs={{0,4},{4,0},{8,12},{12,8},{1,5},{5,1},{9,13},{13,9},{2,6},{6,2},{1... | collective-permute-start | bytes 393224 | tf_op jit(solution)/shard_map/ppermute | solution.py:23
  40.5 3.7 %collective-permute-start.13 = (f32[2,256]{1,0:T(2,128)S(1)}, f32[2,256]{1,0:T(2,128)S(1)}, u32[]{:S(2)}, u32[]{:S(2)}) collective-permute-start(f32[2,256]{1,0:T(2,128)S(1)} %get-tuple-element.29.column), channel_id=1, source_target_pairs={{0,8},{4,12},{8,0},{12,4},{1,9},{5,13},{9,1},{13,5},{2,10},{6,14},... | collective-permute-start | bytes 6152 | tf_op jit(solution)/shard_map/ppermute | solution.py:23
  42.1 1.1 %collective-permute-start.12 = (f32[1,256]{1,0:T(1,128)S(1)}, f32[1,256]{1,0:T(1,128)S(1)}, u32[]{:S(2)}, u32[]{:S(2)}) collective-permute-start(f32[1,256]{1,0:T(1,128)S(1)} %get-tuple-element.28.row), channel_id=1, source_target_pairs={{0,4},{4,0},{8,12},{12,8},{1,5},{5,1},{9,13},{13,9},{2,6},{6,2},{1... | collective-permute-start | bytes 3080 | tf_op jit(solution)/shard_map/ppermute | solution.py:23
  44.2 5.4 %collective-permute-start.15 = (f32[2,256]{1,0:T(2,128)S(1)}, f32[2,256]{1,0:T(2,128)S(1)}, u32[]{:S(2)}, u32[]{:S(2)}) collective-permute-start(f32[2,256]{1,0:T(2,128)S(1)} %get-tuple-element.31.column), channel_id=1, source_target_pairs={{0,2},{1,3},{2,0},{3,1},{4,6},{5,7},{6,4},{7,5},{8,10},{9,11},{10,... | collective-permute-start | bytes 6152 | tf_op jit(solution)/shard_map/ppermute | solution.py:23
  45.8 3.8 %collective-permute-start.14 = (f32[1,256]{1,0:T(1,128)S(1)}, f32[1,256]{1,0:T(1,128)S(1)}, u32[]{:S(2)}, u32[]{:S(2)}) collective-permute-start(f32[1,256]{1,0:T(1,128)S(1)} %get-tuple-element.30.row), channel_id=1, source_target_pairs={{0,1},{1,0},{2,3},{3,2},{4,5},{5,4},{6,7},{7,6},{8,9},{9,8},{10,11... | collective-permute-start | bytes 3080 | tf_op jit(solution)/shard_map/ppermute | solution.py:23
  50.2 1.6 %collective-permute-start.16 = (bf16[128,1024]{1,0:T(8,128)(2,1)S(1)}, bf16[128,1024]{1,0:T(8,128)(2,1)S(1)}, u32[]{:S(2)}, u32[]{:S(2)}) collective-permute-start(bf16[128,1024]{1,0:T(8,128)(2,1)S(1)} %get-tuple-element.33), channel_id=1, source_target_pairs={{0,4},{4,0},{8,12},{12,8},{1,5},{5,1},{9,13},{13,9},{2,6},{6,2},{1... | collective-permute-start | bytes 786440 | tf_op jit(solution)/shard_map/ppermute | solution.py:23
  50.3 1.5 %collective-permute-start.17 = (f32[1,128]{1,0:T(1,128)S(1)}, f32[1,128]{1,0:T(1,128)S(1)}, u32[]{:S(2)}, u32[]{:S(2)}) collective-permute-start(f32[1,128]{1,0:T(1,128)S(1)} %get-tuple-element.34.loss), channel_id=1, source_target_pairs={{0,4},{4,0},{8,12},{12,8},{1,5},{5,1},{9,13},{13,9},{2,6},{6,2},{1... | collective-permute-start | bytes 1544 | tf_op jit(solution)/shard_map/ppermute | solution.py:23
  51.9 7.2 %collective-permute-start.18 = (bf16[64,1024]{1,0:T(8,128)(2,1)S(1)}, bf16[64,1024]{1,0:T(8,128)(2,1)S(1)}, u32[]{:S(2)}, u32[]{:S(2)}) collective-permute-start(bf16[64,1024]{1,0:T(8,128)(2,1)S(1)} %get-tuple-element.36), channel_id=1, source_target_pairs={{0,1},{1,0},{2,3},{3,2},{4,5},{5,4},{6,7},{7,6},{8,9},{9,8},{10,11... | collective-permute-start | bytes 393224 | tf_op jit(solution)/shard_map/ppermute | solution.py:23
  54.0 4.8 %collective-permute-start.21 = (f32[1,128]{1,0:T(1,128)S(1)}, f32[1,128]{1,0:T(1,128)S(1)}, u32[]{:S(2)}, u32[]{:S(2)}) collective-permute-start(f32[1,128]{1,0:T(1,128)S(1)} %get-tuple-element.37.rest_0_), channel_id=1, source_target_pairs={{0,17},{1,16},{2,19},{3,18},{16,1},{17,0},{18,3},{19,2},{4,21},{5,... | collective-permute-start | bytes 1544 | tf_op jit(solution)/shard_map/ppermute | solution.py:33
  55.3 3.5 %collective-permute-start.20 = (f32[1,128]{1,0:T(1,128)S(1)}, f32[1,128]{1,0:T(1,128)S(1)}, u32[]{:S(2)}, u32[]{:S(2)}) collective-permute-start(f32[1,128]{1,0:T(1,128)S(1)} %get-tuple-element.37.rest_0_), channel_id=1, source_target_pairs={{0,16},{1,17},{2,18},{3,19},{16,0},{17,1},{18,2},{19,3},{4,20},{5,... | collective-permute-start | bytes 1544 | tf_op jit(solution)/shard_map/ppermute | solution.py:33
  55.5 3.5 %collective-permute-start.19 = (f32[1,128]{1,0:T(1,128)S(1)}, f32[1,128]{1,0:T(1,128)S(1)}, u32[]{:S(2)}, u32[]{:S(2)}) collective-permute-start(f32[1,128]{1,0:T(1,128)S(1)} %get-tuple-element.37.rest_0_), channel_id=1, source_target_pairs={{0,1},{1,0},{2,3},{3,2},{4,5},{5,4},{6,7},{7,6},{8,9},{9,8},{10,11... | collective-permute-start | bytes 1544 | tf_op jit(solution)/shard_map/ppermute | solution.py:23

commit v3 on v2

--- a/solution.py
+++ b/solution.py
@@ -51,10 +51,7 @@
 
 
 def project_kernel(shards, image_x, text_x, image_g, text_g, image_p, text_p, *rest):
-    own_out = rest[0]
-    parts = rest[1:shards]
-    note = rest[shards]
-    x_buf, p_buf, total, sems = rest[shards + 1 :]
+    own_out, kept_out, near_out, far_out, note, x_buf, p_buf, total, sems = rest
     rows = x_buf.shape[0]
     span = rows // shards
     width_out = total.shape[1]
@@ -119,17 +116,32 @@
     def _():
         tower(image_x, image_g, image_p)
 
-    for k in range(shards):
-        block = total[pl.ds(pl.multiple_of((me ^ k) * span, span), span), :]
-        if k == 0:
-            own_out[...] = block
-        else:
-            parts[k - 1][...] = block.astype(bf16)
+    def block(distance):
+        return total[pl.ds(pl.multiple_of((me ^ distance) * span, span), span), :]
+
+    for m in range(1, shards // 2):
+        at = slice((m - 1) * span, m * span)
+        far_out[at, :] = block(2 * m + 1).astype(bf16)
+        kept_out[at, :] = block(2 * m)
+    near_out[...] = block(1).astype(bf16)
+    own_out[...] = block(0)
+
+
+def pair_kernel(kept, received, near, note, note_other, *rest):
+    *outs, near_out, notes = rest
+    near_out[...] = near[...]
+    span = outs[0].shape[0]
+    for m, out in enumerate(outs):
+        at = slice(m * span, (m + 1) * span)
+        out[...] = (kept[at, :] + received[at, :].astype(f32)).astype(bf16)
+    notes[0] = note[0]
+    notes[1] = note_other[0]
 
 
 def finish_kernel(shards, many, widths, own, *rest):
-    parts = rest[: shards - 1]
-    notes = rest[shards - 1 : -4]
+    fars = shards // 2
+    parts = rest[:fars]
+    notes = rest[fars:-4]
     unit_out, turned = rest[-2:]
     span, width_out = own.shape
     height = width_out // lanes
@@ -235,13 +247,13 @@
 
 
 def halve_kernel(kept, received, loss, loss_other, own_out, sent_out, loss_out):
+    loss_out[...] = loss[...] + loss_other[...]
     rows = own_out.shape[0]
     near = lax.rem(lax.axis_index("mp"), 2)
     mine = pl.ds(pl.multiple_of(near * rows, rows), rows)
     yours = pl.ds(pl.multiple_of((1 - near) * rows, rows), rows)
     own_out[...] = kept[mine, :] + received[mine, :].astype(f32)
     sent_out[...] = (kept[yours, :] + received[yours, :].astype(f32)).astype(bf16)
-    loss_out[...] = loss[...] + loss_other[...]
 
 
 def total_kernel(scale, own, received, *rest):
@@ -269,13 +281,17 @@
     shape = jax.ShapeDtypeStruct
 
     widest = max(image_features.shape[1], text_features.shape[1])
-    own, *parts, note = pl.pallas_call(
+    own, kept, near_part, far_part, note = pl.pallas_call(
         functools.partial(project_kernel, shards),
-        out_shape=[shape((span, width_out), f32)]
-        + [shape((span, width_out), bf16)] * (shards - 1)
-        + [shape((1, note_height, lanes), f32)],
+        out_shape=[
+            shape((span, width_out), f32),
+            shape(((fars - 1) * span, width_out), f32),
+            shape((span, width_out), bf16),
+            shape(((fars - 1) * span, width_out), bf16),
+            shape((1, note_height, lanes), f32),
+        ],
         in_specs=[HBM, HBM, VMEM, VMEM, HBM, HBM],
-        out_specs=[VMEM] * (shards + 1),
+        out_specs=[VMEM] * 5,
         scratch_shapes=[
             pltpu.VMEM((rows, widest), bf16),
             pltpu.VMEM((widest, width_out), bf16),
@@ -292,13 +308,23 @@
         image_proj,
         text_proj,
     )
-    parts = [exchange(parts[k - 1], "mp", k) for k in range(1, shards)]
-    notes = [note]
-    distance = 1
-    while distance < shards:
-        held = jnp.concatenate(notes, axis=0) if len(notes) > 1 else notes[0]
-        notes.append(exchange(held, "mp", distance))
-        distance *= 2
+    far_other = exchange(far_part, "mp", 1)
+    note_other = exchange(note, "mp", 1)
+    *pairs, near_part, both = pl.pallas_call(
+        pair_kernel,
+        out_shape=[shape((span, width_out), bf16)] * fars
+        + [shape((2, note_height, lanes), f32)],
+        in_specs=[VMEM] * 5,
+        out_specs=[VMEM] * (fars + 1),
+        compiler_params=PARAMS,
+        name="pair",
+    )(kept, far_other, near_part, note, note_other)
+    parts = []
+    notes = [both]
+    for m in range(1, fars):
+        parts.append(exchange(pairs[m - 1], "mp", 2 * m))
+        notes.append(exchange(both, "mp", 2 * m))
+    parts.append(exchange(near_part, "mp", 1))
 
     core, near = owner % 2, me % 2
     half, far = owner // 2, me // 2
@@ -329,7 +355,7 @@
             (text_features.shape[1] * shards, image_features.shape[1] * shards),
         ),
         out_shape=shape((span, width_out), bf16),
-        in_specs=[VMEM] * (shards + len(notes) + 2),
+        in_specs=[VMEM] * (1 + len(parts) + len(notes) + 2),
         out_specs=VMEM,
         scratch_shapes=[
             pltpu.VMEM(
@@ -345,8 +371,7 @@
     )(own, *parts, *notes, left, right)
 
     others = [unit] + [exchange(unit, "mp", m * 2) for m in range(1, fars)]
-    mine = cross_exchange(unit, 0)
-    owns = [mine, exchange(mine, "mp", 1)]
+    owns = [cross_exchange(unit, 0), cross_exchange(unit, 1)]
     blocks = list(others)
     for h in range(1, halves):
         blocks += [exchange(b, "dp", h * 2) for b in others]

time: 60 us -> 55 us (0.917)
  starting transfers between devices: 30.7 us -> 27.3 us
  waiting for transfers between devices: 21 us -> 19.4 us
    ppermute x19 -> x18, starting transfers between devices: 25.3 us -> 19.4 us  [exchange(): lax.ppermute(shard, axis, [(i, i ^ distance) for i in range(lax.axis_size...]
    ppermute x19 -> x18, waiting for transfers between devices: 18.9 us -> 14.4 us  [exchange(): lax.ppermute(shard, axis, [(i, i ^ distance) for i in range(lax.axis_size...]
    ppermute x3 -> x4, waiting for transfers between devices: 2.12 us -> 5 us  [cross_exchange(): return lax.ppermute(shard, ('group', 'mp'), pairs)]
    ppermute x3 -> x4, starting transfers between devices: 5.31 us -> 7.87 us  [cross_exchange(): return lax.ppermute(shard, ('group', 'mp'), pairs)]
  transfers between devices with their start and end apart: 22 -> 22, of which waited for: 10 -> 12; matrix products, arithmetic and copies ran while one was open for 1% -> 1% of each run, Pallas kernels for 0% -> 0%
where the time goes in v3:
time: 55 us; the launch traced here: 54.8 us
  starting transfers between devices  27.3 us (50%)
  waiting for transfers between devices  19.4 us (35%)
  Pallas kernels  4.04 us (7%)
  local copies, waits for them, and re-layouts  2.68 us (5%)
  between operations  1.4 us (3%)
    ppermute x18, starting transfers between devices, exchange(): lax.ppermute(shard, axis, [(i, i ^ distance) for i in range(lax.axis_size...  19.4 us
    ppermute x18, waiting for transfers between devices, exchange(): lax.ppermute(shard, axis, [(i, i ^ distance) for i in range(lax.axis_size...  14.4 us
    ppermute x4, starting transfers between devices, cross_exchange(): return lax.ppermute(shard, ('group', 'mp'), pairs)  7.87 us
    ppermute x4, waiting for transfers between devices, cross_exchange(): return lax.ppermute(shard, ('group', 'mp'), pairs)  5 us
    unnamed x8, local copies, waits for them, and re-layouts  2.28 us
    pallas_call x1, Pallas kernels, body(): pl.pallas_call(functools.partial(project_kernel, shards), out_shape=[shap...  1.5 us
  transfers between devices with their start and end apart: 22, of which 12 were waited for; matrix products, arithmetic and copies ran while one was open for 1% of the time, Pallas kernels for 0%

profile of v3, /device:TPU:0, one launch (start us, length us, event | category | flops | bytes accessed | tf_op | source)
XLA Modules:
  0.0 54.8 jit_solution(6989501830342440133)
XLA Ops:
  0.6 0.0 copy-start
  0.6 0.9 %copy-done = bf16[256,256]{1,0:T(8,128)(2,1)S(1)} copy-done((bf16[256,256]{1,0:T(8,128)(2,1)S(1)}, bf16[256,256]{1,0:T(8,128)(2,1)}, u32[]{:S(2)}) %copy-start) | copy-done | bytes 131096
  1.5 0.0 copy-start.1
  1.5 0.7 %copy-done.1 = f32[1536]{0:T(1024)S(1)} copy-done((f32[1536]{0:T(1024)S(1)}, f32[1536]{0:T(1024)}, u32[]{:S(2)}) %copy-start.1) | copy-done | bytes 6168
  2.2 0.0 copy-start.2
  2.2 0.7 %copy-done.2 = f32[256]{0:T(256)S(1)} copy-done((f32[256]{0:T(256)S(1)}, f32[256]{0:T(256)}, u32[]{:S(2)}) %copy-start.2) | copy-done | bytes 1048
  2.9 0.0 copy-start.3
  2.9 1.5 %project.1 = (f32[64,1024]{1,0:T(8,128)S(1)}, f32[64,1024]{1,0:T(8,128)S(1)}, bf16[64,1024]{1,0:T(8,128)(2,1)S(1)}, bf16[64,1024]{1,0:T(8,128)(2,1)S(1)}, f32[1,16,128]{2,1,0:T(8,128)S(1)}) custom-call(bf16[256,1536]{1,0:T(8,128)(2,1)} %image_x.1, bf16[256,256]{1,0:T(8,128)(2,1)S(1)} %copy-done, f32[1536]{0:T(1024)S(1)} %copy-done.1, f32[256]{0:T(256)S(1)} %copy-done.2, ...), custom_call_target="tpu_custom_call" | custom-call | tf_op jit(solution)/shard_map/project/pallas_call | solution.py:284
  4.4 3.1 %collective-permute-start = (bf16[64,1024]{1,0:T(8,128)(2,1)S(1)}, bf16[64,1024]{1,0:T(8,128)(2,1)S(1)}, u32[]{:S(2)}, u32[]{:S(2)}) collective-permute-start(bf16[64,1024]{1,0:T(8,128)(2,1)S(1)} %get-tuple-element.26), channel_id=1, source_target_pairs={{0,1},{1,0},{2,3},{3,2},{4,5},{5,4},{6,7},{7,6},{8,9},{9,8},{10,11... | collective-permute-start | bytes 393224 | tf_op jit(solution)/shard_map/ppermute | solution.py:23
  7.5 0.1 collective-permute-start.1
  7.6 3.6 %collective-permute-done.1.note_other = f32[1,16,128]{2,1,0:T(8,128)S(1)} collective-permute-done((f32[1,16,128]{2,1,0:T(8,128)S(1)}, f32[1,16,128]{2,1,0:T(8,128)S(1)}, u32[]{:S(2)}, u32[]{:S(2)}) %collective-permute-start.1) | collective-permute-done | bytes 8224 | tf_op jit(solution)/shard_map/ppermute | solution.py:23
  11.2 0.0 collective-permute-done.received
  11.2 2.8 %collective-permute-start.2 = (bf16[64,1024]{1,0:T(8,128)(2,1)S(1)}, bf16[64,1024]{1,0:T(8,128)(2,1)S(1)}, u32[]{:S(2)}, u32[]{:S(2)}) collective-permute-start(bf16[64,1024]{1,0:T(8,128)(2,1)S(1)} %get-tuple-element.29), channel_id=1, source_target_pairs={{0,2},{1,3},{2,0},{3,1},{4,6},{5,7},{6,4},{7,5},{8,10},{9,11},{10,... | collective-permute-start | bytes 393224 | tf_op jit(solution)/shard_map/ppermute | solution.py:23
  14.0 1.6 %collective-permute-start.3 = (bf16[64,1024]{1,0:T(8,128)(2,1)S(1)}, bf16[64,1024]{1,0:T(8,128)(2,1)S(1)}, u32[]{:S(2)}, u32[]{:S(2)}) collective-permute-start(bf16[64,1024]{1,0:T(8,128)(2,1)S(1)} %get-tuple-element.30), channel_id=1, source_target_pairs={{0,1},{1,0},{2,3},{3,2},{4,5},{5,4},{6,7},{7,6},{8,9},{9,8},{10,11... | collective-permute-start | bytes 393224 | tf_op jit(solution)/shard_map/ppermute | solution.py:23
  15.6 0.0 copy-done.3
  15.6 0.1 reshape.20
  15.7 0.3 collective-permute-start.4
  16.1 0.1 reshape.22
  16.2 0.1 reshape.23.rest_5_.right
  16.2 0.1 reshape.24.rest_4_.left
  16.4 4.0 %collective-permute-done.4.rest_3_ = f32[2,16,128]{2,1,0:T(8,128)S(1)} collective-permute-done((f32[2,16,128]{2,1,0:T(8,128)S(1)}, f32[2,16,128]{2,1,0:T(8,128)S(1)}, u32[]{:S(2)}, u32[]{:S(2)}) %collective-permute-start.4) | collective-permute-done | bytes 16416 | tf_op jit(solution)/shard_map/ppermute | solution.py:23
  20.4 0.0 collective-permute-done.2.rest_0_
  20.4 0.0 collective-permute-done.3.rest_1_
  20.4 0.4 finish.1.rest_4_
  20.8 2.3 %collective-permute-start.9 = (bf16[64,1024]{1,0:T(8,128)(2,1)S(1)}, bf16[64,1024]{1,0:T(8,128)(2,1)S(1)}, u32[]{:S(2)}, u32[]{:S(2)}) collective-permute-start(bf16[64,1024]{1,0:T(8,128)(2,1)S(1)} %finish.1.rest_4_), channel_id=1, source_target_pairs={{0,2},{1,3},{2,0},{3,1},{4,6},{5,7},{6,4},{7,5},{8,10},{9,11},{10,... | collective-permute-start | bytes 393224 | tf_op jit(solution)/shard_map/ppermute | solution.py:23
  23.1 4.6 %collective-permute-start.6 = (bf16[64,1024]{1,0:T(8,128)(2,1)S(1)}, bf16[64,1024]{1,0:T(8,128)(2,1)S(1)}, u32[]{:S(2)}, u32[]{:S(2)}) collective-permute-start(bf16[64,1024]{1,0:T(8,128)(2,1)S(1)} %finish.1.rest_4_), channel_id=1, source_target_pairs={{0,17},{1,16},{2,19},{3,18},{16,1},{17,0},{18,3},{19,2},{4,21},{5,... | collective-permute-start | bytes 393224 | tf_op jit(solution)/shard_map/ppermute | solution.py:33
  27.6 0.0 collective-permute-start.5
  27.6 1.5 %collective-permute-start.10 = (bf16[64,1024]{1,0:T(8,128)(2,1)S(1)}, bf16[64,1024]{1,0:T(8,128)(2,1)S(1)}, u32[]{:S(2)}, u32[]{:S(2)}) collective-permute-start(bf16[64,1024]{1,0:T(8,128)(2,1)S(1)} %finish.1.rest_4_), channel_id=1, source_target_pairs={{0,8},{4,12},{8,0},{12,4},{1,9},{5,13},{9,1},{13,5},{2,10},{6,14},... | collective-permute-start | bytes 393224 | tf_op jit(solution)/shard_map/ppermute | solution.py:23
  29.2 0.0 collective-permute-done.9.rest_5_
  29.2 0.8 %collective-permute-start.11 = (bf16[64,1024]{1,0:T(8,128)(2,1)S(1)}, bf16[64,1024]{1,0:T(8,128)(2,1)S(1)}, u32[]{:S(2)}, u32[]{:S(2)}) collective-permute-start(bf16[64,1024]{1,0:T(8,128)(2,1)S(1)} %collective-permute-done.9.rest_5_), channel_id=1, source_target_pairs={{0,8},{4,12},{8,0},{12,4},{1,9},{5,13},{9,1},{13,5},{2,10},{6,14},... | collective-permute-start | bytes 393224 | tf_op jit(solution)/shard_map/ppermute | solution.py:23
  30.0 1.7 %collective-permute-done.6.rest_1_ = bf16[64,1024]{1,0:T(8,128)(2,1)S(1)} collective-permute-done((bf16[64,1024]{1,0:T(8,128)(2,1)S(1)}, bf16[64,1024]{1,0:T(8,128)(2,1)S(1)}, u32[]{:S(2)}, u32[]{:S(2)}) %collective-permute-start.6) | collective-permute-done | bytes 131104 | tf_op jit(solution)/shard_map/ppermute | solution.py:33
  31.7 0.0 collective-permute-start.8
  31.7 1.5 %collective-permute-done.5.rest_0_ = bf16[64,1024]{1,0:T(8,128)(2,1)S(1)} collective-permute-done((bf16[64,1024]{1,0:T(8,128)(2,1)S(1)}, bf16[64,1024]{1,0:T(8,128)(2,1)S(1)}, u32[]{:S(2)}, u32[]{:S(2)}) %collective-permute-start.5) | collective-permute-done | bytes 131104 | tf_op jit(solution)/shard_map/ppermute | solution.py:33
  33.3 0.0 collective-permute-start.7
  33.9 0.0 collective-permute-done.10.rest_6_
  33.9 0.6 %collective-permute-done.11.rest_7_ = bf16[64,1024]{1,0:T(8,128)(2,1)S(1)} collective-permute-done((bf16[64,1024]{1,0:T(8,128)(2,1)S(1)}, bf16[64,1024]{1,0:T(8,128)(2,1)S(1)}, u32[]{:S(2)}, u32[]{:S(2)}) %collective-permute-start.11) | collective-permute-done | bytes 131104 | tf_op jit(solution)/shard_map/ppermute | solution.py:23
  34.5 0.0 collective-permute-done.8.rest_3_
  34.5 0.1 collective-permute-done.7.rest_2_
  34.6 0.6 %scores.1 = (f32[256,256]{1,0:T(8,128)S(1)}, f32[1,256]{1,0:T(1,128)S(1)}, f32[2,256]{1,0:T(2,128)S(1)}, bf16[256,1024]{1,0:T(8,128)(2,1)S(1)}) custom-call(f32[1]{0:T(128)} %bitcast.3.multiplier, s32[256,1]{1,0:T(8,128)S(1)} %reshape.24.rest_4_.left, s32[1,256]{1,0:T(1,128)S(1)} %reshape.23.rest_5_.right, ...), custom_call_target="tpu_custom_call" | custom-call | tf_op jit(solution)/shard_map/scores/pallas_call | solution.py:380
  35.3 1.6 %collective-permute-start.13 = (f32[2,256]{1,0:T(2,128)S(1)}, f32[2,256]{1,0:T(2,128)S(1)}, u32[]{:S(2)}, u32[]{:S(2)}) collective-permute-start(f32[2,256]{1,0:T(2,128)S(1)} %get-tuple-element.35.column), channel_id=1, source_target_pairs={{0,8},{4,12},{8,0},{12,4},{1,9},{5,13},{9,1},{13,5},{2,10},{6,14},... | collective-permute-start | bytes 6152 | tf_op jit(solution)/shard_map/ppermute | solution.py:23
  36.8 0.0 collective-permute-start.12
  36.8 1.1 %collective-permute-done.12.row_other = f32[1,256]{1,0:T(1,128)S(1)} collective-permute-done((f32[1,256]{1,0:T(1,128)S(1)}, f32[1,256]{1,0:T(1,128)S(1)}, u32[]{:S(2)}, u32[]{:S(2)}) %collective-permute-start.12) | collective-permute-done | bytes 1056 | tf_op jit(solution)/shard_map/ppermute | solution.py:23
  38.0 0.9 %collective-permute-done.13.column_other = f32[2,256]{1,0:T(2,128)S(1)} collective-permute-done((f32[2,256]{1,0:T(2,128)S(1)}, f32[2,256]{1,0:T(2,128)S(1)}, u32[]{:S(2)}, u32[]{:S(2)}) %collective-permute-start.13) | collective-permute-done | bytes 2080 | tf_op jit(solution)/shard_map/ppermute | solution.py:23
  38.9 1.5 %collective-permute-start.15 = (f32[2,256]{1,0:T(2,128)S(1)}, f32[2,256]{1,0:T(2,128)S(1)}, u32[]{:S(2)}, u32[]{:S(2)}) collective-permute-start(f32[2,256]{1,0:T(2,128)S(1)} %get-tuple-element.37.column), channel_id=1, source_target_pairs={{0,2},{1,3},{2,0},{3,1},{4,6},{5,7},{6,4},{7,5},{8,10},{9,11},{10,... | collective-permute-start | bytes 6152 | tf_op jit(solution)/shard_map/ppermute | solution.py:23
  40.4 0.8 %collective-permute-start.14 = (f32[1,256]{1,0:T(1,128)S(1)}, f32[1,256]{1,0:T(1,128)S(1)}, u32[]{:S(2)}, u32[]{:S(2)}) collective-permute-start(f32[1,256]{1,0:T(1,128)S(1)} %get-tuple-element.36.row), channel_id=1, source_target_pairs={{0,1},{1,0},{2,3},{3,2},{4,5},{5,4},{6,7},{7,6},{8,9},{9,8},{10,11... | collective-permute-start | bytes 3080 | tf_op jit(solution)/shard_map/ppermute | solution.py:23
  41.3 2.7 %collective-permute-done.14.row_other = f32[1,256]{1,0:T(1,128)S(1)} collective-permute-done((f32[1,256]{1,0:T(1,128)S(1)}, f32[1,256]{1,0:T(1,128)S(1)}, u32[]{:S(2)}, u32[]{:S(2)}) %collective-permute-start.14) | collective-permute-done | bytes 1056 | tf_op jit(solution)/shard_map/ppermute | solution.py:23
  44.0 0.0 collective-permute-done.15.column_other
  44.0 0.6 %grads.1 = (f32[128,1024]{1,0:T(8,128)S(1)}, bf16[128,1024]{1,0:T(8,128)(2,1)S(1)}, f32[1,128]{1,0:T(1,128)S(1)}) custom-call(f32[1]{0:T(128)} %bitcast.4.multiplier, s32[256,1]{1,0:T(8,128)S(1)} %reshape.24.rest_4_.left, s32[1,256]{1,0:T(1,128)S(1)} %reshape.23.rest_5_.right, f32[256,256]{1,0:T(8,128)S(1)} %get-tuple-element.32.scores, ...), custom_call_target="tpu_custom_call" | custom-call | tf_op jit(solution)/shard_map/grads/pallas_call | solution.py:415
  44.6 0.1 collective-permute-start.16
  44.7 0.5 collective-permute-start.17
  45.2 1.0 %collective-permute-done.17.loss_other = f32[1,128]{1,0:T(1,128)S(1)} collective-permute-done((f32[1,128]{1,0:T(1,128)S(1)}, f32[1,128]{1,0:T(1,128)S(1)}, u32[]{:S(2)}, u32[]{:S(2)}) %collective-permute-start.17) | collective-permute-done | bytes 544 | tf_op jit(solution)/shard_map/ppermute | solution.py:23
  46.2 0.0 collective-permute-done.16.received
  46.2 0.1 halve.1
  46.3 0.9 %collective-permute-start.18 = (bf16[64,1024]{1,0:T(8,128)(2,1)S(1)}, bf16[64,1024]{1,0:T(8,128)(2,1)S(1)}, u32[]{:S(2)}, u32[]{:S(2)}) collective-permute-start(bf16[64,1024]{1,0:T(8,128)(2,1)S(1)} %get-tuple-element.42), channel_id=1, source_target_pairs={{0,1},{1,0},{2,3},{3,2},{4,5},{5,4},{6,7},{7,6},{8,9},{9,8},{10,11... | collective-permute-start | bytes 393224 | tf_op jit(solution)/shard_map/ppermute | solution.py:23
  47.2 2.8 %collective-permute-start.21 = (f32[1,128]{1,0:T(1,128)S(1)}, f32[1,128]{1,0:T(1,128)S(1)}, u32[]{:S(2)}, u32[]{:S(2)}) collective-permute-start(f32[1,128]{1,0:T(1,128)S(1)} %get-tuple-element.43.rest_0_), channel_id=1, source_target_pairs={{0,17},{1,16},{2,19},{3,18},{16,1},{17,0},{18,3},{19,2},{4,21},{5,... | collective-permute-start | bytes 1544 | tf_op jit(solution)/shard_map/ppermute | solution.py:33
  50.0 0.5 collective-permute-start.20
  50.5 1.5 %collective-permute-start.19 = (f32[1,128]{1,0:T(1,128)S(1)}, f32[1,128]{1,0:T(1,128)S(1)}, u32[]{:S(2)}, u32[]{:S(2)}) collective-permute-start(f32[1,128]{1,0:T(1,128)S(1)} %get-tuple-element.43.rest_0_), channel_id=1, source_target_pairs={{0,1},{1,0},{2,3},{3,2},{4,5},{5,4},{6,7},{7,6},{8,9},{9,8},{10,11... | collective-permute-start | bytes 1544 | tf_op jit(solution)/shard_map/ppermute | solution.py:23
  52.0 1.8 %collective-permute-done.21.rest_3_ = f32[1,128]{1,0:T(1,128)S(1)} collective-permute-done((f32[1,128]{1,0:T(1,128)S(1)}, f32[1,128]{1,0:T(1,128)S(1)}, u32[]{:S(2)}, u32[]{:S(2)}) %collective-permute-start.21) | collective-permute-done | bytes 544 | tf_op jit(solution)/shard_map/ppermute | solution.py:33
  53.8 0.0 collective-permute-done.20.rest_2_
  53.8 0.3 collective-permute-done.19.rest_1_
  54.1 0.0 collective-permute-done.18.received
  54.1 0.7 %total.1 = (f32[64,1024]{1,0:T(8,128)}, f32[1,1]{1,0:T(1,128)}) custom-call(f32[64,1024]{1,0:T(8,128)S(1)} %get-tuple-element.41.own, bf16[64,1024]{1,0:T(8,128)(2,1)S(1)} %collective-permute-done.18.received, f32[1,128]{1,0:T(1,128)S(1)} %get-tuple-element.43.rest_0_, f32[1,128]{1,0:T(1,128)S(1)} %collective-permute-done.19.rest_1_, ...), custom_call_target="tpu_custom_call" | custom-call | tf_op jit(solution)/shard_map/total/pallas_call | solution.py:440
  (5 shorter events, 0.1 us)
Async XLA Ops:
  0.6 0.9 %copy-start = (bf16[256,256]{1,0:T(8,128)(2,1)S(1)}, bf16[256,256]{1,0:T(8,128)(2,1)}, u32[]{:S(2)}) copy-start(bf16[256,256]{1,0:T(8,128)(2,1)} %text_x.1) | copy-start | bytes 393220
  1.5 0.7 %copy-start.1 = (f32[1536]{0:T(1024)S(1)}, f32[1536]{0:T(1024)}, u32[]{:S(2)}) copy-start(f32[1536]{0:T(1024)} %image_g.1) | copy-start | bytes 18436
  2.2 0.7 %copy-start.2 = (f32[256]{0:T(256)S(1)}, f32[256]{0:T(256)}, u32[]{:S(2)}) copy-start(f32[256]{0:T(256)} %text_g.1) | copy-start | bytes 3076
  2.9 12.7 %copy-start.3 = (s32[1024]{0:T(1024)S(1)}, s32[1024]{0:T(1024)}, u32[]{:S(2)}) copy-start(s32[1024]{0:T(1024)} %param.14) | copy-start | bytes 12292
  4.4 6.8 %collective-permute-start = (bf16[64,1024]{1,0:T(8,128)(2,1)S(1)}, bf16[64,1024]{1,0:T(8,128)(2,1)S(1)}, u32[]{:S(2)}, u32[]{:S(2)}) collective-permute-start(bf16[64,1024]{1,0:T(8,128)(2,1)S(1)} %get-tuple-element.26), channel_id=1, source_target_pairs={{0,1},{1,0},{2,3},{3,2},{4,5},{5,4},{6,7},{7,6},{8,9},{9,8},{10,11... | collective-permute-start | bytes 393224 | tf_op jit(solution)/shard_map/ppermute | solution.py:23
  7.5 3.7 %collective-permute-start.1 = (f32[1,16,128]{2,1,0:T(8,128)S(1)}, f32[1,16,128]{2,1,0:T(8,128)S(1)}, u32[]{:S(2)}, u32[]{:S(2)}) collective-permute-start(f32[1,16,128]{2,1,0:T(8,128)S(1)} %get-tuple-element.28.note), channel_id=1, source_target_pairs={{0,1},{1,0},{2,3},{3,2},{4,5},{5,4},{6,7},{7,6},{8,9},{9,8},{10,11... | collective-permute-start | bytes 24584 | tf_op jit(solution)/shard_map/ppermute | solution.py:23
  11.2 9.1 %collective-permute-start.2 = (bf16[64,1024]{1,0:T(8,128)(2,1)S(1)}, bf16[64,1024]{1,0:T(8,128)(2,1)S(1)}, u32[]{:S(2)}, u32[]{:S(2)}) collective-permute-start(bf16[64,1024]{1,0:T(8,128)(2,1)S(1)} %get-tuple-element.29), channel_id=1, source_target_pairs={{0,2},{1,3},{2,0},{3,1},{4,6},{5,7},{6,4},{7,5},{8,10},{9,11},{10,... | collective-permute-start | bytes 393224 | tf_op jit(solution)/shard_map/ppermute | solution.py:23
  14.0 6.3 %collective-permute-start.3 = (bf16[64,1024]{1,0:T(8,128)(2,1)S(1)}, bf16[64,1024]{1,0:T(8,128)(2,1)S(1)}, u32[]{:S(2)}, u32[]{:S(2)}) collective-permute-start(bf16[64,1024]{1,0:T(8,128)(2,1)S(1)} %get-tuple-element.30), channel_id=1, source_target_pairs={{0,1},{1,0},{2,3},{3,2},{4,5},{5,4},{6,7},{7,6},{8,9},{9,8},{10,11... | collective-permute-start | bytes 393224 | tf_op jit(solution)/shard_map/ppermute | solution.py:23
  15.7 4.6 %collective-permute-start.4 = (f32[2,16,128]{2,1,0:T(8,128)S(1)}, f32[2,16,128]{2,1,0:T(8,128)S(1)}, u32[]{:S(2)}, u32[]{:S(2)}) collective-permute-start(f32[2,16,128]{2,1,0:T(8,128)S(1)} %get-tuple-element.31.rest_2_), channel_id=1, source_target_pairs={{0,2},{1,3},{2,0},{3,1},{4,6},{5,7},{6,4},{7,5},{8,10},{9,11},{10,... | collective-permute-start | bytes 49160 | tf_op jit(solution)/shard_map/ppermute | solution.py:23
  20.8 8.4 %collective-permute-start.9 = (bf16[64,1024]{1,0:T(8,128)(2,1)S(1)}, bf16[64,1024]{1,0:T(8,128)(2,1)S(1)}, u32[]{:S(2)}, u32[]{:S(2)}) collective-permute-start(bf16[64,1024]{1,0:T(8,128)(2,1)S(1)} %finish.1.rest_4_), channel_id=1, source_target_pairs={{0,2},{1,3},{2,0},{3,1},{4,6},{5,7},{6,4},{7,5},{8,10},{9,11},{10,... | collective-permute-start | bytes 393224 | tf_op jit(solution)/shard_map/ppermute | solution.py:23
  23.1 8.6 %collective-permute-start.6 = (bf16[64,1024]{1,0:T(8,128)(2,1)S(1)}, bf16[64,1024]{1,0:T(8,128)(2,1)S(1)}, u32[]{:S(2)}, u32[]{:S(2)}) collective-permute-start(bf16[64,1024]{1,0:T(8,128)(2,1)S(1)} %finish.1.rest_4_), channel_id=1, source_target_pairs={{0,17},{1,16},{2,19},{3,18},{16,1},{17,0},{18,3},{19,2},{4,21},{5,... | collective-permute-start | bytes 393224 | tf_op jit(solution)/shard_map/ppermute | solution.py:33
  27.6 5.6 %collective-permute-start.5 = (bf16[64,1024]{1,0:T(8,128)(2,1)S(1)}, bf16[64,1024]{1,0:T(8,128)(2,1)S(1)}, u32[]{:S(2)}, u32[]{:S(2)}) collective-permute-start(bf16[64,1024]{1,0:T(8,128)(2,1)S(1)} %finish.1.rest_4_), channel_id=1, source_target_pairs={{0,16},{1,17},{2,18},{3,19},{16,0},{17,1},{18,2},{19,3},{4,20},{5,... | collective-permute-start | bytes 393224 | tf_op jit(solution)/shard_map/ppermute | solution.py:33
  27.6 6.3 %collective-permute-start.10 = (bf16[64,1024]{1,0:T(8,128)(2,1)S(1)}, bf16[64,1024]{1,0:T(8,128)(2,1)S(1)}, u32[]{:S(2)}, u32[]{:S(2)}) collective-permute-start(bf16[64,1024]{1,0:T(8,128)(2,1)S(1)} %finish.1.rest_4_), channel_id=1, source_target_pairs={{0,8},{4,12},{8,0},{12,4},{1,9},{5,13},{9,1},{13,5},{2,10},{6,14},... | collective-permute-start | bytes 393224 | tf_op jit(solution)/shard_map/ppermute | solution.py:23
  29.2 5.3 %collective-permute-start.11 = (bf16[64,1024]{1,0:T(8,128)(2,1)S(1)}, bf16[64,1024]{1,0:T(8,128)(2,1)S(1)}, u32[]{:S(2)}, u32[]{:S(2)}) collective-permute-start(bf16[64,1024]{1,0:T(8,128)(2,1)S(1)} %collective-permute-done.9.rest_5_), channel_id=1, source_target_pairs={{0,8},{4,12},{8,0},{12,4},{1,9},{5,13},{9,1},{13,5},{2,10},{6,14},... | collective-permute-start | bytes 393224 | tf_op jit(solution)/shard_map/ppermute | solution.py:23
  31.7 2.8 %collective-permute-start.8 = (bf16[64,1024]{1,0:T(8,128)(2,1)S(1)}, bf16[64,1024]{1,0:T(8,128)(2,1)S(1)}, u32[]{:S(2)}, u32[]{:S(2)}) collective-permute-start(bf16[64,1024]{1,0:T(8,128)(2,1)S(1)} %collective-permute-done.6.rest_1_), channel_id=1, source_target_pairs={{0,4},{4,0},{8,12},{12,8},{1,5},{5,1},{9,13},{13,9},{2,6},{6,2},{1... | collective-permute-start | bytes 393224 | tf_op jit(solution)/shard_map/ppermute | solution.py:23
  33.3 1.3 %collective-permute-start.7 = (bf16[64,1024]{1,0:T(8,128)(2,1)S(1)}, bf16[64,1024]{1,0:T(8,128)(2,1)S(1)}, u32[]{:S(2)}, u32[]{:S(2)}) collective-permute-start(bf16[64,1024]{1,0:T(8,128)(2,1)S(1)} %collective-permute-done.5.rest_0_), channel_id=1, source_target_pairs={{0,4},{4,0},{8,12},{12,8},{1,5},{5,1},{9,13},{13,9},{2,6},{6,2},{1... | collective-permute-start | bytes 393224 | tf_op jit(solution)/shard_map/ppermute | solution.py:23
  35.3 3.7 %collective-permute-start.13 = (f32[2,256]{1,0:T(2,128)S(1)}, f32[2,256]{1,0:T(2,128)S(1)}, u32[]{:S(2)}, u32[]{:S(2)}) collective-permute-start(f32[2,256]{1,0:T(2,128)S(1)} %get-tuple-element.35.column), channel_id=1, source_target_pairs={{0,8},{4,12},{8,0},{12,4},{1,9},{5,13},{9,1},{13,5},{2,10},{6,14},... | collective-permute-start | bytes 6152 | tf_op jit(solution)/shard_map/ppermute | solution.py:23
  36.8 1.1 %collective-permute-start.12 = (f32[1,256]{1,0:T(1,128)S(1)}, f32[1,256]{1,0:T(1,128)S(1)}, u32[]{:S(2)}, u32[]{:S(2)}) collective-permute-start(f32[1,256]{1,0:T(1,128)S(1)} %get-tuple-element.34.row), channel_id=1, source_target_pairs={{0,4},{4,0},{8,12},{12,8},{1,5},{5,1},{9,13},{13,9},{2,6},{6,2},{1... | collective-permute-start | bytes 3080 | tf_op jit(solution)/shard_map/ppermute | solution.py:23
  38.9 5.1 %collective-permute-start.15 = (f32[2,256]{1,0:T(2,128)S(1)}, f32[2,256]{1,0:T(2,128)S(1)}, u32[]{:S(2)}, u32[]{:S(2)}) collective-permute-start(f32[2,256]{1,0:T(2,128)S(1)} %get-tuple-element.37.column), channel_id=1, source_target_pairs={{0,2},{1,3},{2,0},{3,1},{4,6},{5,7},{6,4},{7,5},{8,10},{9,11},{10,... | collective-permute-start | bytes 6152 | tf_op jit(solution)/shard_map/ppermute | solution.py:23
  40.4 3.6 %collective-permute-start.14 = (f32[1,256]{1,0:T(1,128)S(1)}, f32[1,256]{1,0:T(1,128)S(1)}, u32[]{:S(2)}, u32[]{:S(2)}) collective-permute-start(f32[1,256]{1,0:T(1,128)S(1)} %get-tuple-element.36.row), channel_id=1, source_target_pairs={{0,1},{1,0},{2,3},{3,2},{4,5},{5,4},{6,7},{7,6},{8,9},{9,8},{10,11... | collective-permute-start | bytes 3080 | tf_op jit(solution)/shard_map/ppermute | solution.py:23
  44.6 1.6 %collective-permute-start.16 = (bf16[128,1024]{1,0:T(8,128)(2,1)S(1)}, bf16[128,1024]{1,0:T(8,128)(2,1)S(1)}, u32[]{:S(2)}, u32[]{:S(2)}) collective-permute-start(bf16[128,1024]{1,0:T(8,128)(2,1)S(1)} %get-tuple-element.39), channel_id=1, source_target_pairs={{0,4},{4,0},{8,12},{12,8},{1,5},{5,1},{9,13},{13,9},{2,6},{6,2},{1... | collective-permute-start | bytes 786440 | tf_op jit(solution)/shard_map/ppermute | solution.py:23
  44.7 1.5 %collective-permute-start.17 = (f32[1,128]{1,0:T(1,128)S(1)}, f32[1,128]{1,0:T(1,128)S(1)}, u32[]{:S(2)}, u32[]{:S(2)}) collective-permute-start(f32[1,128]{1,0:T(1,128)S(1)} %get-tuple-element.40.loss), channel_id=1, source_target_pairs={{0,4},{4,0},{8,12},{12,8},{1,5},{5,1},{9,13},{13,9},{2,6},{6,2},{1... | collective-permute-start | bytes 1544 | tf_op jit(solution)/shard_map/ppermute | solution.py:23
  46.3 7.8 %collective-permute-start.18 = (bf16[64,1024]{1,0:T(8,128)(2,1)S(1)}, bf16[64,1024]{1,0:T(8,128)(2,1)S(1)}, u32[]{:S(2)}, u32[]{:S(2)}) collective-permute-start(bf16[64,1024]{1,0:T(8,128)(2,1)S(1)} %get-tuple-element.42), channel_id=1, source_target_pairs={{0,1},{1,0},{2,3},{3,2},{4,5},{5,4},{6,7},{7,6},{8,9},{9,8},{10,11... | collective-permute-start | bytes 393224 | tf_op jit(solution)/shard_map/ppermute | solution.py:23
  47.2 6.5 %collective-permute-start.21 = (f32[1,128]{1,0:T(1,128)S(1)}, f32[1,128]{1,0:T(1,128)S(1)}, u32[]{:S(2)}, u32[]{:S(2)}) collective-permute-start(f32[1,128]{1,0:T(1,128)S(1)} %get-tuple-element.43.rest_0_), channel_id=1, source_target_pairs={{0,17},{1,16},{2,19},{3,18},{16,1},{17,0},{18,3},{19,2},{4,21},{5,... | collective-permute-start | bytes 1544 | tf_op jit(solution)/shard_map/ppermute | solution.py:33
  50.0 3.7 %collective-permute-start.20 = (f32[1,128]{1,0:T(1,128)S(1)}, f32[1,128]{1,0:T(1,128)S(1)}, u32[]{:S(2)}, u32[]{:S(2)}) collective-permute-start(f32[1,128]{1,0:T(1,128)S(1)} %get-tuple-element.43.rest_0_), channel_id=1, source_target_pairs={{0,16},{1,17},{2,18},{3,19},{16,0},{17,1},{18,2},{19,3},{4,20},{5,... | collective-permute-start | bytes 1544 | tf_op jit(solution)/shard_map/ppermute | solution.py:33
  50.5 3.5 %collective-permute-start.19 = (f32[1,128]{1,0:T(1,128)S(1)}, f32[1,128]{1,0:T(1,128)S(1)}, u32[]{:S(2)}, u32[]{:S(2)}) collective-permute-start(f32[1,128]{1,0:T(1,128)S(1)} %get-tuple-element.43.rest_0_), channel_id=1, source_target_pairs={{0,1},{1,0},{2,3},{3,2},{4,5},{5,4},{6,7},{7,6},{8,9},{9,8},{10,11... | collective-permute-start | bytes 1544 | tf_op jit(solution)/shard_map/ppermute | solution.py:23

commit v4 on v3

--- a/solution.py
+++ b/solution.py
@@ -10,6 +10,11 @@
 norm_epsilon = 1e-05
 unit_epsilon = 1e-06
 lanes = 128
+X_CUTS = 1
+R_BLOCK = 16
+ROW_COPIES = 8
+COLUMN_COPIES = 8
+P_STEP = 512
 VMEM = pl.BlockSpec(memory_space=pltpu.VMEM)
 SMEM = pl.BlockSpec(memory_space=pltpu.SMEM)
 HBM = pl.BlockSpec(memory_space=pltpu.HBM)
@@ -50,71 +55,68 @@
     return jnp.where(row == 0, log_add(a, b), a + b)
 
 
-def project_kernel(shards, image_x, text_x, image_g, text_g, image_p, text_p, *rest):
-    own_out, kept_out, near_out, far_out, note, x_buf, p_buf, total, sems = rest
-    rows = x_buf.shape[0]
+def split_rows(value, rows):
+    high = value.astype(bf16).astype(f32)
+    middle = (value - high).astype(bf16).astype(f32)
+    low = value - high - middle
+    row = lax.broadcasted_iota(jnp.int32, (rows, value.shape[1]), 0)
+    parts = jnp.where(row == 0, high, jnp.where(row == 1, middle, jnp.where(row == 2, low, 0.0)))
+    return parts.astype(bf16)
+
+
+def project_kernel(shards, x_hbm, gain, p_hbm, *rest):
+    own_out, kept_out, near_out, far_out, note, x_buf, p_buf, scaled, total, sems = rest
+    rows, width = x_buf.shape
     span = rows // shards
     width_out = total.shape[1]
     me = lax.axis_index("mp")
-
-    def tower(x_hbm, gain, p_hbm):
-        width = x_hbm.shape[1]
-        step = min(width, 512)
-        chunks = width // step
-        x_copy = pltpu.make_async_copy(x_hbm, x_buf.at[:, pl.ds(0, width)], sems.at[0])
-        x_copy.start()
-        copies = []
-        for c in range(chunks):
-            copy = pltpu.make_async_copy(
-                p_hbm.at[pl.ds(c * step, step)], p_buf.at[pl.ds(c * step, step)], sems.at[1 + c]
-            )
-            copy.start()
-            copies.append(copy)
-        x_copy.wait()
-        values = x_buf[:, :width].astype(f32)
-        mean = jnp.sum(values, axis=1, keepdims=True) / width
-        spread = jnp.sum((values - mean) * (values - mean), axis=1, keepdims=True)
-        lane = lax.broadcasted_iota(jnp.int32, (rows, lanes), 1)
-        stats = jnp.transpose(jnp.where(lane == 0, mean, jnp.where(lane == 1, spread, 0.0)))
-        offset = jnp.zeros((16, width_out), f32)
-        for c in range(chunks):
-            g = gain[c * step : (c + 1) * step].reshape(1, step)
-            high = g.astype(bf16).astype(f32)
-            middle = (g - high).astype(bf16).astype(f32)
-            low = g - high - middle
-            row = lax.broadcasted_iota(jnp.int32, (16, step), 0)
-            split = jnp.where(
-                row == 0, high, jnp.where(row == 1, middle, jnp.where(row == 2, low, 0.0))
-            ).astype(bf16)
-            x = x_buf[:, c * step : (c + 1) * step].astype(f32)
-            x = ((x - mean) * g).astype(bf16)
-            copies[c].wait()
-            p = p_buf[c * step : (c + 1) * step, :]
-            product = jnp.dot(x, p, preferred_element_type=f32)
-            if c == 0:
-                total[...] = product
-            else:
-                total[...] += product
-            offset += jnp.dot(split, p, preferred_element_type=f32)
-        offset = jnp.sum(offset, axis=0, keepdims=True)
-        height = width_out // lanes
-        for j in range(height):
-            note[0, j : j + 1, :] = offset[:, j * lanes : (j + 1) * lanes]
-        many = rows // lanes
-        for j in range(many):
-            for kind in range(2):
-                at = height + kind * many + j
-                note[0, at : at + 1, :] = stats[kind : kind + 1, j * lanes : (j + 1) * lanes]
-
-    side = lax.axis_index("group")
-
-    @pl.when(side == 0)
-    def _():
-        tower(text_x, text_g, text_p)
-
-    @pl.when(side == 1)
-    def _():
-        tower(image_x, image_g, image_p)
+    some = rows // X_CUTS
+    x_copies = []
+    for c in range(X_CUTS):
+        at = pl.ds(c * some, some)
+        copy = pltpu.make_async_copy(x_hbm.at[at], x_buf.at[at], sems.at[c])
+        copy.start()
+        x_copies.append(copy)
+    cuts = max(1, width // P_STEP)
+    deep = width // cuts
+    copies = []
+    for c in range(cuts):
+        at = pl.ds(c * deep, deep)
+        copy = pltpu.make_async_copy(p_hbm.at[at], p_buf.at[at], sems.at[X_CUTS + c])
+        copy.start()
+        copies.append(copy)
+    g = gain[...].reshape(1, width)
+    scaled[rows:, :] = split_rows(g, 16)
+    packs = []
+    lane = lax.broadcasted_iota(jnp.int32, (R_BLOCK, lanes), 1)
+    for c in range(X_CUTS):
+        x_copies[c].wait()
+        for r in range(c * some, (c + 1) * some, R_BLOCK):
+            at = slice(r, r + R_BLOCK)
+            values = x_buf[at, :].astype(f32)
+            mean = jnp.sum(values, axis=1, keepdims=True) / width
+            centred = values - mean
+            spread = jnp.sum(centred * centred, axis=1, keepdims=True)
+            scaled[at, :] = (centred * g).astype(bf16)
+            packs.append(jnp.where(lane == 0, mean, jnp.where(lane == 1, spread, 0.0)))
+    stats = jnp.transpose(jnp.concatenate(packs, axis=0))
+    height = width_out // lanes
+    many = rows // lanes
+    for j in range(many):
+        for kind in range(2):
+            at = height + kind * many + j
+            note[0, at : at + 1, :] = stats[kind : kind + 1, j * lanes : (j + 1) * lanes]
+    for c in range(cuts):
+        copies[c].wait()
+        at = slice(c * deep, (c + 1) * deep)
+        product = jnp.dot(scaled[:, at], p_buf[at, :], preferred_element_type=f32)
+        if c == 0:
+            total[...] = product
+        else:
+            total[...] += product
+    offset = jnp.sum(total[rows:, :], axis=0, keepdims=True)
+    for j in range(height):
+        note[0, j : j + 1, :] = offset[:, j * lanes : (j + 1) * lanes]
 
     def block(distance):
         return total[pl.ds(pl.multiple_of((me ^ distance) * span, span), span), :]
@@ -127,13 +129,16 @@
     own_out[...] = block(0)
 
 
-def pair_kernel(kept, received, near, note, note_other, *rest):
-    *outs, near_out, notes = rest
+def pair_kernel(kept, received, near, *rest):
+    *outs, near_out = rest
     near_out[...] = near[...]
     span = outs[0].shape[0]
     for m, out in enumerate(outs):
         at = slice(m * span, (m + 1) * span)
         out[...] = (kept[at, :] + received[at, :].astype(f32)).astype(bf16)
+
+
+def both_kernel(note, note_other, notes):
     notes[0] = note[0]
     notes[1] = note_other[0]
 
@@ -210,29 +215,36 @@
     row_part = row_peak + jnp.log(jnp.sum(jnp.exp(scores - row_peak), axis=1, keepdims=True))
     row_out[...] = jnp.transpose(jnp.broadcast_to(row_part, (scores.shape[0], lanes)))[0:1, :]
     column_peak = jnp.max(scores, axis=0, keepdims=True)
-    column_out[0:1, :] = column_peak + jnp.log(
+    column_part = column_peak + jnp.log(
         jnp.sum(jnp.exp(scores - column_peak), axis=0, keepdims=True)
     )
     matched = left[...] == right[...]
-    column_out[1:2, :] = jnp.sum(jnp.where(matched, scores, 0.0), axis=0, keepdims=True)
-
-
-def merge_kernel(row, row_other, column, column_other, row_out, column_out):
-    row_out[...] = log_add(row[...], row_other[...])
-    column_out[...] = merge_columns(column[...], column_other[...])
+    target = jnp.sum(jnp.where(matched, scores, 0.0), axis=0, keepdims=True)
+    row = lax.broadcasted_iota(jnp.int32, column_out.shape, 0)
+    column_out[...] = jnp.where(row == 0, column_part, jnp.where(row == 1, target, 0.0))
+
+
+def merge_rows_kernel(row, row_other, out):
+    out[...] = jnp.broadcast_to(log_add(row[...], row_other[...]), out.shape)
+
+
+def merge_columns_kernel(column, column_other, after, out):
+    out[...] = merge_columns(column[0:2, :], column_other[0:2, :])
 
 
 def grads_kernel(
-    multiplier, left, right, scores, gathered, row, row_other, column, column_other, *rest
+    multiplier, left, right, scores, gathered, column, column_other, *rest
 ):
-    kept_out, sent_out, loss_out, total = rest
-    rows = kept_out.shape[0]
+    row, row_other, kept_out, sent_out, loss_out, total = rest
+    rows, width_out = kept_out.shape
     core = lax.rem(lax.axis_index("dp"), 2)
-    row_total = log_add(row[...], row_other[...])
+    row_total = log_add(row[0:1, :], row_other[0:1, :])
     column_both = merge_columns(column[...], column_other[...])
     column_total = column_both[0:1, :]
     loss = jnp.sum(column_total - column_both[1:2, :], axis=1, keepdims=True)
-    loss_out[...] = jnp.broadcast_to(loss, loss_out.shape)
+    loss = jnp.broadcast_to(loss, loss_out.shape)
+    loss_out[...] = loss
+    sent_out[:, width_out:] = split_rows(loss, rows)
     row_total = jnp.transpose(jnp.broadcast_to(row_total, (lanes, row_total.shape[1])))[:, 0:1]
     matched = left[...] == right[...]
     values = scores[...]
@@ -243,24 +255,28 @@
     )
     total[...] = jnp.dot(weights.astype(bf16), gathered[...], preferred_element_type=f32)
     kept_out[...] = total[pl.ds(pl.multiple_of(core * rows, rows), rows), :]
-    sent_out[...] = total[pl.ds(pl.multiple_of((1 - core) * rows, rows), rows), :].astype(bf16)
-
-
-def halve_kernel(kept, received, loss, loss_other, own_out, sent_out, loss_out):
-    loss_out[...] = loss[...] + loss_other[...]
-    rows = own_out.shape[0]
+    sent_out[:, :width_out] = total[
+        pl.ds(pl.multiple_of((1 - core) * rows, rows), rows), :
+    ].astype(bf16)
+
+
+def halve_kernel(kept, received, loss, own_out, sent_out, loss_out):
+    rows, width_out = own_out.shape
     near = lax.rem(lax.axis_index("mp"), 2)
     mine = pl.ds(pl.multiple_of(near * rows, rows), rows)
     yours = pl.ds(pl.multiple_of((1 - near) * rows, rows), rows)
-    own_out[...] = kept[mine, :] + received[mine, :].astype(f32)
-    sent_out[...] = (kept[yours, :] + received[yours, :].astype(f32)).astype(bf16)
-
-
-def total_kernel(scale, own, received, *rest):
-    losses = rest[:4]
-    out, loss_out = rest[4:]
-    out[...] = own[...] + received[...].astype(f32)
-    loss = tree([l[...] for l in losses], jnp.add)
+    loss = loss[...] + jnp.sum(received[:, width_out:].astype(f32), axis=0, keepdims=True)
+    loss_out[...] = loss
+    own_out[...] = kept[mine, :] + received[mine, :width_out].astype(f32)
+    sent_out[:, :width_out] = (kept[yours, :] + received[yours, :width_out].astype(f32)).astype(bf16)
+    sent_out[:, width_out:] = split_rows(loss, rows)
+
+
+def total_kernel(scale, own, received, loss, there, there_near, out, loss_out):
+    width_out = own.shape[1]
+    out[...] = own[...] + received[:, :width_out].astype(f32)
+    near = jnp.sum(received[:, width_out:].astype(f32), axis=0, keepdims=True)
+    loss = (loss[...] + near) + (there[...] + there_near[...])
     loss_out[...] = loss[:, 0:1] * scale
 
 
@@ -280,45 +296,53 @@
     note_height = -(-(width_out // lanes + 2 * many) // 8) * 8
     shape = jax.ShapeDtypeStruct
 
-    widest = max(image_features.shape[1], text_features.shape[1])
-    own, kept, near_part, far_part, note = pl.pallas_call(
-        functools.partial(project_kernel, shards),
-        out_shape=[
-            shape((span, width_out), f32),
-            shape(((fars - 1) * span, width_out), f32),
-            shape((span, width_out), bf16),
-            shape(((fars - 1) * span, width_out), bf16),
-            shape((1, note_height, lanes), f32),
-        ],
-        in_specs=[HBM, HBM, VMEM, VMEM, HBM, HBM],
-        out_specs=[VMEM] * 5,
-        scratch_shapes=[
-            pltpu.VMEM((rows, widest), bf16),
-            pltpu.VMEM((widest, width_out), bf16),
-            pltpu.VMEM((rows, width_out), f32),
-            pltpu.SemaphoreType.DMA((1 + max(1, widest // 512),)),
-        ],
-        compiler_params=PARAMS_P,
-        name="project",
-    )(
-        image_features,
-        text_features,
-        image_gain,
-        text_gain,
-        image_proj,
-        text_proj,
+    def project(x, gain, p):
+        width = x.shape[1]
+        return pl.pallas_call(
+            functools.partial(project_kernel, shards),
+            out_shape=[
+                shape((span, width_out), f32),
+                shape(((fars - 1) * span, width_out), f32),
+                shape((span, width_out), bf16),
+                shape(((fars - 1) * span, width_out), bf16),
+                shape((1, note_height, lanes), f32),
+            ],
+            in_specs=[HBM, VMEM, HBM],
+            out_specs=[VMEM] * 5,
+            scratch_shapes=[
+                pltpu.VMEM((rows, width), bf16),
+                pltpu.VMEM((width, width_out), bf16),
+                pltpu.VMEM((rows + 16, width), bf16),
+                pltpu.VMEM((rows + 16, width_out), f32),
+                pltpu.SemaphoreType.DMA((X_CUTS + max(1, width // P_STEP),)),
+            ],
+            compiler_params=PARAMS_P,
+            name="project",
+        )(x, gain, p)
+
+    own, kept, near_part, far_part, note = lax.cond(
+        group == 0,
+        lambda: project(text_features, text_gain, text_proj),
+        lambda: project(image_features, image_gain, image_proj),
     )
     far_other = exchange(far_part, "mp", 1)
     note_other = exchange(note, "mp", 1)
-    *pairs, near_part, both = pl.pallas_call(
+    *pairs, near_part = pl.pallas_call(
         pair_kernel,
-        out_shape=[shape((span, width_out), bf16)] * fars
-        + [shape((2, note_height, lanes), f32)],
-        in_specs=[VMEM] * 5,
-        out_specs=[VMEM] * (fars + 1),
+        out_shape=[shape((span, width_out), bf16)] * fars,
+        in_specs=[VMEM] * 3,
+        out_specs=[VMEM] * fars,
         compiler_params=PARAMS,
         name="pair",
-    )(kept, far_other, near_part, note, note_other)
+    )(kept, far_other, near_part)
+    both = pl.pallas_call(
+        both_kernel,
+        out_shape=shape((2, note_height, lanes), f32),
+        in_specs=[VMEM] * 2,
+        out_specs=VMEM,
+        compiler_params=PARAMS,
+        name="both",
+    )(note, note_other)
     parts = []
     notes = [both]
     for m in range(1, fars):
@@ -382,7 +406,7 @@
         out_shape=[
             shape((row_count, column_count), f32),
             shape((1, row_count), f32),
-            shape((2, column_count), f32),
+            shape((COLUMN_COPIES, column_count), f32),
             shape((column_count, width_out), bf16),
         ],
         in_specs=[SMEM] + [VMEM] * (2 + 4 + halves * fars),
@@ -392,31 +416,30 @@
         name="scores",
     )(multiplier, left, right, *owns, *blocks)
 
-    row_steps = [("dp", 1), ("mp", 1)]
+    def merged(kernel, height, *operands):
+        return pl.pallas_call(
+            kernel,
+            out_shape=shape((height, operands[0].shape[1]), f32),
+            in_specs=[VMEM] * len(operands),
+            out_specs=VMEM,
+            compiler_params=PARAMS,
+            name="merge",
+        )(*operands)
+
     column_steps = [("dp", 2 << i) for i in range((halves - 1).bit_length())]
     column_steps += [("mp", 2 << i) for i in range((fars - 1).bit_length())]
     row, column = row_part, column_part
-    while len(column_steps) > 2:
-        axis, distance = column_steps.pop(0)
-        column = merge_columns(column, exchange(column, axis, distance))
-    for (row_axis, row_distance), (column_axis, column_distance) in zip(row_steps, column_steps):
-        row_other = exchange(row, row_axis, row_distance)
-        column_other = exchange(column, column_axis, column_distance)
-        if row_axis == "dp":
-            row, column = pl.pallas_call(
-                merge_kernel,
-                out_shape=[shape(row.shape, f32), shape(column.shape, f32)],
-                in_specs=[VMEM] * 4,
-                out_specs=[VMEM] * 2,
-                compiler_params=PARAMS,
-        name="merge",
-            )(row, row_other, column, column_other)
+    row = merged(merge_rows_kernel, ROW_COPIES, row, exchange(row, "dp", 1))
+    row_other = exchange(row, "mp", 1)
+    for axis, distance in column_steps[:-1]:
+        column = merged(merge_columns_kernel, 2, column, exchange(column, axis, distance), row)
+    column_other = exchange(column, *column_steps[-1])
 
     kept, sent, loss = pl.pallas_call(
         grads_kernel,
         out_shape=[
             shape((2 * span, width_out), f32),
-            shape((2 * span, width_out), bf16),
+            shape((2 * span, width_out + lanes), bf16),
             shape((1, lanes), f32),
         ],
         in_specs=[SMEM] + [VMEM] * 8,
@@ -424,34 +447,28 @@
         scratch_shapes=[pltpu.VMEM((row_count, width_out), f32)],
         compiler_params=PARAMS,
         name="grads",
-    )(multiplier, left, right, scores, gathered, row, row_other, column, column_other)
+    )(multiplier, left, right, scores, gathered, column, column_other, row, row_other)
     own, sent, loss = pl.pallas_call(
         halve_kernel,
         out_shape=[
             shape((span, width_out), f32),
-            shape((span, width_out), bf16),
+            shape((span, width_out + lanes), bf16),
             shape((1, lanes), f32),
         ],
-        in_specs=[VMEM] * 4,
+        in_specs=[VMEM] * 3,
         out_specs=[VMEM] * 3,
         compiler_params=PARAMS,
         name="halve",
-    )(kept, exchange(sent, "dp", 1), loss, exchange(loss, "dp", 1))
+    )(kept, exchange(sent, "dp", 1), loss)
+    there, there_near = cross_exchange(loss, 0), cross_exchange(loss, 1)
     grads, loss = pl.pallas_call(
         functools.partial(total_kernel, 1.0 / (2.0 * owners * rows)),
         out_shape=[shape((span, width_out), f32), shape((1, 1), f32)],
-        in_specs=[VMEM] * 6,
+        in_specs=[VMEM] * 5,
         out_specs=[VMEM] * 2,
         compiler_params=PARAMS,
         name="total",
-    )(
-        own,
-        exchange(sent, "mp", 1),
-        loss,
-        exchange(loss, "mp", 1),
-        cross_exchange(loss, 0),
-        cross_exchange(loss, 1),
-    )
+    )(own, exchange(sent, "mp", 1), loss, there, there_near)
     return (grads[None, :, :], loss[0, 0])
 
 

time: 55 us -> 51.7 us (0.940)
  starting transfers between devices: 27.3 us -> 24.6 us
  local copies, waits for them, and re-layouts: 2.68 us -> 0.41 us
  waiting for transfers between devices: 19.4 us -> 20.3 us
  Pallas kernels: 4.04 us -> 4.8 us
    unnamed x8 -> x2, local copies, waits for them, and re-layouts: 2.28 us -> 0.01 us
    ppermute x4, waiting for transfers between devices: 5 us -> 6.59 us  [cross_exchange(): return lax.ppermute(shard, ('group', 'mp'), pairs)]
    ppermute x4, starting transfers between devices: 7.87 us -> 6.36 us  [cross_exchange(): return lax.ppermute(shard, ('group', 'mp'), pairs)]
    ppermute x18 -> x16, starting transfers between devices: 19.4 us -> 18.2 us  [exchange(): lax.ppermute(shard, axis, [(i, i ^ distance) for i in range(lax.axis_size...]
    pallas_call x2 -> x4, Pallas kernels: 1.52 us -> 2.25 us  [the longest x1 2.22 us: project(): pl.pallas_call(functools.partial(project_kernel, shards), out_shape=[shap...]
    ppermute x18 -> x16, waiting for transfers between devices: 14.4 us -> 13.7 us  [exchange(): lax.ppermute(shard, axis, [(i, i ^ distance) for i in range(lax.axis_size...]
  transfers between devices with their start and end apart: 22 -> 20, of which waited for: 12 -> 12; matrix products, arithmetic and copies ran while one was open for 1% -> 1% of each run, Pallas kernels for 0% -> 0%
where the time goes in v4:
time: 51.7 us; the launch traced here: 51.5 us
  starting transfers between devices  24.6 us (48%)
  waiting for transfers between devices  20.3 us (39%)
  Pallas kernels  4.8 us (9%)
  between operations  1.38 us (3%)
    ppermute x16, starting transfers between devices, exchange(): lax.ppermute(shard, axis, [(i, i ^ distance) for i in range(lax.axis_size...  18.2 us
    ppermute x16, waiting for transfers between devices, exchange(): lax.ppermute(shard, axis, [(i, i ^ distance) for i in range(lax.axis_size...  13.7 us
    ppermute x4, waiting for transfers between devices, cross_exchange(): return lax.ppermute(shard, ('group', 'mp'), pairs)  6.59 us
    ppermute x4, starting transfers between devices, cross_exchange(): return lax.ppermute(shard, ('group', 'mp'), pairs)  6.36 us
    pallas_call x1, Pallas kernels, project(): pl.pallas_call(functools.partial(project_kernel, shards), out_shape=[shap...  2.22 us
  transfers between devices with their start and end apart: 20, of which 12 were waited for; matrix products, arithmetic and copies ran while one was open for 1% of the time, Pallas kernels for 0%

profile of v4, /device:TPU:0, one launch (start us, length us, event | category | flops | bytes accessed | tf_op | source)
XLA Modules:
  0.0 51.5 jit_solution(3467632212713125148)
XLA Ops:
  0.6 0.0 copy-start
  0.6 2.2 %conditional.1 = ((f32[64,1024]{1,0:T(8,128)S(1)}, f32[64,1024]{1,0:T(8,128)S(1)}, bf16[64,1024]{1,0:T(8,128)(2,1)S(1)}, bf16[64,1024]{1,0:T(8,128)(2,1)S(1)}, f32[1,16,128]{2,1,0:T(8,128)S(1)})) conditional(s32[]{:T(128)} %convert_element_type.3, (bf16[256,1536]{1,0:T(8,128)(2,1)}, f32[1536]{0:T(1024)}, bf16[1536,1024]{1,0:T(8,128)(2,1)}) %tuple.14, ...), branch_computations={%region_0.0_spmd, %region_1.0_spmd} | conditional | bytes 8 | solution.py:323
  0.7 2.2 %project.3 = (f32[64,1024]{1,0:T(8,128)S(1)}, f32[64,1024]{1,0:T(8,128)S(1)}, bf16[64,1024]{1,0:T(8,128)(2,1)S(1)}, bf16[64,1024]{1,0:T(8,128)(2,1)S(1)}, f32[1,16,128]{2,1,0:T(8,128)S(1)}) custom-call(bf16[256,256]{1,0:T(8,128)(2,1)} %get-tuple-element.67.x_hbm, f32[256]{0:T(256)} %get-tuple-element.68.gain, bf16[256,1024]{1,0:T(8,128)(2,1)} %get-tuple-element.69.p_hbm), custom_call_target="tpu_custom_call" | custom-call | tf_op jit(solution)/shard_map/cond/branch_1_fun/project/pallas_call | solution.py:301
  2.9 3.1 %collective-permute-start = (bf16[64,1024]{1,0:T(8,128)(2,1)S(1)}, bf16[64,1024]{1,0:T(8,128)(2,1)S(1)}, u32[]{:S(2)}, u32[]{:S(2)}) collective-permute-start(bf16[64,1024]{1,0:T(8,128)(2,1)S(1)} %get-tuple-element.41), channel_id=1, source_target_pairs={{0,1},{1,0},{2,3},{3,2},{4,5},{5,4},{6,7},{7,6},{8,9},{9,8},{10,11... | collective-permute-start | bytes 393224 | tf_op jit(solution)/shard_map/ppermute | solution.py:28
  6.0 0.1 collective-permute-start.3
  6.1 3.5 %collective-permute-done.received = bf16[64,1024]{1,0:T(8,128)(2,1)S(1)} collective-permute-done((bf16[64,1024]{1,0:T(8,128)(2,1)S(1)}, bf16[64,1024]{1,0:T(8,128)(2,1)S(1)}, u32[]{:S(2)}, u32[]{:S(2)}) %collective-permute-start) | collective-permute-done | bytes 131104 | tf_op jit(solution)/shard_map/ppermute | solution.py:28
  9.6 2.8 %collective-permute-start.1 = (bf16[64,1024]{1,0:T(8,128)(2,1)S(1)}, bf16[64,1024]{1,0:T(8,128)(2,1)S(1)}, u32[]{:S(2)}, u32[]{:S(2)}) collective-permute-start(bf16[64,1024]{1,0:T(8,128)(2,1)S(1)} %get-tuple-element.43), channel_id=1, source_target_pairs={{0,2},{1,3},{2,0},{3,1},{4,6},{5,7},{6,4},{7,5},{8,10},{9,11},{10,... | collective-permute-start | bytes 393224 | tf_op jit(solution)/shard_map/ppermute | solution.py:28
  12.4 1.6 %collective-permute-start.2 = (bf16[64,1024]{1,0:T(8,128)(2,1)S(1)}, bf16[64,1024]{1,0:T(8,128)(2,1)S(1)}, u32[]{:S(2)}, u32[]{:S(2)}) collective-permute-start(bf16[64,1024]{1,0:T(8,128)(2,1)S(1)} %get-tuple-element.44), channel_id=1, source_target_pairs={{0,1},{1,0},{2,3},{3,2},{4,5},{5,4},{6,7},{7,6},{8,9},{9,8},{10,11... | collective-permute-start | bytes 393224 | tf_op jit(solution)/shard_map/ppermute | solution.py:28
  14.0 0.0 copy-done
  14.0 0.1 reshape.20
  14.1 0.0 collective-permute-done.3.note_other
  14.1 0.4 collective-permute-start.4
  14.5 0.1 reshape.22
  14.6 0.1 reshape.23.rest_5_.right
  14.7 0.1 reshape.24.rest_4_.left
  14.8 4.0 %collective-permute-done.4.rest_3_ = f32[2,16,128]{2,1,0:T(8,128)S(1)} collective-permute-done((f32[2,16,128]{2,1,0:T(8,128)S(1)}, f32[2,16,128]{2,1,0:T(8,128)S(1)}, u32[]{:S(2)}, u32[]{:S(2)}) %collective-permute-start.4) | collective-permute-done | bytes 16416 | tf_op jit(solution)/shard_map/ppermute | solution.py:28
  18.8 0.0 collective-permute-done.1.rest_0_
  18.8 0.0 collective-permute-done.2.rest_1_
  18.8 0.4 finish.1.rest_4_
  19.3 2.1 %collective-permute-start.9 = (bf16[64,1024]{1,0:T(8,128)(2,1)S(1)}, bf16[64,1024]{1,0:T(8,128)(2,1)S(1)}, u32[]{:S(2)}, u32[]{:S(2)}) collective-permute-start(bf16[64,1024]{1,0:T(8,128)(2,1)S(1)} %finish.1.rest_4_), channel_id=1, source_target_pairs={{0,2},{1,3},{2,0},{3,1},{4,6},{5,7},{6,4},{7,5},{8,10},{9,11},{10,... | collective-permute-start | bytes 393224 | tf_op jit(solution)/shard_map/ppermute | solution.py:28
  21.4 4.0 %collective-permute-start.6 = (bf16[64,1024]{1,0:T(8,128)(2,1)S(1)}, bf16[64,1024]{1,0:T(8,128)(2,1)S(1)}, u32[]{:S(2)}, u32[]{:S(2)}) collective-permute-start(bf16[64,1024]{1,0:T(8,128)(2,1)S(1)} %finish.1.rest_4_), channel_id=1, source_target_pairs={{0,17},{1,16},{2,19},{3,18},{16,1},{17,0},{18,3},{19,2},{4,21},{5,... | collective-permute-start | bytes 393224 | tf_op jit(solution)/shard_map/ppermute | solution.py:38
  25.3 0.0 collective-permute-start.5
  25.4 1.5 %collective-permute-start.10 = (bf16[64,1024]{1,0:T(8,128)(2,1)S(1)}, bf16[64,1024]{1,0:T(8,128)(2,1)S(1)}, u32[]{:S(2)}, u32[]{:S(2)}) collective-permute-start(bf16[64,1024]{1,0:T(8,128)(2,1)S(1)} %finish.1.rest_4_), channel_id=1, source_target_pairs={{0,8},{4,12},{8,0},{12,4},{1,9},{5,13},{9,1},{13,5},{2,10},{6,14},... | collective-permute-start | bytes 393224 | tf_op jit(solution)/shard_map/ppermute | solution.py:28
  26.9 0.0 collective-permute-done.9.rest_5_
  26.9 1.1 %collective-permute-start.11 = (bf16[64,1024]{1,0:T(8,128)(2,1)S(1)}, bf16[64,1024]{1,0:T(8,128)(2,1)S(1)}, u32[]{:S(2)}, u32[]{:S(2)}) collective-permute-start(bf16[64,1024]{1,0:T(8,128)(2,1)S(1)} %collective-permute-done.9.rest_5_), channel_id=1, source_target_pairs={{0,8},{4,12},{8,0},{12,4},{1,9},{5,13},{9,1},{13,5},{2,10},{6,14},... | collective-permute-start | bytes 393224 | tf_op jit(solution)/shard_map/ppermute | solution.py:28
  28.0 1.3 %collective-permute-done.6.rest_1_ = bf16[64,1024]{1,0:T(8,128)(2,1)S(1)} collective-permute-done((bf16[64,1024]{1,0:T(8,128)(2,1)S(1)}, bf16[64,1024]{1,0:T(8,128)(2,1)S(1)}, u32[]{:S(2)}, u32[]{:S(2)}) %collective-permute-start.6) | collective-permute-done | bytes 131104 | tf_op jit(solution)/shard_map/ppermute | solution.py:38
  29.3 0.0 collective-permute-start.8
  29.3 1.5 %collective-permute-done.5.rest_0_ = bf16[64,1024]{1,0:T(8,128)(2,1)S(1)} collective-permute-done((bf16[64,1024]{1,0:T(8,128)(2,1)S(1)}, bf16[64,1024]{1,0:T(8,128)(2,1)S(1)}, u32[]{:S(2)}, u32[]{:S(2)}) %collective-permute-start.5) | collective-permute-done | bytes 131104 | tf_op jit(solution)/shard_map/ppermute | solution.py:38
  30.9 0.0 collective-permute-start.7
  31.5 0.0 collective-permute-done.10.rest_6_
  31.5 0.6 %collective-permute-done.11.rest_7_ = bf16[64,1024]{1,0:T(8,128)(2,1)S(1)} collective-permute-done((bf16[64,1024]{1,0:T(8,128)(2,1)S(1)}, bf16[64,1024]{1,0:T(8,128)(2,1)S(1)}, u32[]{:S(2)}, u32[]{:S(2)}) %collective-permute-start.11) | collective-permute-done | bytes 131104 | tf_op jit(solution)/shard_map/ppermute | solution.py:28
  32.1 0.0 collective-permute-done.8.rest_3_
  32.1 0.1 collective-permute-done.7.rest_2_
  32.2 0.6 %scores.1 = (f32[256,256]{1,0:T(8,128)S(1)}, f32[1,256]{1,0:T(1,128)S(1)}, f32[8,256]{1,0:T(8,128)S(1)}, bf16[256,1024]{1,0:T(8,128)(2,1)S(1)}) custom-call(f32[1]{0:T(128)} %bitcast.3.multiplier, s32[256,1]{1,0:T(8,128)S(1)} %reshape.24.rest_4_.left, s32[1,256]{1,0:T(1,128)S(1)} %reshape.23.rest_5_.right, ...), custom_call_target="tpu_custom_call" | custom-call | tf_op jit(solution)/shard_map/scores/pallas_call | solution.py:404
  32.9 1.6 %collective-permute-start.12 = (f32[8,256]{1,0:T(8,128)S(1)}, f32[8,256]{1,0:T(8,128)S(1)}, u32[]{:S(2)}, u32[]{:S(2)}) collective-permute-start(f32[8,256]{1,0:T(8,128)S(1)} %get-tuple-element.48.column), channel_id=1, source_target_pairs={{0,8},{4,12},{8,0},{12,4},{1,9},{5,13},{9,1},{13,5},{2,10},{6,14},... | collective-permute-start | bytes 24584 | tf_op jit(solution)/shard_map/ppermute | solution.py:28
  34.4 0.0 collective-permute-start.13
  34.4 1.1 %collective-permute-done.13.row_other = f32[1,256]{1,0:T(1,128)S(1)} collective-permute-done((f32[1,256]{1,0:T(1,128)S(1)}, f32[1,256]{1,0:T(1,128)S(1)}, u32[]{:S(2)}, u32[]{:S(2)}) %collective-permute-start.13) | collective-permute-done | bytes 1056 | tf_op jit(solution)/shard_map/ppermute | solution.py:28
  35.6 0.6 %collective-permute-start.15 = (f32[8,256]{1,0:T(8,128)S(1)}, f32[8,256]{1,0:T(8,128)S(1)}, u32[]{:S(2)}, u32[]{:S(2)}) collective-permute-start(f32[8,256]{1,0:T(8,128)S(1)} %merge.2.after.rest_0_), channel_id=1, source_target_pairs={{0,1},{1,0},{2,3},{3,2},{4,5},{5,4},{6,7},{7,6},{8,9},{9,8},{10,11... | collective-permute-start | bytes 24584 | tf_op jit(solution)/shard_map/ppermute | solution.py:28
  36.2 0.4 collective-permute-done.12.column_other
  36.6 2.1 %collective-permute-start.14 = (f32[2,256]{1,0:T(2,128)S(1)}, f32[2,256]{1,0:T(2,128)S(1)}, u32[]{:S(2)}, u32[]{:S(2)}) collective-permute-start(f32[2,256]{1,0:T(2,128)S(1)} %merge.3.column), channel_id=1, source_target_pairs={{0,2},{1,3},{2,0},{3,1},{4,6},{5,7},{6,4},{7,5},{8,10},{9,11},{10,... | collective-permute-start | bytes 6152 | tf_op jit(solution)/shard_map/ppermute | solution.py:28
  38.7 0.6 %collective-permute-done.15.rest_1_ = f32[8,256]{1,0:T(8,128)S(1)} collective-permute-done((f32[8,256]{1,0:T(8,128)S(1)}, f32[8,256]{1,0:T(8,128)S(1)}, u32[]{:S(2)}, u32[]{:S(2)}) %collective-permute-start.15) | collective-permute-done | bytes 8224 | tf_op jit(solution)/shard_map/ppermute | solution.py:28
  39.3 1.8 %collective-permute-done.14.column_other = f32[2,256]{1,0:T(2,128)S(1)} collective-permute-done((f32[2,256]{1,0:T(2,128)S(1)}, f32[2,256]{1,0:T(2,128)S(1)}, u32[]{:S(2)}, u32[]{:S(2)}) %collective-permute-start.14) | collective-permute-done | bytes 2080 | tf_op jit(solution)/shard_map/ppermute | solution.py:28
  41.1 0.6 %grads.1 = (f32[128,1024]{1,0:T(8,128)S(1)}, bf16[128,1152]{1,0:T(8,128)(2,1)S(1)}, f32[1,128]{1,0:T(1,128)S(1)}) custom-call(f32[1]{0:T(128)} %bitcast.4.multiplier, s32[256,1]{1,0:T(8,128)S(1)} %reshape.24.rest_4_.left, s32[1,256]{1,0:T(1,128)S(1)} %reshape.23.rest_5_.right, f32[256,256]{1,0:T(8,128)S(1)} %get-tuple-element.46.scores, ...), custom_call_target="tpu_custom_call" | custom-call | tf_op jit(solution)/shard_map/grads/pallas_call | solution.py:438
  41.8 0.1 collective-permute-start.16
  41.8 1.6 %collective-permute-done.16.received = bf16[128,1152]{1,0:T(8,128)(2,1)S(1)} collective-permute-done((bf16[128,1152]{1,0:T(8,128)(2,1)S(1)}, bf16[128,1152]{1,0:T(8,128)(2,1)S(1)}, u32[]{:S(2)}, u32[]{:S(2)}) %collective-permute-start.16) | collective-permute-done | bytes 294944 | tf_op jit(solution)/shard_map/ppermute | solution.py:28
  43.4 0.1 halve.1
  43.5 1.2 %collective-permute-start.17 = (bf16[64,1152]{1,0:T(8,128)(2,1)S(1)}, bf16[64,1152]{1,0:T(8,128)(2,1)S(1)}, u32[]{:S(2)}, u32[]{:S(2)}) collective-permute-start(bf16[64,1152]{1,0:T(8,128)(2,1)S(1)} %get-tuple-element.54), channel_id=1, source_target_pairs={{0,1},{1,0},{2,3},{3,2},{4,5},{5,4},{6,7},{7,6},{8,9},{9,8},{10,11... | collective-permute-start | bytes 442376 | tf_op jit(solution)/shard_map/ppermute | solution.py:28
  44.6 2.3 %collective-permute-start.19 = (f32[1,128]{1,0:T(1,128)S(1)}, f32[1,128]{1,0:T(1,128)S(1)}, u32[]{:S(2)}, u32[]{:S(2)}) collective-permute-start(f32[1,128]{1,0:T(1,128)S(1)} %get-tuple-element.55.loss), channel_id=1, source_target_pairs={{0,17},{1,16},{2,19},{3,18},{16,1},{17,0},{18,3},{19,2},{4,21},{5,... | collective-permute-start | bytes 1544 | tf_op jit(solution)/shard_map/ppermute | solution.py:38
  46.9 0.1 collective-permute-start.18
  47.0 3.7 %collective-permute-done.19.there_near = f32[1,128]{1,0:T(1,128)S(1)} collective-permute-done((f32[1,128]{1,0:T(1,128)S(1)}, f32[1,128]{1,0:T(1,128)S(1)}, u32[]{:S(2)}, u32[]{:S(2)}) %collective-permute-start.19) | collective-permute-done | bytes 544 | tf_op jit(solution)/shard_map/ppermute | solution.py:38
  50.8 0.0 collective-permute-done.18.there
  50.8 0.0 collective-permute-done.17.received
  50.8 0.7 %total.1 = (f32[64,1024]{1,0:T(8,128)}, f32[1,1]{1,0:T(1,128)}) custom-call(f32[64,1024]{1,0:T(8,128)S(1)} %get-tuple-element.53.own, bf16[64,1152]{1,0:T(8,128)(2,1)S(1)} %collective-permute-done.17.received, f32[1,128]{1,0:T(1,128)S(1)} %get-tuple-element.55.loss, f32[1,128]{1,0:T(1,128)S(1)} %collective-permute-done.18.there, ...), custom_call_target="tpu_custom_call" | custom-call | tf_op jit(solution)/shard_map/total/pallas_call | solution.py:464
  (7 shorter events, 0.1 us)
Async XLA Ops:
  0.6 13.4 %copy-start = (s32[1024]{0:T(1024)S(1)}, s32[1024]{0:T(1024)}, u32[]{:S(2)}) copy-start(s32[1024]{0:T(1024)} %param.16) | copy-start | bytes 12292
  2.9 6.7 %collective-permute-start = (bf16[64,1024]{1,0:T(8,128)(2,1)S(1)}, bf16[64,1024]{1,0:T(8,128)(2,1)S(1)}, u32[]{:S(2)}, u32[]{:S(2)}) collective-permute-start(bf16[64,1024]{1,0:T(8,128)(2,1)S(1)} %get-tuple-element.41), channel_id=1, source_target_pairs={{0,1},{1,0},{2,3},{3,2},{4,5},{5,4},{6,7},{7,6},{8,9},{9,8},{10,11... | collective-permute-start | bytes 393224 | tf_op jit(solution)/shard_map/ppermute | solution.py:28
  6.0 8.1 %collective-permute-start.3 = (f32[1,16,128]{2,1,0:T(8,128)S(1)}, f32[1,16,128]{2,1,0:T(8,128)S(1)}, u32[]{:S(2)}, u32[]{:S(2)}) collective-permute-start(f32[1,16,128]{2,1,0:T(8,128)S(1)} %get-tuple-element.45.note), channel_id=1, source_target_pairs={{0,1},{1,0},{2,3},{3,2},{4,5},{5,4},{6,7},{7,6},{8,9},{9,8},{10,11... | collective-permute-start | bytes 24584 | tf_op jit(solution)/shard_map/ppermute | solution.py:28
  9.6 9.2 %collective-permute-start.1 = (bf16[64,1024]{1,0:T(8,128)(2,1)S(1)}, bf16[64,1024]{1,0:T(8,128)(2,1)S(1)}, u32[]{:S(2)}, u32[]{:S(2)}) collective-permute-start(bf16[64,1024]{1,0:T(8,128)(2,1)S(1)} %get-tuple-element.43), channel_id=1, source_target_pairs={{0,2},{1,3},{2,0},{3,1},{4,6},{5,7},{6,4},{7,5},{8,10},{9,11},{10,... | collective-permute-start | bytes 393224 | tf_op jit(solution)/shard_map/ppermute | solution.py:28
  12.4 6.4 %collective-permute-start.2 = (bf16[64,1024]{1,0:T(8,128)(2,1)S(1)}, bf16[64,1024]{1,0:T(8,128)(2,1)S(1)}, u32[]{:S(2)}, u32[]{:S(2)}) collective-permute-start(bf16[64,1024]{1,0:T(8,128)(2,1)S(1)} %get-tuple-element.44), channel_id=1, source_target_pairs={{0,1},{1,0},{2,3},{3,2},{4,5},{5,4},{6,7},{7,6},{8,9},{9,8},{10,11... | collective-permute-start | bytes 393224 | tf_op jit(solution)/shard_map/ppermute | solution.py:28
  14.1 4.7 %collective-permute-start.4 = (f32[2,16,128]{2,1,0:T(8,128)S(1)}, f32[2,16,128]{2,1,0:T(8,128)S(1)}, u32[]{:S(2)}, u32[]{:S(2)}) collective-permute-start(f32[2,16,128]{2,1,0:T(8,128)S(1)} %both.1.rest_2_), channel_id=1, source_target_pairs={{0,2},{1,3},{2,0},{3,1},{4,6},{5,7},{6,4},{7,5},{8,10},{9,11},{10,... | collective-permute-start | bytes 49160 | tf_op jit(solution)/shard_map/ppermute | solution.py:28
  19.3 7.6 %collective-permute-start.9 = (bf16[64,1024]{1,0:T(8,128)(2,1)S(1)}, bf16[64,1024]{1,0:T(8,128)(2,1)S(1)}, u32[]{:S(2)}, u32[]{:S(2)}) collective-permute-start(bf16[64,1024]{1,0:T(8,128)(2,1)S(1)} %finish.1.rest_4_), channel_id=1, source_target_pairs={{0,2},{1,3},{2,0},{3,1},{4,6},{5,7},{6,4},{7,5},{8,10},{9,11},{10,... | collective-permute-start | bytes 393224 | tf_op jit(solution)/shard_map/ppermute | solution.py:28
  21.4 8.0 %collective-permute-start.6 = (bf16[64,1024]{1,0:T(8,128)(2,1)S(1)}, bf16[64,1024]{1,0:T(8,128)(2,1)S(1)}, u32[]{:S(2)}, u32[]{:S(2)}) collective-permute-start(bf16[64,1024]{1,0:T(8,128)(2,1)S(1)} %finish.1.rest_4_), channel_id=1, source_target_pairs={{0,17},{1,16},{2,19},{3,18},{16,1},{17,0},{18,3},{19,2},{4,21},{5,... | collective-permute-start | bytes 393224 | tf_op jit(solution)/shard_map/ppermute | solution.py:38
  25.3 5.5 %collective-permute-start.5 = (bf16[64,1024]{1,0:T(8,128)(2,1)S(1)}, bf16[64,1024]{1,0:T(8,128)(2,1)S(1)}, u32[]{:S(2)}, u32[]{:S(2)}) collective-permute-start(bf16[64,1024]{1,0:T(8,128)(2,1)S(1)} %finish.1.rest_4_), channel_id=1, source_target_pairs={{0,16},{1,17},{2,18},{3,19},{16,0},{17,1},{18,2},{19,3},{4,20},{5,... | collective-permute-start | bytes 393224 | tf_op jit(solution)/shard_map/ppermute | solution.py:38
  25.4 6.2 %collective-permute-start.10 = (bf16[64,1024]{1,0:T(8,128)(2,1)S(1)}, bf16[64,1024]{1,0:T(8,128)(2,1)S(1)}, u32[]{:S(2)}, u32[]{:S(2)}) collective-permute-start(bf16[64,1024]{1,0:T(8,128)(2,1)S(1)} %finish.1.rest_4_), channel_id=1, source_target_pairs={{0,8},{4,12},{8,0},{12,4},{1,9},{5,13},{9,1},{13,5},{2,10},{6,14},... | collective-permute-start | bytes 393224 | tf_op jit(solution)/shard_map/ppermute | solution.py:28
  26.9 5.2 %collective-permute-start.11 = (bf16[64,1024]{1,0:T(8,128)(2,1)S(1)}, bf16[64,1024]{1,0:T(8,128)(2,1)S(1)}, u32[]{:S(2)}, u32[]{:S(2)}) collective-permute-start(bf16[64,1024]{1,0:T(8,128)(2,1)S(1)} %collective-permute-done.9.rest_5_), channel_id=1, source_target_pairs={{0,8},{4,12},{8,0},{12,4},{1,9},{5,13},{9,1},{13,5},{2,10},{6,14},... | collective-permute-start | bytes 393224 | tf_op jit(solution)/shard_map/ppermute | solution.py:28
  29.3 2.8 %collective-permute-start.8 = (bf16[64,1024]{1,0:T(8,128)(2,1)S(1)}, bf16[64,1024]{1,0:T(8,128)(2,1)S(1)}, u32[]{:S(2)}, u32[]{:S(2)}) collective-permute-start(bf16[64,1024]{1,0:T(8,128)(2,1)S(1)} %collective-permute-done.6.rest_1_), channel_id=1, source_target_pairs={{0,4},{4,0},{8,12},{12,8},{1,5},{5,1},{9,13},{13,9},{2,6},{6,2},{1... | collective-permute-start | bytes 393224 | tf_op jit(solution)/shard_map/ppermute | solution.py:28
  30.9 1.3 %collective-permute-start.7 = (bf16[64,1024]{1,0:T(8,128)(2,1)S(1)}, bf16[64,1024]{1,0:T(8,128)(2,1)S(1)}, u32[]{:S(2)}, u32[]{:S(2)}) collective-permute-start(bf16[64,1024]{1,0:T(8,128)(2,1)S(1)} %collective-permute-done.5.rest_0_), channel_id=1, source_target_pairs={{0,4},{4,0},{8,12},{12,8},{1,5},{5,1},{9,13},{13,9},{2,6},{6,2},{1... | collective-permute-start | bytes 393224 | tf_op jit(solution)/shard_map/ppermute | solution.py:28
  32.9 3.7 %collective-permute-start.12 = (f32[8,256]{1,0:T(8,128)S(1)}, f32[8,256]{1,0:T(8,128)S(1)}, u32[]{:S(2)}, u32[]{:S(2)}) collective-permute-start(f32[8,256]{1,0:T(8,128)S(1)} %get-tuple-element.48.column), channel_id=1, source_target_pairs={{0,8},{4,12},{8,0},{12,4},{1,9},{5,13},{9,1},{13,5},{2,10},{6,14},... | collective-permute-start | bytes 24584 | tf_op jit(solution)/shard_map/ppermute | solution.py:28
  34.4 1.1 %collective-permute-start.13 = (f32[1,256]{1,0:T(1,128)S(1)}, f32[1,256]{1,0:T(1,128)S(1)}, u32[]{:S(2)}, u32[]{:S(2)}) collective-permute-start(f32[1,256]{1,0:T(1,128)S(1)} %get-tuple-element.49.row), channel_id=1, source_target_pairs={{0,4},{4,0},{8,12},{12,8},{1,5},{5,1},{9,13},{13,9},{2,6},{6,2},{1... | collective-permute-start | bytes 3080 | tf_op jit(solution)/shard_map/ppermute | solution.py:28
  35.6 3.7 %collective-permute-start.15 = (f32[8,256]{1,0:T(8,128)S(1)}, f32[8,256]{1,0:T(8,128)S(1)}, u32[]{:S(2)}, u32[]{:S(2)}) collective-permute-start(f32[8,256]{1,0:T(8,128)S(1)} %merge.2.after.rest_0_), channel_id=1, source_target_pairs={{0,1},{1,0},{2,3},{3,2},{4,5},{5,4},{6,7},{7,6},{8,9},{9,8},{10,11... | collective-permute-start | bytes 24584 | tf_op jit(solution)/shard_map/ppermute | solution.py:28
  36.6 4.5 %collective-permute-start.14 = (f32[2,256]{1,0:T(2,128)S(1)}, f32[2,256]{1,0:T(2,128)S(1)}, u32[]{:S(2)}, u32[]{:S(2)}) collective-permute-start(f32[2,256]{1,0:T(2,128)S(1)} %merge.3.column), channel_id=1, source_target_pairs={{0,2},{1,3},{2,0},{3,1},{4,6},{5,7},{6,4},{7,5},{8,10},{9,11},{10,... | collective-permute-start | bytes 6152 | tf_op jit(solution)/shard_map/ppermute | solution.py:28
  41.8 1.6 %collective-permute-start.16 = (bf16[128,1152]{1,0:T(8,128)(2,1)S(1)}, bf16[128,1152]{1,0:T(8,128)(2,1)S(1)}, u32[]{:S(2)}, u32[]{:S(2)}) collective-permute-start(bf16[128,1152]{1,0:T(8,128)(2,1)S(1)} %get-tuple-element.51), channel_id=1, source_target_pairs={{0,4},{4,0},{8,12},{12,8},{1,5},{5,1},{9,13},{13,9},{2,6},{6,2},{1... | collective-permute-start | bytes 884744 | tf_op jit(solution)/shard_map/ppermute | solution.py:28
  43.5 7.3 %collective-permute-start.17 = (bf16[64,1152]{1,0:T(8,128)(2,1)S(1)}, bf16[64,1152]{1,0:T(8,128)(2,1)S(1)}, u32[]{:S(2)}, u32[]{:S(2)}) collective-permute-start(bf16[64,1152]{1,0:T(8,128)(2,1)S(1)} %get-tuple-element.54), channel_id=1, source_target_pairs={{0,1},{1,0},{2,3},{3,2},{4,5},{5,4},{6,7},{7,6},{8,9},{9,8},{10,11... | collective-permute-start | bytes 442376 | tf_op jit(solution)/shard_map/ppermute | solution.py:28
  44.6 6.1 %collective-permute-start.19 = (f32[1,128]{1,0:T(1,128)S(1)}, f32[1,128]{1,0:T(1,128)S(1)}, u32[]{:S(2)}, u32[]{:S(2)}) collective-permute-start(f32[1,128]{1,0:T(1,128)S(1)} %get-tuple-element.55.loss), channel_id=1, source_target_pairs={{0,17},{1,16},{2,19},{3,18},{16,1},{17,0},{18,3},{19,2},{4,21},{5,... | collective-permute-start | bytes 1544 | tf_op jit(solution)/shard_map/ppermute | solution.py:38
  46.9 3.8 %collective-permute-start.18 = (f32[1,128]{1,0:T(1,128)S(1)}, f32[1,128]{1,0:T(1,128)S(1)}, u32[]{:S(2)}, u32[]{:S(2)}) collective-permute-start(f32[1,128]{1,0:T(1,128)S(1)} %get-tuple-element.55.loss), channel_id=1, source_target_pairs={{0,16},{1,17},{2,18},{3,19},{16,0},{17,1},{18,2},{19,3},{4,20},{5,... | collective-permute-start | bytes 1544 | tf_op jit(solution)/shard_map/ppermute | solution.py:38

commit v5 on v4

--- a/solution.py
+++ b/solution.py
@@ -192,8 +192,8 @@
 
 def scores_kernel(halves, shards, multiplier, left, right, *rest):
     owns = rest[:4]
-    others = rest[4:-5]
-    scores_out, row_out, column_out, gathered, mine = rest[-5:]
+    others = rest[4:-4]
+    scores_out, column_out, gathered, mine = rest[-4:]
     span = owns[0].shape[0]
     fars = shards // 2
     dp, mp = lax.axis_index("dp"), lax.axis_index("mp")
@@ -211,9 +211,6 @@
         mine[...], gathered[...], (((1,), (1,)), ((), ())), preferred_element_type=f32
     )
     scores_out[...] = scores
-    row_peak = jnp.max(scores, axis=1, keepdims=True)
-    row_part = row_peak + jnp.log(jnp.sum(jnp.exp(scores - row_peak), axis=1, keepdims=True))
-    row_out[...] = jnp.transpose(jnp.broadcast_to(row_part, (scores.shape[0], lanes)))[0:1, :]
     column_peak = jnp.max(scores, axis=0, keepdims=True)
     column_part = column_peak + jnp.log(
         jnp.sum(jnp.exp(scores - column_peak), axis=0, keepdims=True)
@@ -224,6 +221,13 @@
     column_out[...] = jnp.where(row == 0, column_part, jnp.where(row == 1, target, 0.0))
 
 
+def rows_kernel(scores, out):
+    values = scores[...]
+    peak = jnp.max(values, axis=1, keepdims=True)
+    part = peak + jnp.log(jnp.sum(jnp.exp(values - peak), axis=1, keepdims=True))
+    out[...] = jnp.transpose(jnp.broadcast_to(part, (values.shape[0], lanes)))[0:1, :]
+
+
 def merge_rows_kernel(row, row_other, out):
     out[...] = jnp.broadcast_to(log_add(row[...], row_other[...]), out.shape)
 
@@ -235,8 +239,8 @@
 def grads_kernel(
     multiplier, left, right, scores, gathered, column, column_other, *rest
 ):
-    row, row_other, kept_out, sent_out, loss_out, total = rest
-    rows, width_out = kept_out.shape
+    row, row_other, sent_out, loss_out, weights = rest
+    rows, width_out = sent_out.shape[0], gathered.shape[1]
     core = lax.rem(lax.axis_index("dp"), 2)
     row_total = log_add(row[0:1, :], row_other[0:1, :])
     column_both = merge_columns(column[...], column_other[...])
@@ -248,16 +252,25 @@
     row_total = jnp.transpose(jnp.broadcast_to(row_total, (lanes, row_total.shape[1])))[:, 0:1]
     matched = left[...] == right[...]
     values = scores[...]
-    weights = multiplier[0] * (
-        jnp.exp(values - row_total)
-        + jnp.exp(values - column_total)
-        - jnp.where(matched, 2.0, 0.0)
-    )
-    total[...] = jnp.dot(weights.astype(bf16), gathered[...], preferred_element_type=f32)
-    kept_out[...] = total[pl.ds(pl.multiple_of(core * rows, rows), rows), :]
-    sent_out[:, :width_out] = total[
-        pl.ds(pl.multiple_of((1 - core) * rows, rows), rows), :
-    ].astype(bf16)
+    weights[...] = (
+        multiplier[0]
+        * (
+            jnp.exp(values - row_total)
+            + jnp.exp(values - column_total)
+            - jnp.where(matched, 2.0, 0.0)
+        )
+    ).astype(bf16)
+    part = weights[pl.ds(pl.multiple_of((1 - core) * rows, rows), rows), :]
+    sent_out[:, :width_out] = jnp.dot(
+        part, gathered[...], preferred_element_type=f32
+    ).astype(bf16)
+
+
+def kept_kernel(weights, gathered, out):
+    rows = out.shape[0]
+    core = lax.rem(lax.axis_index("dp"), 2)
+    part = weights[pl.ds(pl.multiple_of(core * rows, rows), rows), :]
+    out[...] = jnp.dot(part, gathered[...], preferred_element_type=f32)
 
 
 def halve_kernel(kept, received, loss, own_out, sent_out, loss_out):
@@ -401,16 +414,15 @@
         blocks += [exchange(b, "dp", h * 2) for b in others]
     owns += [exchange(b, "dp", 1) for b in owns]
 
-    scores, row_part, column_part, gathered = pl.pallas_call(
+    scores, column_part, gathered = pl.pallas_call(
         functools.partial(scores_kernel, halves, shards),
         out_shape=[
             shape((row_count, column_count), f32),
-            shape((1, row_count), f32),
             shape((COLUMN_COPIES, column_count), f32),
             shape((column_count, width_out), bf16),
         ],
         in_specs=[SMEM] + [VMEM] * (2 + 4 + halves * fars),
-        out_specs=[VMEM] * 4,
+        out_specs=[VMEM] * 3,
         scratch_shapes=[pltpu.VMEM((row_count, width_out), bf16)],
         compiler_params=PARAMS,
         name="scores",
@@ -426,6 +438,15 @@
             name="merge",
         )(*operands)
 
+    row_part = pl.pallas_call(
+        rows_kernel,
+        out_shape=shape((1, row_count), f32),
+        in_specs=[VMEM],
+        out_specs=VMEM,
+        compiler_params=PARAMS,
+        name="rows",
+    )(scores)
+
     column_steps = [("dp", 2 << i) for i in range((halves - 1).bit_length())]
     column_steps += [("mp", 2 << i) for i in range((fars - 1).bit_length())]
     row, column = row_part, column_part
@@ -435,19 +456,26 @@
         column = merged(merge_columns_kernel, 2, column, exchange(column, axis, distance), row)
     column_other = exchange(column, *column_steps[-1])
 
-    kept, sent, loss = pl.pallas_call(
+    sent, loss, weights = pl.pallas_call(
         grads_kernel,
         out_shape=[
-            shape((2 * span, width_out), f32),
             shape((2 * span, width_out + lanes), bf16),
             shape((1, lanes), f32),
+            shape((row_count, column_count), bf16),
         ],
         in_specs=[SMEM] + [VMEM] * 8,
         out_specs=[VMEM] * 3,
-        scratch_shapes=[pltpu.VMEM((row_count, width_out), f32)],
         compiler_params=PARAMS,
         name="grads",
     )(multiplier, left, right, scores, gathered, column, column_other, row, row_other)
+    kept = pl.pallas_call(
+        kept_kernel,
+        out_shape=shape((2 * span, width_out), f32),
+        in_specs=[VMEM] * 2,
+        out_specs=VMEM,
+        compiler_params=PARAMS,
+        name="kept",
+    )(weights, gathered)
     own, sent, loss = pl.pallas_call(
         halve_kernel,
         out_shape=[

time: 51.7 us -> 51.6 us (level)
  waiting for transfers between devices: 20.3 us -> 19.6 us
    ppermute x16, waiting for transfers between devices: 13.7 us -> 12.9 us  [exchange(): lax.ppermute(shard, axis, [(i, i ^ distance) for i in range(lax.axis_size...]
    ppermute x16, starting transfers between devices: 18.2 us -> 18.9 us  [exchange(): lax.ppermute(shard, axis, [(i, i ^ distance) for i in range(lax.axis_size...]
  transfers between devices with their start and end apart: 20 -> 20, of which waited for: 12 -> 12; matrix products, arithmetic and copies ran while one was open for 1% -> 1% of each run, Pallas kernels for 0% -> 1%
where the time goes in v5:
time: 51.6 us; the launch traced here: 51.5 us
  starting transfers between devices  25.1 us (49%)
  waiting for transfers between devices  19.6 us (38%)
  Pallas kernels  4.9 us (9%)
  between operations  1.4 us (3%)
    ppermute x16, starting transfers between devices, exchange(): lax.ppermute(shard, axis, [(i, i ^ distance) for i in range(lax.axis_size...  18.9 us
    ppermute x16, waiting for transfers between devices, exchange(): lax.ppermute(shard, axis, [(i, i ^ distance) for i in range(lax.axis_size...  12.9 us
    ppermute x4, waiting for transfers between devices, cross_exchange(): return lax.ppermute(shard, ('group', 'mp'), pairs)  6.71 us
    ppermute x4, starting transfers between devices, cross_exchange(): return lax.ppermute(shard, ('group', 'mp'), pairs)  6.24 us
    pallas_call x1, Pallas kernels, project(): pl.pallas_call(functools.partial(project_kernel, shards), out_shape=[shap...  2.22 us
  transfers between devices with their start and end apart: 20, of which 12 were waited for; matrix products, arithmetic and copies ran while one was open for 1% of the time, Pallas kernels for 1%

profile of v5, /device:TPU:0, one launch (start us, length us, event | category | flops | bytes accessed | tf_op | source)
XLA Modules:
  0.0 51.5 jit_solution(220948166240988568)
XLA Ops:
  0.6 0.0 copy-start
  0.6 2.2 %conditional.1 = ((f32[64,1024]{1,0:T(8,128)S(1)}, f32[64,1024]{1,0:T(8,128)S(1)}, bf16[64,1024]{1,0:T(8,128)(2,1)S(1)}, bf16[64,1024]{1,0:T(8,128)(2,1)S(1)}, f32[1,16,128]{2,1,0:T(8,128)S(1)})) conditional(s32[]{:T(128)} %convert_element_type.3, (bf16[256,1536]{1,0:T(8,128)(2,1)}, f32[1536]{0:T(1024)}, bf16[1536,1024]{1,0:T(8,128)(2,1)}) %tuple.14, ...), branch_computations={%region_0.0_spmd, %region_1.0_spmd} | conditional | bytes 8 | solution.py:336
  0.7 2.2 %project.3 = (f32[64,1024]{1,0:T(8,128)S(1)}, f32[64,1024]{1,0:T(8,128)S(1)}, bf16[64,1024]{1,0:T(8,128)(2,1)S(1)}, bf16[64,1024]{1,0:T(8,128)(2,1)S(1)}, f32[1,16,128]{2,1,0:T(8,128)S(1)}) custom-call(bf16[256,256]{1,0:T(8,128)(2,1)} %get-tuple-element.65.x_hbm, f32[256]{0:T(256)} %get-tuple-element.66.gain, bf16[256,1024]{1,0:T(8,128)(2,1)} %get-tuple-element.67.p_hbm), custom_call_target="tpu_custom_call" | custom-call | tf_op jit(solution)/shard_map/cond/branch_1_fun/project/pallas_call | solution.py:314
  2.9 3.1 %collective-permute-start = (bf16[64,1024]{1,0:T(8,128)(2,1)S(1)}, bf16[64,1024]{1,0:T(8,128)(2,1)S(1)}, u32[]{:S(2)}, u32[]{:S(2)}) collective-permute-start(bf16[64,1024]{1,0:T(8,128)(2,1)S(1)} %get-tuple-element.40), channel_id=1, source_target_pairs={{0,1},{1,0},{2,3},{3,2},{4,5},{5,4},{6,7},{7,6},{8,9},{9,8},{10,11... | collective-permute-start | bytes 393224 | tf_op jit(solution)/shard_map/ppermute | solution.py:28
  6.0 0.1 collective-permute-start.3
  6.1 3.5 %collective-permute-done.received = bf16[64,1024]{1,0:T(8,128)(2,1)S(1)} collective-permute-done((bf16[64,1024]{1,0:T(8,128)(2,1)S(1)}, bf16[64,1024]{1,0:T(8,128)(2,1)S(1)}, u32[]{:S(2)}, u32[]{:S(2)}) %collective-permute-start) | collective-permute-done | bytes 131104 | tf_op jit(solution)/shard_map/ppermute | solution.py:28
  9.6 2.8 %collective-permute-start.1 = (bf16[64,1024]{1,0:T(8,128)(2,1)S(1)}, bf16[64,1024]{1,0:T(8,128)(2,1)S(1)}, u32[]{:S(2)}, u32[]{:S(2)}) collective-permute-start(bf16[64,1024]{1,0:T(8,128)(2,1)S(1)} %get-tuple-element.42), channel_id=1, source_target_pairs={{0,2},{1,3},{2,0},{3,1},{4,6},{5,7},{6,4},{7,5},{8,10},{9,11},{10,... | collective-permute-start | bytes 393224 | tf_op jit(solution)/shard_map/ppermute | solution.py:28
  12.4 1.6 %collective-permute-start.2 = (bf16[64,1024]{1,0:T(8,128)(2,1)S(1)}, bf16[64,1024]{1,0:T(8,128)(2,1)S(1)}, u32[]{:S(2)}, u32[]{:S(2)}) collective-permute-start(bf16[64,1024]{1,0:T(8,128)(2,1)S(1)} %get-tuple-element.43), channel_id=1, source_target_pairs={{0,1},{1,0},{2,3},{3,2},{4,5},{5,4},{6,7},{7,6},{8,9},{9,8},{10,11... | collective-permute-start | bytes 393224 | tf_op jit(solution)/shard_map/ppermute | solution.py:28
  14.0 0.0 copy-done
  14.0 0.1 reshape.20
  14.1 0.0 collective-permute-done.3.note_other
  14.1 0.4 collective-permute-start.4
  14.5 0.1 reshape.22
  14.6 0.1 reshape.23.rest_5_.right
  14.7 0.1 reshape.24.rest_4_.left
  14.8 4.0 %collective-permute-done.4.rest_3_ = f32[2,16,128]{2,1,0:T(8,128)S(1)} collective-permute-done((f32[2,16,128]{2,1,0:T(8,128)S(1)}, f32[2,16,128]{2,1,0:T(8,128)S(1)}, u32[]{:S(2)}, u32[]{:S(2)}) %collective-permute-start.4) | collective-permute-done | bytes 16416 | tf_op jit(solution)/shard_map/ppermute | solution.py:28
  18.8 0.0 collective-permute-done.1.rest_0_
  18.8 0.0 collective-permute-done.2.rest_1_
  18.8 0.4 finish.1.rest_4_
  19.3 2.1 %collective-permute-start.9 = (bf16[64,1024]{1,0:T(8,128)(2,1)S(1)}, bf16[64,1024]{1,0:T(8,128)(2,1)S(1)}, u32[]{:S(2)}, u32[]{:S(2)}) collective-permute-start(bf16[64,1024]{1,0:T(8,128)(2,1)S(1)} %finish.1.rest_4_), channel_id=1, source_target_pairs={{0,2},{1,3},{2,0},{3,1},{4,6},{5,7},{6,4},{7,5},{8,10},{9,11},{10,... | collective-permute-start | bytes 393224 | tf_op jit(solution)/shard_map/ppermute | solution.py:28
  21.4 4.0 %collective-permute-start.6 = (bf16[64,1024]{1,0:T(8,128)(2,1)S(1)}, bf16[64,1024]{1,0:T(8,128)(2,1)S(1)}, u32[]{:S(2)}, u32[]{:S(2)}) collective-permute-start(bf16[64,1024]{1,0:T(8,128)(2,1)S(1)} %finish.1.rest_4_), channel_id=1, source_target_pairs={{0,17},{1,16},{2,19},{3,18},{16,1},{17,0},{18,3},{19,2},{4,21},{5,... | collective-permute-start | bytes 393224 | tf_op jit(solution)/shard_map/ppermute | solution.py:38
  25.3 0.0 collective-permute-start.5
  25.4 1.5 %collective-permute-start.10 = (bf16[64,1024]{1,0:T(8,128)(2,1)S(1)}, bf16[64,1024]{1,0:T(8,128)(2,1)S(1)}, u32[]{:S(2)}, u32[]{:S(2)}) collective-permute-start(bf16[64,1024]{1,0:T(8,128)(2,1)S(1)} %finish.1.rest_4_), channel_id=1, source_target_pairs={{0,8},{4,12},{8,0},{12,4},{1,9},{5,13},{9,1},{13,5},{2,10},{6,14},... | collective-permute-start | bytes 393224 | tf_op jit(solution)/shard_map/ppermute | solution.py:28
  26.9 0.0 collective-permute-done.9.rest_5_
  26.9 1.1 %collective-permute-start.11 = (bf16[64,1024]{1,0:T(8,128)(2,1)S(1)}, bf16[64,1024]{1,0:T(8,128)(2,1)S(1)}, u32[]{:S(2)}, u32[]{:S(2)}) collective-permute-start(bf16[64,1024]{1,0:T(8,128)(2,1)S(1)} %collective-permute-done.9.rest_5_), channel_id=1, source_target_pairs={{0,8},{4,12},{8,0},{12,4},{1,9},{5,13},{9,1},{13,5},{2,10},{6,14},... | collective-permute-start | bytes 393224 | tf_op jit(solution)/shard_map/ppermute | solution.py:28
  28.0 1.3 %collective-permute-done.6.rest_1_ = bf16[64,1024]{1,0:T(8,128)(2,1)S(1)} collective-permute-done((bf16[64,1024]{1,0:T(8,128)(2,1)S(1)}, bf16[64,1024]{1,0:T(8,128)(2,1)S(1)}, u32[]{:S(2)}, u32[]{:S(2)}) %collective-permute-start.6) | collective-permute-done | bytes 131104 | tf_op jit(solution)/shard_map/ppermute | solution.py:38
  29.3 0.0 collective-permute-start.8
  29.3 1.5 %collective-permute-done.5.rest_0_ = bf16[64,1024]{1,0:T(8,128)(2,1)S(1)} collective-permute-done((bf16[64,1024]{1,0:T(8,128)(2,1)S(1)}, bf16[64,1024]{1,0:T(8,128)(2,1)S(1)}, u32[]{:S(2)}, u32[]{:S(2)}) %collective-permute-start.5) | collective-permute-done | bytes 131104 | tf_op jit(solution)/shard_map/ppermute | solution.py:38
  30.9 0.0 collective-permute-start.7
  31.5 0.0 collective-permute-done.10.rest_6_
  31.5 0.6 %collective-permute-done.11.rest_7_ = bf16[64,1024]{1,0:T(8,128)(2,1)S(1)} collective-permute-done((bf16[64,1024]{1,0:T(8,128)(2,1)S(1)}, bf16[64,1024]{1,0:T(8,128)(2,1)S(1)}, u32[]{:S(2)}, u32[]{:S(2)}) %collective-permute-start.11) | collective-permute-done | bytes 131104 | tf_op jit(solution)/shard_map/ppermute | solution.py:28
  32.1 0.0 collective-permute-done.8.rest_3_
  32.1 0.1 collective-permute-done.7.rest_2_
  32.2 0.5 scores.1
  32.7 1.6 %collective-permute-start.12 = (f32[8,256]{1,0:T(8,128)S(1)}, f32[8,256]{1,0:T(8,128)S(1)}, u32[]{:S(2)}, u32[]{:S(2)}) collective-permute-start(f32[8,256]{1,0:T(8,128)S(1)} %get-tuple-element.47.column), channel_id=1, source_target_pairs={{0,8},{4,12},{8,0},{12,4},{1,9},{5,13},{9,1},{13,5},{2,10},{6,14},... | collective-permute-start | bytes 24584 | tf_op jit(solution)/shard_map/ppermute | solution.py:28
  34.3 0.2 rows.1.row
  34.5 0.0 collective-permute-start.13
  34.6 1.1 %collective-permute-done.13.row_other = f32[1,256]{1,0:T(1,128)S(1)} collective-permute-done((f32[1,256]{1,0:T(1,128)S(1)}, f32[1,256]{1,0:T(1,128)S(1)}, u32[]{:S(2)}, u32[]{:S(2)}) %collective-permute-start.13) | collective-permute-done | bytes 1056 | tf_op jit(solution)/shard_map/ppermute | solution.py:28
  35.7 0.6 %collective-permute-start.15 = (f32[8,256]{1,0:T(8,128)S(1)}, f32[8,256]{1,0:T(8,128)S(1)}, u32[]{:S(2)}, u32[]{:S(2)}) collective-permute-start(f32[8,256]{1,0:T(8,128)S(1)} %merge.2.after.rest_0_), channel_id=1, source_target_pairs={{0,1},{1,0},{2,3},{3,2},{4,5},{5,4},{6,7},{7,6},{8,9},{9,8},{10,11... | collective-permute-start | bytes 24584 | tf_op jit(solution)/shard_map/ppermute | solution.py:28
  36.3 0.1 collective-permute-done.12.column_other
  36.4 2.4 %collective-permute-start.14 = (f32[2,256]{1,0:T(2,128)S(1)}, f32[2,256]{1,0:T(2,128)S(1)}, u32[]{:S(2)}, u32[]{:S(2)}) collective-permute-start(f32[2,256]{1,0:T(2,128)S(1)} %merge.3.column), channel_id=1, source_target_pairs={{0,2},{1,3},{2,0},{3,1},{4,6},{5,7},{6,4},{7,5},{8,10},{9,11},{10,... | collective-permute-start | bytes 6152 | tf_op jit(solution)/shard_map/ppermute | solution.py:28
  38.8 0.6 %collective-permute-done.15.rest_1_ = f32[8,256]{1,0:T(8,128)S(1)} collective-permute-done((f32[8,256]{1,0:T(8,128)S(1)}, f32[8,256]{1,0:T(8,128)S(1)}, u32[]{:S(2)}, u32[]{:S(2)}) %collective-permute-start.15) | collective-permute-done | bytes 8224 | tf_op jit(solution)/shard_map/ppermute | solution.py:28
  39.4 1.6 %collective-permute-done.14.column_other = f32[2,256]{1,0:T(2,128)S(1)} collective-permute-done((f32[2,256]{1,0:T(2,128)S(1)}, f32[2,256]{1,0:T(2,128)S(1)}, u32[]{:S(2)}, u32[]{:S(2)}) %collective-permute-start.14) | collective-permute-done | bytes 2080 | tf_op jit(solution)/shard_map/ppermute | solution.py:28
  41.0 0.4 grads.1
  41.4 0.1 collective-permute-start.16
  41.5 0.2 kept.1
  41.7 1.3 %collective-permute-done.16.received = bf16[128,1152]{1,0:T(8,128)(2,1)S(1)} collective-permute-done((bf16[128,1152]{1,0:T(8,128)(2,1)S(1)}, bf16[128,1152]{1,0:T(8,128)(2,1)S(1)}, u32[]{:S(2)}, u32[]{:S(2)}) %collective-permute-start.16) | collective-permute-done | bytes 294944 | tf_op jit(solution)/shard_map/ppermute | solution.py:28
  43.1 0.1 halve.1
  43.1 1.4 %collective-permute-start.17 = (bf16[64,1152]{1,0:T(8,128)(2,1)S(1)}, bf16[64,1152]{1,0:T(8,128)(2,1)S(1)}, u32[]{:S(2)}, u32[]{:S(2)}) collective-permute-start(bf16[64,1152]{1,0:T(8,128)(2,1)S(1)} %get-tuple-element.52), channel_id=1, source_target_pairs={{0,1},{1,0},{2,3},{3,2},{4,5},{5,4},{6,7},{7,6},{8,9},{9,8},{10,11... | collective-permute-start | bytes 442376 | tf_op jit(solution)/shard_map/ppermute | solution.py:28
  44.6 2.3 %collective-permute-start.19 = (f32[1,128]{1,0:T(1,128)S(1)}, f32[1,128]{1,0:T(1,128)S(1)}, u32[]{:S(2)}, u32[]{:S(2)}) collective-permute-start(f32[1,128]{1,0:T(1,128)S(1)} %get-tuple-element.53.loss), channel_id=1, source_target_pairs={{0,17},{1,16},{2,19},{3,18},{16,1},{17,0},{18,3},{19,2},{4,21},{5,... | collective-permute-start | bytes 1544 | tf_op jit(solution)/shard_map/ppermute | solution.py:38
  46.9 0.0 collective-permute-start.18
  46.9 3.8 %collective-permute-done.19.there_near = f32[1,128]{1,0:T(1,128)S(1)} collective-permute-done((f32[1,128]{1,0:T(1,128)S(1)}, f32[1,128]{1,0:T(1,128)S(1)}, u32[]{:S(2)}, u32[]{:S(2)}) %collective-permute-start.19) | collective-permute-done | bytes 544 | tf_op jit(solution)/shard_map/ppermute | solution.py:38
  50.7 0.0 collective-permute-done.18.there
  50.7 0.0 collective-permute-done.17.received
  50.7 0.7 %total.1 = (f32[64,1024]{1,0:T(8,128)}, f32[1,1]{1,0:T(1,128)}) custom-call(f32[64,1024]{1,0:T(8,128)S(1)} %get-tuple-element.51.own, bf16[64,1152]{1,0:T(8,128)(2,1)S(1)} %collective-permute-done.17.received, f32[1,128]{1,0:T(1,128)S(1)} %get-tuple-element.53.loss, f32[1,128]{1,0:T(1,128)S(1)} %collective-permute-done.18.there, ...), custom_call_target="tpu_custom_call" | custom-call | tf_op jit(solution)/shard_map/total/pallas_call | solution.py:492
  (7 shorter events, 0.1 us)
Async XLA Ops:
  0.6 13.4 %copy-start = (s32[1024]{0:T(1024)S(1)}, s32[1024]{0:T(1024)}, u32[]{:S(2)}) copy-start(s32[1024]{0:T(1024)} %param.16) | copy-start | bytes 12292
  2.9 6.7 %collective-permute-start = (bf16[64,1024]{1,0:T(8,128)(2,1)S(1)}, bf16[64,1024]{1,0:T(8,128)(2,1)S(1)}, u32[]{:S(2)}, u32[]{:S(2)}) collective-permute-start(bf16[64,1024]{1,0:T(8,128)(2,1)S(1)} %get-tuple-element.40), channel_id=1, source_target_pairs={{0,1},{1,0},{2,3},{3,2},{4,5},{5,4},{6,7},{7,6},{8,9},{9,8},{10,11... | collective-permute-start | bytes 393224 | tf_op jit(solution)/shard_map/ppermute | solution.py:28
  6.0 8.1 %collective-permute-start.3 = (f32[1,16,128]{2,1,0:T(8,128)S(1)}, f32[1,16,128]{2,1,0:T(8,128)S(1)}, u32[]{:S(2)}, u32[]{:S(2)}) collective-permute-start(f32[1,16,128]{2,1,0:T(8,128)S(1)} %get-tuple-element.44.note), channel_id=1, source_target_pairs={{0,1},{1,0},{2,3},{3,2},{4,5},{5,4},{6,7},{7,6},{8,9},{9,8},{10,11... | collective-permute-start | bytes 24584 | tf_op jit(solution)/shard_map/ppermute | solution.py:28
  9.6 9.2 %collective-permute-start.1 = (bf16[64,1024]{1,0:T(8,128)(2,1)S(1)}, bf16[64,1024]{1,0:T(8,128)(2,1)S(1)}, u32[]{:S(2)}, u32[]{:S(2)}) collective-permute-start(bf16[64,1024]{1,0:T(8,128)(2,1)S(1)} %get-tuple-element.42), channel_id=1, source_target_pairs={{0,2},{1,3},{2,0},{3,1},{4,6},{5,7},{6,4},{7,5},{8,10},{9,11},{10,... | collective-permute-start | bytes 393224 | tf_op jit(solution)/shard_map/ppermute | solution.py:28
  12.4 6.4 %collective-permute-start.2 = (bf16[64,1024]{1,0:T(8,128)(2,1)S(1)}, bf16[64,1024]{1,0:T(8,128)(2,1)S(1)}, u32[]{:S(2)}, u32[]{:S(2)}) collective-permute-start(bf16[64,1024]{1,0:T(8,128)(2,1)S(1)} %get-tuple-element.43), channel_id=1, source_target_pairs={{0,1},{1,0},{2,3},{3,2},{4,5},{5,4},{6,7},{7,6},{8,9},{9,8},{10,11... | collective-permute-start | bytes 393224 | tf_op jit(solution)/shard_map/ppermute | solution.py:28
  14.1 4.7 %collective-permute-start.4 = (f32[2,16,128]{2,1,0:T(8,128)S(1)}, f32[2,16,128]{2,1,0:T(8,128)S(1)}, u32[]{:S(2)}, u32[]{:S(2)}) collective-permute-start(f32[2,16,128]{2,1,0:T(8,128)S(1)} %both.1.rest_2_), channel_id=1, source_target_pairs={{0,2},{1,3},{2,0},{3,1},{4,6},{5,7},{6,4},{7,5},{8,10},{9,11},{10,... | collective-permute-start | bytes 49160 | tf_op jit(solution)/shard_map/ppermute | solution.py:28
  19.3 7.6 %collective-permute-start.9 = (bf16[64,1024]{1,0:T(8,128)(2,1)S(1)}, bf16[64,1024]{1,0:T(8,128)(2,1)S(1)}, u32[]{:S(2)}, u32[]{:S(2)}) collective-permute-start(bf16[64,1024]{1,0:T(8,128)(2,1)S(1)} %finish.1.rest_4_), channel_id=1, source_target_pairs={{0,2},{1,3},{2,0},{3,1},{4,6},{5,7},{6,4},{7,5},{8,10},{9,11},{10,... | collective-permute-start | bytes 393224 | tf_op jit(solution)/shard_map/ppermute | solution.py:28
  21.4 8.0 %collective-permute-start.6 = (bf16[64,1024]{1,0:T(8,128)(2,1)S(1)}, bf16[64,1024]{1,0:T(8,128)(2,1)S(1)}, u32[]{:S(2)}, u32[]{:S(2)}) collective-permute-start(bf16[64,1024]{1,0:T(8,128)(2,1)S(1)} %finish.1.rest_4_), channel_id=1, source_target_pairs={{0,17},{1,16},{2,19},{3,18},{16,1},{17,0},{18,3},{19,2},{4,21},{5,... | collective-permute-start | bytes 393224 | tf_op jit(solution)/shard_map/ppermute | solution.py:38
  25.3 5.5 %collective-permute-start.5 = (bf16[64,1024]{1,0:T(8,128)(2,1)S(1)}, bf16[64,1024]{1,0:T(8,128)(2,1)S(1)}, u32[]{:S(2)}, u32[]{:S(2)}) collective-permute-start(bf16[64,1024]{1,0:T(8,128)(2,1)S(1)} %finish.1.rest_4_), channel_id=1, source_target_pairs={{0,16},{1,17},{2,18},{3,19},{16,0},{17,1},{18,2},{19,3},{4,20},{5,... | collective-permute-start | bytes 393224 | tf_op jit(solution)/shard_map/ppermute | solution.py:38
  25.4 6.2 %collective-permute-start.10 = (bf16[64,1024]{1,0:T(8,128)(2,1)S(1)}, bf16[64,1024]{1,0:T(8,128)(2,1)S(1)}, u32[]{:S(2)}, u32[]{:S(2)}) collective-permute-start(bf16[64,1024]{1,0:T(8,128)(2,1)S(1)} %finish.1.rest_4_), channel_id=1, source_target_pairs={{0,8},{4,12},{8,0},{12,4},{1,9},{5,13},{9,1},{13,5},{2,10},{6,14},... | collective-permute-start | bytes 393224 | tf_op jit(solution)/shard_map/ppermute | solution.py:28
  26.9 5.2 %collective-permute-start.11 = (bf16[64,1024]{1,0:T(8,128)(2,1)S(1)}, bf16[64,1024]{1,0:T(8,128)(2,1)S(1)}, u32[]{:S(2)}, u32[]{:S(2)}) collective-permute-start(bf16[64,1024]{1,0:T(8,128)(2,1)S(1)} %collective-permute-done.9.rest_5_), channel_id=1, source_target_pairs={{0,8},{4,12},{8,0},{12,4},{1,9},{5,13},{9,1},{13,5},{2,10},{6,14},... | collective-permute-start | bytes 393224 | tf_op jit(solution)/shard_map/ppermute | solution.py:28
  29.3 2.8 %collective-permute-start.8 = (bf16[64,1024]{1,0:T(8,128)(2,1)S(1)}, bf16[64,1024]{1,0:T(8,128)(2,1)S(1)}, u32[]{:S(2)}, u32[]{:S(2)}) collective-permute-start(bf16[64,1024]{1,0:T(8,128)(2,1)S(1)} %collective-permute-done.6.rest_1_), channel_id=1, source_target_pairs={{0,4},{4,0},{8,12},{12,8},{1,5},{5,1},{9,13},{13,9},{2,6},{6,2},{1... | collective-permute-start | bytes 393224 | tf_op jit(solution)/shard_map/ppermute | solution.py:28
  30.9 1.3 %collective-permute-start.7 = (bf16[64,1024]{1,0:T(8,128)(2,1)S(1)}, bf16[64,1024]{1,0:T(8,128)(2,1)S(1)}, u32[]{:S(2)}, u32[]{:S(2)}) collective-permute-start(bf16[64,1024]{1,0:T(8,128)(2,1)S(1)} %collective-permute-done.5.rest_0_), channel_id=1, source_target_pairs={{0,4},{4,0},{8,12},{12,8},{1,5},{5,1},{9,13},{13,9},{2,6},{6,2},{1... | collective-permute-start | bytes 393224 | tf_op jit(solution)/shard_map/ppermute | solution.py:28
  32.7 3.7 %collective-permute-start.12 = (f32[8,256]{1,0:T(8,128)S(1)}, f32[8,256]{1,0:T(8,128)S(1)}, u32[]{:S(2)}, u32[]{:S(2)}) collective-permute-start(f32[8,256]{1,0:T(8,128)S(1)} %get-tuple-element.47.column), channel_id=1, source_target_pairs={{0,8},{4,12},{8,0},{12,4},{1,9},{5,13},{9,1},{13,5},{2,10},{6,14},... | collective-permute-start | bytes 24584 | tf_op jit(solution)/shard_map/ppermute | solution.py:28
  34.5 1.2 %collective-permute-start.13 = (f32[1,256]{1,0:T(1,128)S(1)}, f32[1,256]{1,0:T(1,128)S(1)}, u32[]{:S(2)}, u32[]{:S(2)}) collective-permute-start(f32[1,256]{1,0:T(1,128)S(1)} %rows.1.row), channel_id=1, source_target_pairs={{0,4},{4,0},{8,12},{12,8},{1,5},{5,1},{9,13},{13,9},{2,6},{6,2},{1... | collective-permute-start | bytes 3080 | tf_op jit(solution)/shard_map/ppermute | solution.py:28
  35.7 3.7 %collective-permute-start.15 = (f32[8,256]{1,0:T(8,128)S(1)}, f32[8,256]{1,0:T(8,128)S(1)}, u32[]{:S(2)}, u32[]{:S(2)}) collective-permute-start(f32[8,256]{1,0:T(8,128)S(1)} %merge.2.after.rest_0_), channel_id=1, source_target_pairs={{0,1},{1,0},{2,3},{3,2},{4,5},{5,4},{6,7},{7,6},{8,9},{9,8},{10,11... | collective-permute-start | bytes 24584 | tf_op jit(solution)/shard_map/ppermute | solution.py:28
  36.4 4.5 %collective-permute-start.14 = (f32[2,256]{1,0:T(2,128)S(1)}, f32[2,256]{1,0:T(2,128)S(1)}, u32[]{:S(2)}, u32[]{:S(2)}) collective-permute-start(f32[2,256]{1,0:T(2,128)S(1)} %merge.3.column), channel_id=1, source_target_pairs={{0,2},{1,3},{2,0},{3,1},{4,6},{5,7},{6,4},{7,5},{8,10},{9,11},{10,... | collective-permute-start | bytes 6152 | tf_op jit(solution)/shard_map/ppermute | solution.py:28
  41.4 1.6 %collective-permute-start.16 = (bf16[128,1152]{1,0:T(8,128)(2,1)S(1)}, bf16[128,1152]{1,0:T(8,128)(2,1)S(1)}, u32[]{:S(2)}, u32[]{:S(2)}) collective-permute-start(bf16[128,1152]{1,0:T(8,128)(2,1)S(1)} %get-tuple-element.49), channel_id=1, source_target_pairs={{0,4},{4,0},{8,12},{12,8},{1,5},{5,1},{9,13},{13,9},{2,6},{6,2},{1... | collective-permute-start | bytes 884744 | tf_op jit(solution)/shard_map/ppermute | solution.py:28
  43.1 7.6 %collective-permute-start.17 = (bf16[64,1152]{1,0:T(8,128)(2,1)S(1)}, bf16[64,1152]{1,0:T(8,128)(2,1)S(1)}, u32[]{:S(2)}, u32[]{:S(2)}) collective-permute-start(bf16[64,1152]{1,0:T(8,128)(2,1)S(1)} %get-tuple-element.52), channel_id=1, source_target_pairs={{0,1},{1,0},{2,3},{3,2},{4,5},{5,4},{6,7},{7,6},{8,9},{9,8},{10,11... | collective-permute-start | bytes 442376 | tf_op jit(solution)/shard_map/ppermute | solution.py:28
  44.6 6.1 %collective-permute-start.19 = (f32[1,128]{1,0:T(1,128)S(1)}, f32[1,128]{1,0:T(1,128)S(1)}, u32[]{:S(2)}, u32[]{:S(2)}) collective-permute-start(f32[1,128]{1,0:T(1,128)S(1)} %get-tuple-element.53.loss), channel_id=1, source_target_pairs={{0,17},{1,16},{2,19},{3,18},{16,1},{17,0},{18,3},{19,2},{4,21},{5,... | collective-permute-start | bytes 1544 | tf_op jit(solution)/shard_map/ppermute | solution.py:38
  46.9 3.8 %collective-permute-start.18 = (f32[1,128]{1,0:T(1,128)S(1)}, f32[1,128]{1,0:T(1,128)S(1)}, u32[]{:S(2)}, u32[]{:S(2)}) collective-permute-start(f32[1,128]{1,0:T(1,128)S(1)} %get-tuple-element.53.loss), channel_id=1, source_target_pairs={{0,16},{1,17},{2,18},{3,19},{16,0},{17,1},{18,2},{19,3},{4,20},{5,... | collective-permute-start | bytes 1544 | tf_op jit(solution)/shard_map/ppermute | solution.py:38

commit v6 on v5

--- a/solution.py
+++ b/solution.py
@@ -285,14 +285,6 @@
     sent_out[:, width_out:] = split_rows(loss, rows)
 
 
-def total_kernel(scale, own, received, loss, there, there_near, out, loss_out):
-    width_out = own.shape[1]
-    out[...] = own[...] + received[:, :width_out].astype(f32)
-    near = jnp.sum(received[:, width_out:].astype(f32), axis=0, keepdims=True)
-    loss = (loss[...] + near) + (there[...] + there_near[...])
-    loss_out[...] = loss[:, 0:1] * scale
-
-
 def body(
     image_features, text_features, image_gain, text_gain, image_proj, text_proj, pair, logit_scale
 ):
@@ -489,14 +481,10 @@
         name="halve",
     )(kept, exchange(sent, "dp", 1), loss)
     there, there_near = cross_exchange(loss, 0), cross_exchange(loss, 1)
-    grads, loss = pl.pallas_call(
-        functools.partial(total_kernel, 1.0 / (2.0 * owners * rows)),
-        out_shape=[shape((span, width_out), f32), shape((1, 1), f32)],
-        in_specs=[VMEM] * 5,
-        out_specs=[VMEM] * 2,
-        compiler_params=PARAMS,
-        name="total",
-    )(own, exchange(sent, "mp", 1), loss, there, there_near)
+    received = exchange(sent, "mp", 1)
+    grads = own + received[:, :width_out].astype(f32)
+    near_loss = jnp.sum(received[:, width_out:].astype(f32), axis=0, keepdims=True)
+    loss = ((loss + near_loss) + (there + there_near)) * (1.0 / (2.0 * owners * rows))
     return (grads[None, :, :], loss[0, 0])
 
 

time: 51.6 us -> 51.4 us (level)
  other arithmetic: 0.01 us -> 1.28 us
  waiting for transfers between devices: 19.6 us -> 18.8 us
  Pallas kernels: 4.9 us -> 4.16 us
    ppermute x4, waiting for transfers between devices: 6.71 us -> 3.71 us  [cross_exchange(): return lax.ppermute(shard, ('group', 'mp'), pairs)]
    ppermute x16, waiting for transfers between devices: 12.9 us -> 15.1 us  [exchange(): lax.ppermute(shard, axis, [(i, i ^ distance) for i in range(lax.axis_size...]
    pallas_call x1 -> x0, Pallas kernels: 0.74 us -> none  [body(): pl.pallas_call(functools.partial(total_kernel, 1.0 / (2.0 * owners * rows...]
    broadcast_in_dim x0 -> x1, other arithmetic: none -> 0.73 us  [body(): return (grads[None, :, :], loss[0, 0])]
    mul x0 -> x1, other arithmetic: none -> 0.52 us  [body(): (loss + near_loss + (there + there_near)) * (1.0 / (2.0 * owners * rows))]
  transfers between devices with their start and end apart: 20 -> 20, of which waited for: 12 -> 13; matrix products, arithmetic and copies ran while one was open for 1% -> 2% of each run, Pallas kernels for 1% -> 1%
where the time goes in v6:
time: 51.4 us; the launch traced here: 51.2 us
  starting transfers between devices  25.1 us (49%)
  waiting for transfers between devices  18.8 us (37%)
  Pallas kernels  4.16 us (8%)
  between operations  1.4 us (3%)
  other arithmetic  1.28 us (2%)
    ppermute x16, starting transfers between devices, exchange(): lax.ppermute(shard, axis, [(i, i ^ distance) for i in range(lax.axis_size...  18.9 us
    ppermute x16, waiting for transfers between devices, exchange(): lax.ppermute(shard, axis, [(i, i ^ distance) for i in range(lax.axis_size...  15.1 us
    ppermute x4, starting transfers between devices, cross_exchange(): return lax.ppermute(shard, ('group', 'mp'), pairs)  6.24 us
    ppermute x4, waiting for transfers between devices, cross_exchange(): return lax.ppermute(shard, ('group', 'mp'), pairs)  3.71 us
    pallas_call x1, Pallas kernels, project(): pl.pallas_call(functools.partial(project_kernel, shards), out_shape=[shap...  2.22 us
  transfers between devices with their start and end apart: 20, of which 13 were waited for; matrix products, arithmetic and copies ran while one was open for 2% of the time, Pallas kernels for 1%

profile of v6, /device:TPU:0, one launch (start us, length us, event | category | flops | bytes accessed | tf_op | source)
XLA Modules:
  0.0 51.2 jit_solution(2047529378305384082)
XLA Ops:
  0.6 0.0 copy-start
  0.6 2.2 %conditional.1 = ((f32[64,1024]{1,0:T(8,128)S(1)}, f32[64,1024]{1,0:T(8,128)S(1)}, bf16[64,1024]{1,0:T(8,128)(2,1)S(1)}, bf16[64,1024]{1,0:T(8,128)(2,1)S(1)}, f32[1,16,128]{2,1,0:T(8,128)S(1)})) conditional(s32[]{:T(128)} %convert_element_type.9, (bf16[256,1536]{1,0:T(8,128)(2,1)}, f32[1536]{0:T(1024)}, bf16[1536,1024]{1,0:T(8,128)(2,1)}) %tuple.14, ...), branch_computations={%region_0.0_spmd, %region_1.0_spmd} | conditional | bytes 8 | solution.py:328
  0.7 2.2 %project.3 = (f32[64,1024]{1,0:T(8,128)S(1)}, f32[64,1024]{1,0:T(8,128)S(1)}, bf16[64,1024]{1,0:T(8,128)(2,1)S(1)}, bf16[64,1024]{1,0:T(8,128)(2,1)S(1)}, f32[1,16,128]{2,1,0:T(8,128)S(1)}) custom-call(bf16[256,256]{1,0:T(8,128)(2,1)} %get-tuple-element.61.x_hbm, f32[256]{0:T(256)} %get-tuple-element.62.gain, bf16[256,1024]{1,0:T(8,128)(2,1)} %get-tuple-element.63.p_hbm), custom_call_target="tpu_custom_call" | custom-call | tf_op jit(solution)/shard_map/cond/branch_1_fun/project/pallas_call | solution.py:306
  2.9 3.1 %collective-permute-start = (bf16[64,1024]{1,0:T(8,128)(2,1)S(1)}, bf16[64,1024]{1,0:T(8,128)(2,1)S(1)}, u32[]{:S(2)}, u32[]{:S(2)}) collective-permute-start(bf16[64,1024]{1,0:T(8,128)(2,1)S(1)} %get-tuple-element.38), channel_id=1, source_target_pairs={{0,1},{1,0},{2,3},{3,2},{4,5},{5,4},{6,7},{7,6},{8,9},{9,8},{10,11... | collective-permute-start | bytes 393224 | tf_op jit(solution)/shard_map/ppermute | solution.py:28
  6.0 0.1 collective-permute-start.3
  6.1 3.5 %collective-permute-done.received = bf16[64,1024]{1,0:T(8,128)(2,1)S(1)} collective-permute-done((bf16[64,1024]{1,0:T(8,128)(2,1)S(1)}, bf16[64,1024]{1,0:T(8,128)(2,1)S(1)}, u32[]{:S(2)}, u32[]{:S(2)}) %collective-permute-start) | collective-permute-done | bytes 131104 | tf_op jit(solution)/shard_map/ppermute | solution.py:28
  9.6 2.8 %collective-permute-start.1 = (bf16[64,1024]{1,0:T(8,128)(2,1)S(1)}, bf16[64,1024]{1,0:T(8,128)(2,1)S(1)}, u32[]{:S(2)}, u32[]{:S(2)}) collective-permute-start(bf16[64,1024]{1,0:T(8,128)(2,1)S(1)} %get-tuple-element.40), channel_id=1, source_target_pairs={{0,2},{1,3},{2,0},{3,1},{4,6},{5,7},{6,4},{7,5},{8,10},{9,11},{10,... | collective-permute-start | bytes 393224 | tf_op jit(solution)/shard_map/ppermute | solution.py:28
  12.4 1.6 %collective-permute-start.2 = (bf16[64,1024]{1,0:T(8,128)(2,1)S(1)}, bf16[64,1024]{1,0:T(8,128)(2,1)S(1)}, u32[]{:S(2)}, u32[]{:S(2)}) collective-permute-start(bf16[64,1024]{1,0:T(8,128)(2,1)S(1)} %get-tuple-element.41), channel_id=1, source_target_pairs={{0,1},{1,0},{2,3},{3,2},{4,5},{5,4},{6,7},{7,6},{8,9},{9,8},{10,11... | collective-permute-start | bytes 393224 | tf_op jit(solution)/shard_map/ppermute | solution.py:28
  14.0 0.0 copy-done
  14.0 0.1 reshape.20
  14.1 0.0 collective-permute-done.3.note_other
  14.1 0.4 collective-permute-start.4
  14.5 0.1 reshape.22
  14.6 0.1 reshape.23.rest_5_.right
  14.7 0.1 reshape.24.rest_4_.left
  14.8 4.0 %collective-permute-done.4.rest_3_ = f32[2,16,128]{2,1,0:T(8,128)S(1)} collective-permute-done((f32[2,16,128]{2,1,0:T(8,128)S(1)}, f32[2,16,128]{2,1,0:T(8,128)S(1)}, u32[]{:S(2)}, u32[]{:S(2)}) %collective-permute-start.4) | collective-permute-done | bytes 16416 | tf_op jit(solution)/shard_map/ppermute | solution.py:28
  18.8 0.0 collective-permute-done.1.rest_0_
  18.8 0.0 collective-permute-done.2.rest_1_
  18.8 0.4 finish.1.rest_4_
  19.3 2.1 %collective-permute-start.9 = (bf16[64,1024]{1,0:T(8,128)(2,1)S(1)}, bf16[64,1024]{1,0:T(8,128)(2,1)S(1)}, u32[]{:S(2)}, u32[]{:S(2)}) collective-permute-start(bf16[64,1024]{1,0:T(8,128)(2,1)S(1)} %finish.1.rest_4_), channel_id=1, source_target_pairs={{0,2},{1,3},{2,0},{3,1},{4,6},{5,7},{6,4},{7,5},{8,10},{9,11},{10,... | collective-permute-start | bytes 393224 | tf_op jit(solution)/shard_map/ppermute | solution.py:28
  21.4 4.0 %collective-permute-start.6 = (bf16[64,1024]{1,0:T(8,128)(2,1)S(1)}, bf16[64,1024]{1,0:T(8,128)(2,1)S(1)}, u32[]{:S(2)}, u32[]{:S(2)}) collective-permute-start(bf16[64,1024]{1,0:T(8,128)(2,1)S(1)} %finish.1.rest_4_), channel_id=1, source_target_pairs={{0,17},{1,16},{2,19},{3,18},{16,1},{17,0},{18,3},{19,2},{4,21},{5,... | collective-permute-start | bytes 393224 | tf_op jit(solution)/shard_map/ppermute | solution.py:38
  25.3 0.0 collective-permute-start.5
  25.4 1.5 %collective-permute-start.10 = (bf16[64,1024]{1,0:T(8,128)(2,1)S(1)}, bf16[64,1024]{1,0:T(8,128)(2,1)S(1)}, u32[]{:S(2)}, u32[]{:S(2)}) collective-permute-start(bf16[64,1024]{1,0:T(8,128)(2,1)S(1)} %finish.1.rest_4_), channel_id=1, source_target_pairs={{0,8},{4,12},{8,0},{12,4},{1,9},{5,13},{9,1},{13,5},{2,10},{6,14},... | collective-permute-start | bytes 393224 | tf_op jit(solution)/shard_map/ppermute | solution.py:28
  26.9 0.0 collective-permute-done.9.rest_5_
  26.9 1.1 %collective-permute-start.11 = (bf16[64,1024]{1,0:T(8,128)(2,1)S(1)}, bf16[64,1024]{1,0:T(8,128)(2,1)S(1)}, u32[]{:S(2)}, u32[]{:S(2)}) collective-permute-start(bf16[64,1024]{1,0:T(8,128)(2,1)S(1)} %collective-permute-done.9.rest_5_), channel_id=1, source_target_pairs={{0,8},{4,12},{8,0},{12,4},{1,9},{5,13},{9,1},{13,5},{2,10},{6,14},... | collective-permute-start | bytes 393224 | tf_op jit(solution)/shard_map/ppermute | solution.py:28
  28.0 1.3 %collective-permute-done.6.rest_1_ = bf16[64,1024]{1,0:T(8,128)(2,1)S(1)} collective-permute-done((bf16[64,1024]{1,0:T(8,128)(2,1)S(1)}, bf16[64,1024]{1,0:T(8,128)(2,1)S(1)}, u32[]{:S(2)}, u32[]{:S(2)}) %collective-permute-start.6) | collective-permute-done | bytes 131104 | tf_op jit(solution)/shard_map/ppermute | solution.py:38
  29.3 0.0 collective-permute-start.8
  29.3 1.5 %collective-permute-done.5.rest_0_ = bf16[64,1024]{1,0:T(8,128)(2,1)S(1)} collective-permute-done((bf16[64,1024]{1,0:T(8,128)(2,1)S(1)}, bf16[64,1024]{1,0:T(8,128)(2,1)S(1)}, u32[]{:S(2)}, u32[]{:S(2)}) %collective-permute-start.5) | collective-permute-done | bytes 131104 | tf_op jit(solution)/shard_map/ppermute | solution.py:38
  30.9 0.0 collective-permute-start.7
  31.5 0.0 collective-permute-done.10.rest_6_
  31.5 0.6 %collective-permute-done.11.rest_7_ = bf16[64,1024]{1,0:T(8,128)(2,1)S(1)} collective-permute-done((bf16[64,1024]{1,0:T(8,128)(2,1)S(1)}, bf16[64,1024]{1,0:T(8,128)(2,1)S(1)}, u32[]{:S(2)}, u32[]{:S(2)}) %collective-permute-start.11) | collective-permute-done | bytes 131104 | tf_op jit(solution)/shard_map/ppermute | solution.py:28
  32.1 0.0 collective-permute-done.8.rest_3_
  32.1 0.1 collective-permute-done.7.rest_2_
  32.2 0.5 scores.1
  32.7 1.6 %collective-permute-start.12 = (f32[8,256]{1,0:T(8,128)S(1)}, f32[8,256]{1,0:T(8,128)S(1)}, u32[]{:S(2)}, u32[]{:S(2)}) collective-permute-start(f32[8,256]{1,0:T(8,128)S(1)} %get-tuple-element.45.column), channel_id=1, source_target_pairs={{0,8},{4,12},{8,0},{12,4},{1,9},{5,13},{9,1},{13,5},{2,10},{6,14},... | collective-permute-start | bytes 24584 | tf_op jit(solution)/shard_map/ppermute | solution.py:28
  34.3 0.2 rows.1.row
  34.5 0.0 collective-permute-start.13
  34.6 1.1 %collective-permute-done.13.row_other = f32[1,256]{1,0:T(1,128)S(1)} collective-permute-done((f32[1,256]{1,0:T(1,128)S(1)}, f32[1,256]{1,0:T(1,128)S(1)}, u32[]{:S(2)}, u32[]{:S(2)}) %collective-permute-start.13) | collective-permute-done | bytes 1056 | tf_op jit(solution)/shard_map/ppermute | solution.py:28
  35.7 0.6 %collective-permute-start.15 = (f32[8,256]{1,0:T(8,128)S(1)}, f32[8,256]{1,0:T(8,128)S(1)}, u32[]{:S(2)}, u32[]{:S(2)}) collective-permute-start(f32[8,256]{1,0:T(8,128)S(1)} %merge.2.after.rest_0_), channel_id=1, source_target_pairs={{0,1},{1,0},{2,3},{3,2},{4,5},{5,4},{6,7},{7,6},{8,9},{9,8},{10,11... | collective-permute-start | bytes 24584 | tf_op jit(solution)/shard_map/ppermute | solution.py:28
  36.3 0.1 collective-permute-done.12.column_other
  36.4 2.4 %collective-permute-start.14 = (f32[2,256]{1,0:T(2,128)S(1)}, f32[2,256]{1,0:T(2,128)S(1)}, u32[]{:S(2)}, u32[]{:S(2)}) collective-permute-start(f32[2,256]{1,0:T(2,128)S(1)} %merge.3.column), channel_id=1, source_target_pairs={{0,2},{1,3},{2,0},{3,1},{4,6},{5,7},{6,4},{7,5},{8,10},{9,11},{10,... | collective-permute-start | bytes 6152 | tf_op jit(solution)/shard_map/ppermute | solution.py:28
  38.8 0.6 %collective-permute-done.15.rest_1_ = f32[8,256]{1,0:T(8,128)S(1)} collective-permute-done((f32[8,256]{1,0:T(8,128)S(1)}, f32[8,256]{1,0:T(8,128)S(1)}, u32[]{:S(2)}, u32[]{:S(2)}) %collective-permute-start.15) | collective-permute-done | bytes 8224 | tf_op jit(solution)/shard_map/ppermute | solution.py:28
  39.4 1.6 %collective-permute-done.14.column_other = f32[2,256]{1,0:T(2,128)S(1)} collective-permute-done((f32[2,256]{1,0:T(2,128)S(1)}, f32[2,256]{1,0:T(2,128)S(1)}, u32[]{:S(2)}, u32[]{:S(2)}) %collective-permute-start.14) | collective-permute-done | bytes 2080 | tf_op jit(solution)/shard_map/ppermute | solution.py:28
  41.0 0.4 grads.1
  41.4 0.1 collective-permute-start.16
  41.5 0.2 kept.1
  41.7 1.3 %collective-permute-done.16.received = bf16[128,1152]{1,0:T(8,128)(2,1)S(1)} collective-permute-done((bf16[128,1152]{1,0:T(8,128)(2,1)S(1)}, bf16[128,1152]{1,0:T(8,128)(2,1)S(1)}, u32[]{:S(2)}, u32[]{:S(2)}) %collective-permute-start.16) | collective-permute-done | bytes 294944 | tf_op jit(solution)/shard_map/ppermute | solution.py:28
  43.1 0.1 halve.1
  43.1 1.4 %collective-permute-start.17 = (bf16[64,1152]{1,0:T(8,128)(2,1)S(1)}, bf16[64,1152]{1,0:T(8,128)(2,1)S(1)}, u32[]{:S(2)}, u32[]{:S(2)}) collective-permute-start(bf16[64,1152]{1,0:T(8,128)(2,1)S(1)} %get-tuple-element.50), channel_id=1, source_target_pairs={{0,1},{1,0},{2,3},{3,2},{4,5},{5,4},{6,7},{7,6},{8,9},{9,8},{10,11... | collective-permute-start | bytes 442376 | tf_op jit(solution)/shard_map/ppermute | solution.py:28
  44.6 2.3 %collective-permute-start.19 = (f32[1,128]{1,0:T(1,128)S(1)}, f32[1,128]{1,0:T(1,128)S(1)}, u32[]{:S(2)}, u32[]{:S(2)}) collective-permute-start(f32[1,128]{1,0:T(1,128)S(1)} %get-tuple-element.51), channel_id=1, source_target_pairs={{0,17},{1,16},{2,19},{3,18},{16,1},{17,0},{18,3},{19,2},{4,21},{5,... | collective-permute-start | bytes 1544 | tf_op jit(solution)/shard_map/ppermute | solution.py:38
  46.9 0.0 collective-permute-start.18
  46.9 2.2 %collective-permute-done.17 = bf16[64,1152]{1,0:T(8,128)(2,1)S(1)} collective-permute-done((bf16[64,1152]{1,0:T(8,128)(2,1)S(1)}, bf16[64,1152]{1,0:T(8,128)(2,1)S(1)}, u32[]{:S(2)}, u32[]{:S(2)}) %collective-permute-start.17) | collective-permute-done | bytes 147488 | tf_op jit(solution)/shard_map/ppermute | solution.py:28
  49.1 0.7 %add_bitcast_fusion = f32[1,64,1024]{2,1,0:T(8,128)} fusion(f32[64,1024]{1,0:T(8,128)S(1)} %get-tuple-element.49, bf16[64,1152]{1,0:T(8,128)(2,1)S(1)} %collective-permute-done.17), kind=kLoop, calls=%fused_computation | loop fusion | flops 131072 | bytes 655360 | tf_op jit(solution)/shard_map/broadcast_in_dim | solution.py:488
  49.9 0.8 %collective-permute-done.19 = f32[1,128]{1,0:T(1,128)S(1)} collective-permute-done((f32[1,128]{1,0:T(1,128)S(1)}, f32[1,128]{1,0:T(1,128)S(1)}, u32[]{:S(2)}, u32[]{:S(2)}) %collective-permute-start.19) | collective-permute-done | bytes 544 | tf_op jit(solution)/shard_map/ppermute | solution.py:38
  50.7 0.0 collective-permute-done.18
  50.7 0.5 %fusion.1 = f32[1,128]{1,0:T(1,128)} fusion(f32[1,128]{1,0:T(1,128)S(1)} %get-tuple-element.51, f32[128]{0:T(128)S(1)} %convert_reduce_fusion, f32[1,128]{1,0:T(1,128)S(1)} %collective-permute-done.18, f32[1,128]{1,0:T(1,128)S(1)} %collective-permute-done.19), kind=kLoop, calls=%fused_computation.7 | loop fusion | flops 512 | bytes 2560 | tf_op jit(solution)/shard_map/mul | solution.py:487
  (8 shorter events, 0.1 us)
Async XLA Ops:
  0.6 13.4 %copy-start = (s32[1024]{0:T(1024)S(1)}, s32[1024]{0:T(1024)}, u32[]{:S(2)}) copy-start(s32[1024]{0:T(1024)} %param.16) | copy-start | bytes 12292
  2.9 6.7 %collective-permute-start = (bf16[64,1024]{1,0:T(8,128)(2,1)S(1)}, bf16[64,1024]{1,0:T(8,128)(2,1)S(1)}, u32[]{:S(2)}, u32[]{:S(2)}) collective-permute-start(bf16[64,1024]{1,0:T(8,128)(2,1)S(1)} %get-tuple-element.38), channel_id=1, source_target_pairs={{0,1},{1,0},{2,3},{3,2},{4,5},{5,4},{6,7},{7,6},{8,9},{9,8},{10,11... | collective-permute-start | bytes 393224 | tf_op jit(solution)/shard_map/ppermute | solution.py:28
  6.0 8.1 %collective-permute-start.3 = (f32[1,16,128]{2,1,0:T(8,128)S(1)}, f32[1,16,128]{2,1,0:T(8,128)S(1)}, u32[]{:S(2)}, u32[]{:S(2)}) collective-permute-start(f32[1,16,128]{2,1,0:T(8,128)S(1)} %get-tuple-element.42.note), channel_id=1, source_target_pairs={{0,1},{1,0},{2,3},{3,2},{4,5},{5,4},{6,7},{7,6},{8,9},{9,8},{10,11... | collective-permute-start | bytes 24584 | tf_op jit(solution)/shard_map/ppermute | solution.py:28
  9.6 9.2 %collective-permute-start.1 = (bf16[64,1024]{1,0:T(8,128)(2,1)S(1)}, bf16[64,1024]{1,0:T(8,128)(2,1)S(1)}, u32[]{:S(2)}, u32[]{:S(2)}) collective-permute-start(bf16[64,1024]{1,0:T(8,128)(2,1)S(1)} %get-tuple-element.40), channel_id=1, source_target_pairs={{0,2},{1,3},{2,0},{3,1},{4,6},{5,7},{6,4},{7,5},{8,10},{9,11},{10,... | collective-permute-start | bytes 393224 | tf_op jit(solution)/shard_map/ppermute | solution.py:28
  12.4 6.4 %collective-permute-start.2 = (bf16[64,1024]{1,0:T(8,128)(2,1)S(1)}, bf16[64,1024]{1,0:T(8,128)(2,1)S(1)}, u32[]{:S(2)}, u32[]{:S(2)}) collective-permute-start(bf16[64,1024]{1,0:T(8,128)(2,1)S(1)} %get-tuple-element.41), channel_id=1, source_target_pairs={{0,1},{1,0},{2,3},{3,2},{4,5},{5,4},{6,7},{7,6},{8,9},{9,8},{10,11... | collective-permute-start | bytes 393224 | tf_op jit(solution)/shard_map/ppermute | solution.py:28
  14.1 4.7 %collective-permute-start.4 = (f32[2,16,128]{2,1,0:T(8,128)S(1)}, f32[2,16,128]{2,1,0:T(8,128)S(1)}, u32[]{:S(2)}, u32[]{:S(2)}) collective-permute-start(f32[2,16,128]{2,1,0:T(8,128)S(1)} %both.1.rest_2_), channel_id=1, source_target_pairs={{0,2},{1,3},{2,0},{3,1},{4,6},{5,7},{6,4},{7,5},{8,10},{9,11},{10,... | collective-permute-start | bytes 49160 | tf_op jit(solution)/shard_map/ppermute | solution.py:28
  19.3 7.6 %collective-permute-start.9 = (bf16[64,1024]{1,0:T(8,128)(2,1)S(1)}, bf16[64,1024]{1,0:T(8,128)(2,1)S(1)}, u32[]{:S(2)}, u32[]{:S(2)}) collective-permute-start(bf16[64,1024]{1,0:T(8,128)(2,1)S(1)} %finish.1.rest_4_), channel_id=1, source_target_pairs={{0,2},{1,3},{2,0},{3,1},{4,6},{5,7},{6,4},{7,5},{8,10},{9,11},{10,... | collective-permute-start | bytes 393224 | tf_op jit(solution)/shard_map/ppermute | solution.py:28
  21.4 8.0 %collective-permute-start.6 = (bf16[64,1024]{1,0:T(8,128)(2,1)S(1)}, bf16[64,1024]{1,0:T(8,128)(2,1)S(1)}, u32[]{:S(2)}, u32[]{:S(2)}) collective-permute-start(bf16[64,1024]{1,0:T(8,128)(2,1)S(1)} %finish.1.rest_4_), channel_id=1, source_target_pairs={{0,17},{1,16},{2,19},{3,18},{16,1},{17,0},{18,3},{19,2},{4,21},{5,... | collective-permute-start | bytes 393224 | tf_op jit(solution)/shard_map/ppermute | solution.py:38
  25.3 5.5 %collective-permute-start.5 = (bf16[64,1024]{1,0:T(8,128)(2,1)S(1)}, bf16[64,1024]{1,0:T(8,128)(2,1)S(1)}, u32[]{:S(2)}, u32[]{:S(2)}) collective-permute-start(bf16[64,1024]{1,0:T(8,128)(2,1)S(1)} %finish.1.rest_4_), channel_id=1, source_target_pairs={{0,16},{1,17},{2,18},{3,19},{16,0},{17,1},{18,2},{19,3},{4,20},{5,... | collective-permute-start | bytes 393224 | tf_op jit(solution)/shard_map/ppermute | solution.py:38
  25.4 6.2 %collective-permute-start.10 = (bf16[64,1024]{1,0:T(8,128)(2,1)S(1)}, bf16[64,1024]{1,0:T(8,128)(2,1)S(1)}, u32[]{:S(2)}, u32[]{:S(2)}) collective-permute-start(bf16[64,1024]{1,0:T(8,128)(2,1)S(1)} %finish.1.rest_4_), channel_id=1, source_target_pairs={{0,8},{4,12},{8,0},{12,4},{1,9},{5,13},{9,1},{13,5},{2,10},{6,14},... | collective-permute-start | bytes 393224 | tf_op jit(solution)/shard_map/ppermute | solution.py:28
  26.9 5.2 %collective-permute-start.11 = (bf16[64,1024]{1,0:T(8,128)(2,1)S(1)}, bf16[64,1024]{1,0:T(8,128)(2,1)S(1)}, u32[]{:S(2)}, u32[]{:S(2)}) collective-permute-start(bf16[64,1024]{1,0:T(8,128)(2,1)S(1)} %collective-permute-done.9.rest_5_), channel_id=1, source_target_pairs={{0,8},{4,12},{8,0},{12,4},{1,9},{5,13},{9,1},{13,5},{2,10},{6,14},... | collective-permute-start | bytes 393224 | tf_op jit(solution)/shard_map/ppermute | solution.py:28
  29.3 2.8 %collective-permute-start.8 = (bf16[64,1024]{1,0:T(8,128)(2,1)S(1)}, bf16[64,1024]{1,0:T(8,128)(2,1)S(1)}, u32[]{:S(2)}, u32[]{:S(2)}) collective-permute-start(bf16[64,1024]{1,0:T(8,128)(2,1)S(1)} %collective-permute-done.6.rest_1_), channel_id=1, source_target_pairs={{0,4},{4,0},{8,12},{12,8},{1,5},{5,1},{9,13},{13,9},{2,6},{6,2},{1... | collective-permute-start | bytes 393224 | tf_op jit(solution)/shard_map/ppermute | solution.py:28
  30.9 1.3 %collective-permute-start.7 = (bf16[64,1024]{1,0:T(8,128)(2,1)S(1)}, bf16[64,1024]{1,0:T(8,128)(2,1)S(1)}, u32[]{:S(2)}, u32[]{:S(2)}) collective-permute-start(bf16[64,1024]{1,0:T(8,128)(2,1)S(1)} %collective-permute-done.5.rest_0_), channel_id=1, source_target_pairs={{0,4},{4,0},{8,12},{12,8},{1,5},{5,1},{9,13},{13,9},{2,6},{6,2},{1... | collective-permute-start | bytes 393224 | tf_op jit(solution)/shard_map/ppermute | solution.py:28
  32.7 3.7 %collective-permute-start.12 = (f32[8,256]{1,0:T(8,128)S(1)}, f32[8,256]{1,0:T(8,128)S(1)}, u32[]{:S(2)}, u32[]{:S(2)}) collective-permute-start(f32[8,256]{1,0:T(8,128)S(1)} %get-tuple-element.45.column), channel_id=1, source_target_pairs={{0,8},{4,12},{8,0},{12,4},{1,9},{5,13},{9,1},{13,5},{2,10},{6,14},... | collective-permute-start | bytes 24584 | tf_op jit(solution)/shard_map/ppermute | solution.py:28
  34.5 1.2 %collective-permute-start.13 = (f32[1,256]{1,0:T(1,128)S(1)}, f32[1,256]{1,0:T(1,128)S(1)}, u32[]{:S(2)}, u32[]{:S(2)}) collective-permute-start(f32[1,256]{1,0:T(1,128)S(1)} %rows.1.row), channel_id=1, source_target_pairs={{0,4},{4,0},{8,12},{12,8},{1,5},{5,1},{9,13},{13,9},{2,6},{6,2},{1... | collective-permute-start | bytes 3080 | tf_op jit(solution)/shard_map/ppermute | solution.py:28
  35.7 3.7 %collective-permute-start.15 = (f32[8,256]{1,0:T(8,128)S(1)}, f32[8,256]{1,0:T(8,128)S(1)}, u32[]{:S(2)}, u32[]{:S(2)}) collective-permute-start(f32[8,256]{1,0:T(8,128)S(1)} %merge.2.after.rest_0_), channel_id=1, source_target_pairs={{0,1},{1,0},{2,3},{3,2},{4,5},{5,4},{6,7},{7,6},{8,9},{9,8},{10,11... | collective-permute-start | bytes 24584 | tf_op jit(solution)/shard_map/ppermute | solution.py:28
  36.4 4.5 %collective-permute-start.14 = (f32[2,256]{1,0:T(2,128)S(1)}, f32[2,256]{1,0:T(2,128)S(1)}, u32[]{:S(2)}, u32[]{:S(2)}) collective-permute-start(f32[2,256]{1,0:T(2,128)S(1)} %merge.3.column), channel_id=1, source_target_pairs={{0,2},{1,3},{2,0},{3,1},{4,6},{5,7},{6,4},{7,5},{8,10},{9,11},{10,... | collective-permute-start | bytes 6152 | tf_op jit(solution)/shard_map/ppermute | solution.py:28
  41.4 1.6 %collective-permute-start.16 = (bf16[128,1152]{1,0:T(8,128)(2,1)S(1)}, bf16[128,1152]{1,0:T(8,128)(2,1)S(1)}, u32[]{:S(2)}, u32[]{:S(2)}) collective-permute-start(bf16[128,1152]{1,0:T(8,128)(2,1)S(1)} %get-tuple-element.47), channel_id=1, source_target_pairs={{0,4},{4,0},{8,12},{12,8},{1,5},{5,1},{9,13},{13,9},{2,6},{6,2},{1... | collective-permute-start | bytes 884744 | tf_op jit(solution)/shard_map/ppermute | solution.py:28
  43.1 6.0 %collective-permute-start.17 = (bf16[64,1152]{1,0:T(8,128)(2,1)S(1)}, bf16[64,1152]{1,0:T(8,128)(2,1)S(1)}, u32[]{:S(2)}, u32[]{:S(2)}) collective-permute-start(bf16[64,1152]{1,0:T(8,128)(2,1)S(1)} %get-tuple-element.50), channel_id=1, source_target_pairs={{0,1},{1,0},{2,3},{3,2},{4,5},{5,4},{6,7},{7,6},{8,9},{9,8},{10,11... | collective-permute-start | bytes 442376 | tf_op jit(solution)/shard_map/ppermute | solution.py:28
  44.6 6.1 %collective-permute-start.19 = (f32[1,128]{1,0:T(1,128)S(1)}, f32[1,128]{1,0:T(1,128)S(1)}, u32[]{:S(2)}, u32[]{:S(2)}) collective-permute-start(f32[1,128]{1,0:T(1,128)S(1)} %get-tuple-element.51), channel_id=1, source_target_pairs={{0,17},{1,16},{2,19},{3,18},{16,1},{17,0},{18,3},{19,2},{4,21},{5,... | collective-permute-start | bytes 1544 | tf_op jit(solution)/shard_map/ppermute | solution.py:38
  46.9 3.8 %collective-permute-start.18 = (f32[1,128]{1,0:T(1,128)S(1)}, f32[1,128]{1,0:T(1,128)S(1)}, u32[]{:S(2)}, u32[]{:S(2)}) collective-permute-start(f32[1,128]{1,0:T(1,128)S(1)} %get-tuple-element.51), channel_id=1, source_target_pairs={{0,16},{1,17},{2,18},{3,19},{16,0},{17,1},{18,2},{19,3},{4,20},{5,... | collective-permute-start | bytes 1544 | tf_op jit(solution)/shard_map/ppermute | solution.py:38

commit v7 on v6

--- a/solution.py
+++ b/solution.py
@@ -65,7 +65,7 @@
 
 
 def project_kernel(shards, x_hbm, gain, p_hbm, *rest):
-    own_out, kept_out, near_out, far_out, note, x_buf, p_buf, scaled, total, sems = rest
+    own_out, kept_out, near_out, far_out, note, x_buf, p_buf, scaled, total, stat, sems = rest
     rows, width = x_buf.shape
     span = rows // shards
     width_out = total.shape[1]
@@ -87,19 +87,19 @@
         copies.append(copy)
     g = gain[...].reshape(1, width)
     scaled[rows:, :] = split_rows(g, 16)
-    packs = []
     lane = lax.broadcasted_iota(jnp.int32, (R_BLOCK, lanes), 1)
-    for c in range(X_CUTS):
-        x_copies[c].wait()
-        for r in range(c * some, (c + 1) * some, R_BLOCK):
-            at = slice(r, r + R_BLOCK)
+    for copy in x_copies:
+        copy.wait()
+    for k in range(shards):
+        for r in range(0, span, R_BLOCK):
+            at = pl.ds(pl.multiple_of((me ^ k) * span + r, R_BLOCK), R_BLOCK)
             values = x_buf[at, :].astype(f32)
             mean = jnp.sum(values, axis=1, keepdims=True) / width
             centred = values - mean
             spread = jnp.sum(centred * centred, axis=1, keepdims=True)
-            scaled[at, :] = (centred * g).astype(bf16)
-            packs.append(jnp.where(lane == 0, mean, jnp.where(lane == 1, spread, 0.0)))
-    stats = jnp.transpose(jnp.concatenate(packs, axis=0))
+            scaled[k * span + r : k * span + r + R_BLOCK, :] = (centred * g).astype(bf16)
+            stat[at, :] = jnp.where(lane == 0, mean, jnp.where(lane == 1, spread, 0.0))
+    stats = jnp.transpose(stat[...])
     height = width_out // lanes
     many = rows // lanes
     for j in range(many):
@@ -110,23 +110,22 @@
         copies[c].wait()
         at = slice(c * deep, (c + 1) * deep)
         product = jnp.dot(scaled[:, at], p_buf[at, :], preferred_element_type=f32)
-        if c == 0:
-            total[...] = product
-        else:
-            total[...] += product
-    offset = jnp.sum(total[rows:, :], axis=0, keepdims=True)
+        if c < cuts - 1:
+            total[...] = product if c == 0 else total[...] + product
+
+    def block(first, size):
+        at = slice(first, first + size)
+        return product[at] if cuts == 1 else total[at, :] + product[at]
+
+    for m in range(1, shards // 2):
+        at = slice((m - 1) * span, m * span)
+        far_out[at, :] = block((2 * m + 1) * span, span).astype(bf16)
+        kept_out[at, :] = block(2 * m * span, span)
+    near_out[...] = block(span, span).astype(bf16)
+    own_out[...] = block(0, span)
+    offset = jnp.sum(block(rows, 16), axis=0, keepdims=True)
     for j in range(height):
         note[0, j : j + 1, :] = offset[:, j * lanes : (j + 1) * lanes]
-
-    def block(distance):
-        return total[pl.ds(pl.multiple_of((me ^ distance) * span, span), span), :]
-
-    for m in range(1, shards // 2):
-        at = slice((m - 1) * span, m * span)
-        far_out[at, :] = block(2 * m + 1).astype(bf16)
-        kept_out[at, :] = block(2 * m)
-    near_out[...] = block(1).astype(bf16)
-    own_out[...] = block(0)
 
 
 def pair_kernel(kept, received, near, *rest):
@@ -319,6 +318,7 @@
                 pltpu.VMEM((width, width_out), bf16),
                 pltpu.VMEM((rows + 16, width), bf16),
                 pltpu.VMEM((rows + 16, width_out), f32),
+                pltpu.VMEM((rows, lanes), f32),
                 pltpu.SemaphoreType.DMA((X_CUTS + max(1, width // P_STEP),)),
             ],
             compiler_params=PARAMS_P,

time: 51.4 us -> 51.4 us (level)
  no operation moved by 1% of the time
where the time goes in v7:
time: 51.4 us; the launch traced here: 51.2 us
  starting transfers between devices  25.2 us (49%)
  waiting for transfers between devices  18.8 us (37%)
  Pallas kernels  4.13 us (8%)
  between operations  1.4 us (3%)
  other arithmetic  1.28 us (2%)
    ppermute x16, starting transfers between devices, exchange(): lax.ppermute(shard, axis, [(i, i ^ distance) for i in range(lax.axis_size...  18.9 us
    ppermute x16, waiting for transfers between devices, exchange(): lax.ppermute(shard, axis, [(i, i ^ distance) for i in range(lax.axis_size...  15.1 us
    ppermute x4, starting transfers between devices, cross_exchange(): return lax.ppermute(shard, ('group', 'mp'), pairs)  6.25 us
    ppermute x4, waiting for transfers between devices, cross_exchange(): return lax.ppermute(shard, ('group', 'mp'), pairs)  3.71 us
    pallas_call x1, Pallas kernels, project(): pl.pallas_call(functools.partial(project_kernel, shards), out_shape=[shap...  2.19 us
  transfers between devices with their start and end apart: 20, of which 13 were waited for; matrix products, arithmetic and copies ran while one was open for 2% of the time, Pallas kernels for 1%

profile of v7, /device:TPU:0, one launch (start us, length us, event | category | flops | bytes accessed | tf_op | source)
XLA Modules:
  0.0 51.2 jit_solution(18433131177529829415)
XLA Ops:
  0.6 0.0 copy-start
  0.6 2.2 %conditional.1 = ((f32[64,1024]{1,0:T(8,128)S(1)}, f32[64,1024]{1,0:T(8,128)S(1)}, bf16[64,1024]{1,0:T(8,128)(2,1)S(1)}, bf16[64,1024]{1,0:T(8,128)(2,1)S(1)}, f32[1,16,128]{2,1,0:T(8,128)S(1)})) conditional(s32[]{:T(128)} %convert_element_type.9, (bf16[256,1536]{1,0:T(8,128)(2,1)}, f32[1536]{0:T(1024)}, bf16[1536,1024]{1,0:T(8,128)(2,1)}) %tuple.14, ...), branch_computations={%region_0.0_spmd, %region_1.0_spmd} | conditional | bytes 8 | solution.py:328
  0.7 2.2 %project.3 = (f32[64,1024]{1,0:T(8,128)S(1)}, f32[64,1024]{1,0:T(8,128)S(1)}, bf16[64,1024]{1,0:T(8,128)(2,1)S(1)}, bf16[64,1024]{1,0:T(8,128)(2,1)S(1)}, f32[1,16,128]{2,1,0:T(8,128)S(1)}) custom-call(bf16[256,256]{1,0:T(8,128)(2,1)} %get-tuple-element.61.x_hbm, f32[256]{0:T(256)} %get-tuple-element.62.gain, bf16[256,1024]{1,0:T(8,128)(2,1)} %get-tuple-element.63.p_hbm), custom_call_target="tpu_custom_call" | custom-call | tf_op jit(solution)/shard_map/cond/branch_1_fun/project/pallas_call | solution.py:305
  2.9 3.1 %collective-permute-start = (bf16[64,1024]{1,0:T(8,128)(2,1)S(1)}, bf16[64,1024]{1,0:T(8,128)(2,1)S(1)}, u32[]{:S(2)}, u32[]{:S(2)}) collective-permute-start(bf16[64,1024]{1,0:T(8,128)(2,1)S(1)} %get-tuple-element.38), channel_id=1, source_target_pairs={{0,1},{1,0},{2,3},{3,2},{4,5},{5,4},{6,7},{7,6},{8,9},{9,8},{10,11... | collective-permute-start | bytes 393224 | tf_op jit(solution)/shard_map/ppermute | solution.py:28
  6.0 0.1 collective-permute-start.3
  6.0 3.5 %collective-permute-done.received = bf16[64,1024]{1,0:T(8,128)(2,1)S(1)} collective-permute-done((bf16[64,1024]{1,0:T(8,128)(2,1)S(1)}, bf16[64,1024]{1,0:T(8,128)(2,1)S(1)}, u32[]{:S(2)}, u32[]{:S(2)}) %collective-permute-start) | collective-permute-done | bytes 131104 | tf_op jit(solution)/shard_map/ppermute | solution.py:28
  9.6 2.8 %collective-permute-start.1 = (bf16[64,1024]{1,0:T(8,128)(2,1)S(1)}, bf16[64,1024]{1,0:T(8,128)(2,1)S(1)}, u32[]{:S(2)}, u32[]{:S(2)}) collective-permute-start(bf16[64,1024]{1,0:T(8,128)(2,1)S(1)} %get-tuple-element.40), channel_id=1, source_target_pairs={{0,2},{1,3},{2,0},{3,1},{4,6},{5,7},{6,4},{7,5},{8,10},{9,11},{10,... | collective-permute-start | bytes 393224 | tf_op jit(solution)/shard_map/ppermute | solution.py:28
  12.4 1.6 %collective-permute-start.2 = (bf16[64,1024]{1,0:T(8,128)(2,1)S(1)}, bf16[64,1024]{1,0:T(8,128)(2,1)S(1)}, u32[]{:S(2)}, u32[]{:S(2)}) collective-permute-start(bf16[64,1024]{1,0:T(8,128)(2,1)S(1)} %get-tuple-element.41), channel_id=1, source_target_pairs={{0,1},{1,0},{2,3},{3,2},{4,5},{5,4},{6,7},{7,6},{8,9},{9,8},{10,11... | collective-permute-start | bytes 393224 | tf_op jit(solution)/shard_map/ppermute | solution.py:28
  14.0 0.0 copy-done
  14.0 0.1 reshape.20
  14.1 0.0 collective-permute-done.3.note_other
  14.1 0.4 collective-permute-start.4
  14.5 0.1 reshape.22
  14.6 0.1 reshape.23.rest_5_.right
  14.7 0.1 reshape.24.rest_4_.left
  14.8 4.0 %collective-permute-done.4.rest_3_ = f32[2,16,128]{2,1,0:T(8,128)S(1)} collective-permute-done((f32[2,16,128]{2,1,0:T(8,128)S(1)}, f32[2,16,128]{2,1,0:T(8,128)S(1)}, u32[]{:S(2)}, u32[]{:S(2)}) %collective-permute-start.4) | collective-permute-done | bytes 16416 | tf_op jit(solution)/shard_map/ppermute | solution.py:28
  18.8 0.0 collective-permute-done.1.rest_0_
  18.8 0.0 collective-permute-done.2.rest_1_
  18.8 0.4 finish.1.rest_4_
  19.2 2.1 %collective-permute-start.9 = (bf16[64,1024]{1,0:T(8,128)(2,1)S(1)}, bf16[64,1024]{1,0:T(8,128)(2,1)S(1)}, u32[]{:S(2)}, u32[]{:S(2)}) collective-permute-start(bf16[64,1024]{1,0:T(8,128)(2,1)S(1)} %finish.1.rest_4_), channel_id=1, source_target_pairs={{0,2},{1,3},{2,0},{3,1},{4,6},{5,7},{6,4},{7,5},{8,10},{9,11},{10,... | collective-permute-start | bytes 393224 | tf_op jit(solution)/shard_map/ppermute | solution.py:28
  21.3 4.0 %collective-permute-start.6 = (bf16[64,1024]{1,0:T(8,128)(2,1)S(1)}, bf16[64,1024]{1,0:T(8,128)(2,1)S(1)}, u32[]{:S(2)}, u32[]{:S(2)}) collective-permute-start(bf16[64,1024]{1,0:T(8,128)(2,1)S(1)} %finish.1.rest_4_), channel_id=1, source_target_pairs={{0,17},{1,16},{2,19},{3,18},{16,1},{17,0},{18,3},{19,2},{4,21},{5,... | collective-permute-start | bytes 393224 | tf_op jit(solution)/shard_map/ppermute | solution.py:38
  25.3 0.0 collective-permute-start.5
  25.3 1.5 %collective-permute-start.10 = (bf16[64,1024]{1,0:T(8,128)(2,1)S(1)}, bf16[64,1024]{1,0:T(8,128)(2,1)S(1)}, u32[]{:S(2)}, u32[]{:S(2)}) collective-permute-start(bf16[64,1024]{1,0:T(8,128)(2,1)S(1)} %finish.1.rest_4_), channel_id=1, source_target_pairs={{0,8},{4,12},{8,0},{12,4},{1,9},{5,13},{9,1},{13,5},{2,10},{6,14},... | collective-permute-start | bytes 393224 | tf_op jit(solution)/shard_map/ppermute | solution.py:28
  26.8 0.0 collective-permute-done.9.rest_5_
  26.8 1.1 %collective-permute-start.11 = (bf16[64,1024]{1,0:T(8,128)(2,1)S(1)}, bf16[64,1024]{1,0:T(8,128)(2,1)S(1)}, u32[]{:S(2)}, u32[]{:S(2)}) collective-permute-start(bf16[64,1024]{1,0:T(8,128)(2,1)S(1)} %collective-permute-done.9.rest_5_), channel_id=1, source_target_pairs={{0,8},{4,12},{8,0},{12,4},{1,9},{5,13},{9,1},{13,5},{2,10},{6,14},... | collective-permute-start | bytes 393224 | tf_op jit(solution)/shard_map/ppermute | solution.py:28
  28.0 1.3 %collective-permute-done.6.rest_1_ = bf16[64,1024]{1,0:T(8,128)(2,1)S(1)} collective-permute-done((bf16[64,1024]{1,0:T(8,128)(2,1)S(1)}, bf16[64,1024]{1,0:T(8,128)(2,1)S(1)}, u32[]{:S(2)}, u32[]{:S(2)}) %collective-permute-start.6) | collective-permute-done | bytes 131104 | tf_op jit(solution)/shard_map/ppermute | solution.py:38
  29.3 0.0 collective-permute-start.8
  29.3 1.5 %collective-permute-done.5.rest_0_ = bf16[64,1024]{1,0:T(8,128)(2,1)S(1)} collective-permute-done((bf16[64,1024]{1,0:T(8,128)(2,1)S(1)}, bf16[64,1024]{1,0:T(8,128)(2,1)S(1)}, u32[]{:S(2)}, u32[]{:S(2)}) %collective-permute-start.5) | collective-permute-done | bytes 131104 | tf_op jit(solution)/shard_map/ppermute | solution.py:38
  30.8 0.0 collective-permute-start.7
  31.5 0.0 collective-permute-done.10.rest_6_
  31.5 0.6 %collective-permute-done.11.rest_7_ = bf16[64,1024]{1,0:T(8,128)(2,1)S(1)} collective-permute-done((bf16[64,1024]{1,0:T(8,128)(2,1)S(1)}, bf16[64,1024]{1,0:T(8,128)(2,1)S(1)}, u32[]{:S(2)}, u32[]{:S(2)}) %collective-permute-start.11) | collective-permute-done | bytes 131104 | tf_op jit(solution)/shard_map/ppermute | solution.py:28
  32.1 0.0 collective-permute-done.8.rest_3_
  32.1 0.1 collective-permute-done.7.rest_2_
  32.2 0.5 scores.1
  32.7 1.6 %collective-permute-start.12 = (f32[8,256]{1,0:T(8,128)S(1)}, f32[8,256]{1,0:T(8,128)S(1)}, u32[]{:S(2)}, u32[]{:S(2)}) collective-permute-start(f32[8,256]{1,0:T(8,128)S(1)} %get-tuple-element.45.column), channel_id=1, source_target_pairs={{0,8},{4,12},{8,0},{12,4},{1,9},{5,13},{9,1},{13,5},{2,10},{6,14},... | collective-permute-start | bytes 24584 | tf_op jit(solution)/shard_map/ppermute | solution.py:28
  34.3 0.2 rows.1.row
  34.5 0.0 collective-permute-start.13
  34.5 1.1 %collective-permute-done.13.row_other = f32[1,256]{1,0:T(1,128)S(1)} collective-permute-done((f32[1,256]{1,0:T(1,128)S(1)}, f32[1,256]{1,0:T(1,128)S(1)}, u32[]{:S(2)}, u32[]{:S(2)}) %collective-permute-start.13) | collective-permute-done | bytes 1056 | tf_op jit(solution)/shard_map/ppermute | solution.py:28
  35.7 0.6 %collective-permute-start.15 = (f32[8,256]{1,0:T(8,128)S(1)}, f32[8,256]{1,0:T(8,128)S(1)}, u32[]{:S(2)}, u32[]{:S(2)}) collective-permute-start(f32[8,256]{1,0:T(8,128)S(1)} %merge.2.after.rest_0_), channel_id=1, source_target_pairs={{0,1},{1,0},{2,3},{3,2},{4,5},{5,4},{6,7},{7,6},{8,9},{9,8},{10,11... | collective-permute-start | bytes 24584 | tf_op jit(solution)/shard_map/ppermute | solution.py:28
  36.3 0.1 collective-permute-done.12.column_other
  36.4 2.4 %collective-permute-start.14 = (f32[2,256]{1,0:T(2,128)S(1)}, f32[2,256]{1,0:T(2,128)S(1)}, u32[]{:S(2)}, u32[]{:S(2)}) collective-permute-start(f32[2,256]{1,0:T(2,128)S(1)} %merge.3.column), channel_id=1, source_target_pairs={{0,2},{1,3},{2,0},{3,1},{4,6},{5,7},{6,4},{7,5},{8,10},{9,11},{10,... | collective-permute-start | bytes 6152 | tf_op jit(solution)/shard_map/ppermute | solution.py:28
  38.8 0.6 %collective-permute-done.15.rest_1_ = f32[8,256]{1,0:T(8,128)S(1)} collective-permute-done((f32[8,256]{1,0:T(8,128)S(1)}, f32[8,256]{1,0:T(8,128)S(1)}, u32[]{:S(2)}, u32[]{:S(2)}) %collective-permute-start.15) | collective-permute-done | bytes 8224 | tf_op jit(solution)/shard_map/ppermute | solution.py:28
  39.4 1.5 %collective-permute-done.14.column_other = f32[2,256]{1,0:T(2,128)S(1)} collective-permute-done((f32[2,256]{1,0:T(2,128)S(1)}, f32[2,256]{1,0:T(2,128)S(1)}, u32[]{:S(2)}, u32[]{:S(2)}) %collective-permute-start.14) | collective-permute-done | bytes 2080 | tf_op jit(solution)/shard_map/ppermute | solution.py:28
  40.9 0.4 grads.1
  41.4 0.1 collective-permute-start.16
  41.5 0.2 kept.1
  41.7 1.3 %collective-permute-done.16.received = bf16[128,1152]{1,0:T(8,128)(2,1)S(1)} collective-permute-done((bf16[128,1152]{1,0:T(8,128)(2,1)S(1)}, bf16[128,1152]{1,0:T(8,128)(2,1)S(1)}, u32[]{:S(2)}, u32[]{:S(2)}) %collective-permute-start.16) | collective-permute-done | bytes 294944 | tf_op jit(solution)/shard_map/ppermute | solution.py:28
  43.0 0.1 halve.1
  43.1 1.5 %collective-permute-start.17 = (bf16[64,1152]{1,0:T(8,128)(2,1)S(1)}, bf16[64,1152]{1,0:T(8,128)(2,1)S(1)}, u32[]{:S(2)}, u32[]{:S(2)}) collective-permute-start(bf16[64,1152]{1,0:T(8,128)(2,1)S(1)} %get-tuple-element.50), channel_id=1, source_target_pairs={{0,1},{1,0},{2,3},{3,2},{4,5},{5,4},{6,7},{7,6},{8,9},{9,8},{10,11... | collective-permute-start | bytes 442376 | tf_op jit(solution)/shard_map/ppermute | solution.py:28
  44.6 2.3 %collective-permute-start.19 = (f32[1,128]{1,0:T(1,128)S(1)}, f32[1,128]{1,0:T(1,128)S(1)}, u32[]{:S(2)}, u32[]{:S(2)}) collective-permute-start(f32[1,128]{1,0:T(1,128)S(1)} %get-tuple-element.51), channel_id=1, source_target_pairs={{0,17},{1,16},{2,19},{3,18},{16,1},{17,0},{18,3},{19,2},{4,21},{5,... | collective-permute-start | bytes 1544 | tf_op jit(solution)/shard_map/ppermute | solution.py:38
  46.8 0.0 collective-permute-start.18
  46.8 2.2 %collective-permute-done.17 = bf16[64,1152]{1,0:T(8,128)(2,1)S(1)} collective-permute-done((bf16[64,1152]{1,0:T(8,128)(2,1)S(1)}, bf16[64,1152]{1,0:T(8,128)(2,1)S(1)}, u32[]{:S(2)}, u32[]{:S(2)}) %collective-permute-start.17) | collective-permute-done | bytes 147488 | tf_op jit(solution)/shard_map/ppermute | solution.py:28
  49.1 0.7 %add_bitcast_fusion = f32[1,64,1024]{2,1,0:T(8,128)} fusion(f32[64,1024]{1,0:T(8,128)S(1)} %get-tuple-element.49, bf16[64,1152]{1,0:T(8,128)(2,1)S(1)} %collective-permute-done.17), kind=kLoop, calls=%fused_computation | loop fusion | flops 131072 | bytes 655360 | tf_op jit(solution)/shard_map/broadcast_in_dim | solution.py:488
  49.8 0.9 %collective-permute-done.19 = f32[1,128]{1,0:T(1,128)S(1)} collective-permute-done((f32[1,128]{1,0:T(1,128)S(1)}, f32[1,128]{1,0:T(1,128)S(1)}, u32[]{:S(2)}, u32[]{:S(2)}) %collective-permute-start.19) | collective-permute-done | bytes 544 | tf_op jit(solution)/shard_map/ppermute | solution.py:38
  50.7 0.0 collective-permute-done.18
  50.7 0.5 %fusion.1 = f32[1,128]{1,0:T(1,128)} fusion(f32[1,128]{1,0:T(1,128)S(1)} %get-tuple-element.51, f32[128]{0:T(128)S(1)} %convert_reduce_fusion, f32[1,128]{1,0:T(1,128)S(1)} %collective-permute-done.18, f32[1,128]{1,0:T(1,128)S(1)} %collective-permute-done.19), kind=kLoop, calls=%fused_computation.7 | loop fusion | flops 512 | bytes 2560 | tf_op jit(solution)/shard_map/mul | solution.py:487
  (8 shorter events, 0.1 us)
Async XLA Ops:
  0.6 13.3 %copy-start = (s32[1024]{0:T(1024)S(1)}, s32[1024]{0:T(1024)}, u32[]{:S(2)}) copy-start(s32[1024]{0:T(1024)} %param.16) | copy-start | bytes 12292
  2.9 6.7 %collective-permute-start = (bf16[64,1024]{1,0:T(8,128)(2,1)S(1)}, bf16[64,1024]{1,0:T(8,128)(2,1)S(1)}, u32[]{:S(2)}, u32[]{:S(2)}) collective-permute-start(bf16[64,1024]{1,0:T(8,128)(2,1)S(1)} %get-tuple-element.38), channel_id=1, source_target_pairs={{0,1},{1,0},{2,3},{3,2},{4,5},{5,4},{6,7},{7,6},{8,9},{9,8},{10,11... | collective-permute-start | bytes 393224 | tf_op jit(solution)/shard_map/ppermute | solution.py:28
  6.0 8.1 %collective-permute-start.3 = (f32[1,16,128]{2,1,0:T(8,128)S(1)}, f32[1,16,128]{2,1,0:T(8,128)S(1)}, u32[]{:S(2)}, u32[]{:S(2)}) collective-permute-start(f32[1,16,128]{2,1,0:T(8,128)S(1)} %get-tuple-element.42.note), channel_id=1, source_target_pairs={{0,1},{1,0},{2,3},{3,2},{4,5},{5,4},{6,7},{7,6},{8,9},{9,8},{10,11... | collective-permute-start | bytes 24584 | tf_op jit(solution)/shard_map/ppermute | solution.py:28
  9.6 9.2 %collective-permute-start.1 = (bf16[64,1024]{1,0:T(8,128)(2,1)S(1)}, bf16[64,1024]{1,0:T(8,128)(2,1)S(1)}, u32[]{:S(2)}, u32[]{:S(2)}) collective-permute-start(bf16[64,1024]{1,0:T(8,128)(2,1)S(1)} %get-tuple-element.40), channel_id=1, source_target_pairs={{0,2},{1,3},{2,0},{3,1},{4,6},{5,7},{6,4},{7,5},{8,10},{9,11},{10,... | collective-permute-start | bytes 393224 | tf_op jit(solution)/shard_map/ppermute | solution.py:28
  12.4 6.4 %collective-permute-start.2 = (bf16[64,1024]{1,0:T(8,128)(2,1)S(1)}, bf16[64,1024]{1,0:T(8,128)(2,1)S(1)}, u32[]{:S(2)}, u32[]{:S(2)}) collective-permute-start(bf16[64,1024]{1,0:T(8,128)(2,1)S(1)} %get-tuple-element.41), channel_id=1, source_target_pairs={{0,1},{1,0},{2,3},{3,2},{4,5},{5,4},{6,7},{7,6},{8,9},{9,8},{10,11... | collective-permute-start | bytes 393224 | tf_op jit(solution)/shard_map/ppermute | solution.py:28
  14.1 4.7 %collective-permute-start.4 = (f32[2,16,128]{2,1,0:T(8,128)S(1)}, f32[2,16,128]{2,1,0:T(8,128)S(1)}, u32[]{:S(2)}, u32[]{:S(2)}) collective-permute-start(f32[2,16,128]{2,1,0:T(8,128)S(1)} %both.1.rest_2_), channel_id=1, source_target_pairs={{0,2},{1,3},{2,0},{3,1},{4,6},{5,7},{6,4},{7,5},{8,10},{9,11},{10,... | collective-permute-start | bytes 49160 | tf_op jit(solution)/shard_map/ppermute | solution.py:28
  19.2 7.6 %collective-permute-start.9 = (bf16[64,1024]{1,0:T(8,128)(2,1)S(1)}, bf16[64,1024]{1,0:T(8,128)(2,1)S(1)}, u32[]{:S(2)}, u32[]{:S(2)}) collective-permute-start(bf16[64,1024]{1,0:T(8,128)(2,1)S(1)} %finish.1.rest_4_), channel_id=1, source_target_pairs={{0,2},{1,3},{2,0},{3,1},{4,6},{5,7},{6,4},{7,5},{8,10},{9,11},{10,... | collective-permute-start | bytes 393224 | tf_op jit(solution)/shard_map/ppermute | solution.py:28
  21.3 8.0 %collective-permute-start.6 = (bf16[64,1024]{1,0:T(8,128)(2,1)S(1)}, bf16[64,1024]{1,0:T(8,128)(2,1)S(1)}, u32[]{:S(2)}, u32[]{:S(2)}) collective-permute-start(bf16[64,1024]{1,0:T(8,128)(2,1)S(1)} %finish.1.rest_4_), channel_id=1, source_target_pairs={{0,17},{1,16},{2,19},{3,18},{16,1},{17,0},{18,3},{19,2},{4,21},{5,... | collective-permute-start | bytes 393224 | tf_op jit(solution)/shard_map/ppermute | solution.py:38
  25.3 5.5 %collective-permute-start.5 = (bf16[64,1024]{1,0:T(8,128)(2,1)S(1)}, bf16[64,1024]{1,0:T(8,128)(2,1)S(1)}, u32[]{:S(2)}, u32[]{:S(2)}) collective-permute-start(bf16[64,1024]{1,0:T(8,128)(2,1)S(1)} %finish.1.rest_4_), channel_id=1, source_target_pairs={{0,16},{1,17},{2,18},{3,19},{16,0},{17,1},{18,2},{19,3},{4,20},{5,... | collective-permute-start | bytes 393224 | tf_op jit(solution)/shard_map/ppermute | solution.py:38
  25.3 6.2 %collective-permute-start.10 = (bf16[64,1024]{1,0:T(8,128)(2,1)S(1)}, bf16[64,1024]{1,0:T(8,128)(2,1)S(1)}, u32[]{:S(2)}, u32[]{:S(2)}) collective-permute-start(bf16[64,1024]{1,0:T(8,128)(2,1)S(1)} %finish.1.rest_4_), channel_id=1, source_target_pairs={{0,8},{4,12},{8,0},{12,4},{1,9},{5,13},{9,1},{13,5},{2,10},{6,14},... | collective-permute-start | bytes 393224 | tf_op jit(solution)/shard_map/ppermute | solution.py:28
  26.8 5.2 %collective-permute-start.11 = (bf16[64,1024]{1,0:T(8,128)(2,1)S(1)}, bf16[64,1024]{1,0:T(8,128)(2,1)S(1)}, u32[]{:S(2)}, u32[]{:S(2)}) collective-permute-start(bf16[64,1024]{1,0:T(8,128)(2,1)S(1)} %collective-permute-done.9.rest_5_), channel_id=1, source_target_pairs={{0,8},{4,12},{8,0},{12,4},{1,9},{5,13},{9,1},{13,5},{2,10},{6,14},... | collective-permute-start | bytes 393224 | tf_op jit(solution)/shard_map/ppermute | solution.py:28
  29.3 2.8 %collective-permute-start.8 = (bf16[64,1024]{1,0:T(8,128)(2,1)S(1)}, bf16[64,1024]{1,0:T(8,128)(2,1)S(1)}, u32[]{:S(2)}, u32[]{:S(2)}) collective-permute-start(bf16[64,1024]{1,0:T(8,128)(2,1)S(1)} %collective-permute-done.6.rest_1_), channel_id=1, source_target_pairs={{0,4},{4,0},{8,12},{12,8},{1,5},{5,1},{9,13},{13,9},{2,6},{6,2},{1... | collective-permute-start | bytes 393224 | tf_op jit(solution)/shard_map/ppermute | solution.py:28
  30.8 1.3 %collective-permute-start.7 = (bf16[64,1024]{1,0:T(8,128)(2,1)S(1)}, bf16[64,1024]{1,0:T(8,128)(2,1)S(1)}, u32[]{:S(2)}, u32[]{:S(2)}) collective-permute-start(bf16[64,1024]{1,0:T(8,128)(2,1)S(1)} %collective-permute-done.5.rest_0_), channel_id=1, source_target_pairs={{0,4},{4,0},{8,12},{12,8},{1,5},{5,1},{9,13},{13,9},{2,6},{6,2},{1... | collective-permute-start | bytes 393224 | tf_op jit(solution)/shard_map/ppermute | solution.py:28
  32.7 3.7 %collective-permute-start.12 = (f32[8,256]{1,0:T(8,128)S(1)}, f32[8,256]{1,0:T(8,128)S(1)}, u32[]{:S(2)}, u32[]{:S(2)}) collective-permute-start(f32[8,256]{1,0:T(8,128)S(1)} %get-tuple-element.45.column), channel_id=1, source_target_pairs={{0,8},{4,12},{8,0},{12,4},{1,9},{5,13},{9,1},{13,5},{2,10},{6,14},... | collective-permute-start | bytes 24584 | tf_op jit(solution)/shard_map/ppermute | solution.py:28
  34.5 1.2 %collective-permute-start.13 = (f32[1,256]{1,0:T(1,128)S(1)}, f32[1,256]{1,0:T(1,128)S(1)}, u32[]{:S(2)}, u32[]{:S(2)}) collective-permute-start(f32[1,256]{1,0:T(1,128)S(1)} %rows.1.row), channel_id=1, source_target_pairs={{0,4},{4,0},{8,12},{12,8},{1,5},{5,1},{9,13},{13,9},{2,6},{6,2},{1... | collective-permute-start | bytes 3080 | tf_op jit(solution)/shard_map/ppermute | solution.py:28
  35.7 3.7 %collective-permute-start.15 = (f32[8,256]{1,0:T(8,128)S(1)}, f32[8,256]{1,0:T(8,128)S(1)}, u32[]{:S(2)}, u32[]{:S(2)}) collective-permute-start(f32[8,256]{1,0:T(8,128)S(1)} %merge.2.after.rest_0_), channel_id=1, source_target_pairs={{0,1},{1,0},{2,3},{3,2},{4,5},{5,4},{6,7},{7,6},{8,9},{9,8},{10,11... | collective-permute-start | bytes 24584 | tf_op jit(solution)/shard_map/ppermute | solution.py:28
  36.4 4.5 %collective-permute-start.14 = (f32[2,256]{1,0:T(2,128)S(1)}, f32[2,256]{1,0:T(2,128)S(1)}, u32[]{:S(2)}, u32[]{:S(2)}) collective-permute-start(f32[2,256]{1,0:T(2,128)S(1)} %merge.3.column), channel_id=1, source_target_pairs={{0,2},{1,3},{2,0},{3,1},{4,6},{5,7},{6,4},{7,5},{8,10},{9,11},{10,... | collective-permute-start | bytes 6152 | tf_op jit(solution)/shard_map/ppermute | solution.py:28
  41.4 1.6 %collective-permute-start.16 = (bf16[128,1152]{1,0:T(8,128)(2,1)S(1)}, bf16[128,1152]{1,0:T(8,128)(2,1)S(1)}, u32[]{:S(2)}, u32[]{:S(2)}) collective-permute-start(bf16[128,1152]{1,0:T(8,128)(2,1)S(1)} %get-tuple-element.47), channel_id=1, source_target_pairs={{0,4},{4,0},{8,12},{12,8},{1,5},{5,1},{9,13},{13,9},{2,6},{6,2},{1... | collective-permute-start | bytes 884744 | tf_op jit(solution)/shard_map/ppermute | solution.py:28
  43.1 6.0 %collective-permute-start.17 = (bf16[64,1152]{1,0:T(8,128)(2,1)S(1)}, bf16[64,1152]{1,0:T(8,128)(2,1)S(1)}, u32[]{:S(2)}, u32[]{:S(2)}) collective-permute-start(bf16[64,1152]{1,0:T(8,128)(2,1)S(1)} %get-tuple-element.50), channel_id=1, source_target_pairs={{0,1},{1,0},{2,3},{3,2},{4,5},{5,4},{6,7},{7,6},{8,9},{9,8},{10,11... | collective-permute-start | bytes 442376 | tf_op jit(solution)/shard_map/ppermute | solution.py:28
  44.6 6.1 %collective-permute-start.19 = (f32[1,128]{1,0:T(1,128)S(1)}, f32[1,128]{1,0:T(1,128)S(1)}, u32[]{:S(2)}, u32[]{:S(2)}) collective-permute-start(f32[1,128]{1,0:T(1,128)S(1)} %get-tuple-element.51), channel_id=1, source_target_pairs={{0,17},{1,16},{2,19},{3,18},{16,1},{17,0},{18,3},{19,2},{4,21},{5,... | collective-permute-start | bytes 1544 | tf_op jit(solution)/shard_map/ppermute | solution.py:38
  46.8 3.8 %collective-permute-start.18 = (f32[1,128]{1,0:T(1,128)S(1)}, f32[1,128]{1,0:T(1,128)S(1)}, u32[]{:S(2)}, u32[]{:S(2)}) collective-permute-start(f32[1,128]{1,0:T(1,128)S(1)} %get-tuple-element.51), channel_id=1, source_target_pairs={{0,16},{1,17},{2,18},{3,19},{16,0},{17,1},{18,2},{19,3},{4,20},{5,... | collective-permute-start | bytes 1544 | tf_op jit(solution)/shard_map/ppermute | solution.py:38
